TPU v7x, 32 devices: a whole 2x2x4 slice. The times are simulated.
32 devices in a mesh: grp: 8 (over z, core), fsdp: 4 (over y, x).
Axes of the slice: x: 2, y: 2, z: 4, core: 2. Of those that a mesh axis runs over, the one named last changes fastest.
Arguments:
- tokens: bfloat16 [32, 384, 1536], P(('grp', 'fsdp')), may hold values from -6 to 6
- doc_ids: int32 [32, 384], P(('grp', 'fsdp')), may hold values from 0 to 3, never falling along the last dimension, each value on 1 to 192 neighbouring positions
- cotangent: bfloat16 [32, 384, 1536], P(('grp', 'fsdp')), may hold values from -6 to 6
- gain_in: float32 [1536], P('fsdp'), may hold values from 0.5 to 1.5
- w_query: float32 [1536, 1536], P('fsdp'), may hold values from -0.15625 to 0.15625
- w_key: float32 [1536, 1536], P('fsdp'), may hold values from -0.15625 to 0.15625
- w_value: float32 [1536, 1536], P('fsdp'), may hold values from -0.15625 to 0.15625
- w_house: float32 [1536, 1536], P('fsdp'), may hold values from -0.15625 to 0.15625
- w_rate: float32 [1536, 12], P('fsdp'), may hold values from -0.15625 to 0.15625
- conv_taps: float32 [4, 1536], P(None, 'fsdp'), may hold values from -3 to 3
- w_out: float32 [1536, 1536], P('fsdp'), may hold values from -0.4375 to 0.4375
- gain_mid: float32 [1536], P('fsdp'), may hold values from 0.5 to 1.5
- w_gate: float32 [1536, 4096], P('fsdp'), may hold values from -0.15625 to 0.15625
- w_up: float32 [1536, 4096], P('fsdp'), may hold values from -0.15625 to 0.15625
- w_down: float32 [4096, 1536], P('fsdp'), may hold values from -0.09375 to 0.09375
Outputs:
- result: bfloat16 [32, 384, 1536], P(('grp', 'fsdp'))
- grad_tokens: float32 [32, 384, 1536], P(('grp', 'fsdp'))
- grad_gain_in: float32 [1536], P('fsdp')
- grad_query: float32 [1536, 1536], P('fsdp')
- grad_key: float32 [1536, 1536], P('fsdp')
- grad_value: float32 [1536, 1536], P('fsdp')
- grad_house: float32 [1536, 1536], P('fsdp')
- grad_rate: float32 [1536, 12], P('fsdp')
- grad_taps: float32 [4, 1536], P(None, 'fsdp')
- grad_out: float32 [1536, 1536], P('fsdp')
- grad_gain_mid: float32 [1536], P('fsdp')
- grad_gate: float32 [1536, 4096], P('fsdp')
- grad_up: float32 [1536, 4096], P('fsdp')
- grad_down: float32 [4096, 1536], P('fsdp')
Inputs may be any that keep to these rules, and one draw needn't show every extreme that they name: `doc_ids`: within each row document numbers never fall, each of the 4 documents has 1 to 192 positions, and one has exactly 192.
All inputs are finite; a program needn't handle non-finite values.
Results may differ from a plain program's by a relative error of at most 0.025.
Values may be sent and summed in bfloat16 or wider, within the bound.
No kernel may reach another device: no remote copies, remote signals or barrier semaphores. Data moves between devices by JAX's collectives and lax.ppermute only.
A program may use at most 384 MiB of HBM per device.

v0:
```python
import jax
import jax.numpy as jnp
from jax import lax
from jax.sharding import PartitionSpec as P

epsilon = 1e-06
highest = lax.Precision.HIGHEST


def rms_scale(row_block, gain_row):
    inverse = lax.rsqrt(jnp.mean(row_block * row_block, axis=-1, keepdims=True) + epsilon)
    return row_block * inverse * gain_row


def short_conv(house_raw, tap_values, segment):
    length = house_raw.shape[0]
    summed = house_raw * tap_values[0]
    for offset in range(1, tap_values.shape[0]):
        shifted = jnp.concatenate(
            [
                jnp.zeros((offset, house_raw.shape[1]), house_raw.dtype),
                house_raw[: length - offset],
            ],
            axis=0,
        )
        seg_shift = jnp.concatenate(
            [jnp.full((offset,), -1, jnp.int32), segment[: length - offset]]
        )
        same_doc = (seg_shift == segment)[:, None]
        summed = summed + jnp.where(same_doc, shifted * tap_values[offset], 0.0)
    return summed


def unit_rows(mixed_rows, head_count):
    split_rows = mixed_rows.reshape(mixed_rows.shape[:-1] + (head_count, -1))
    inverse = lax.rsqrt(jnp.sum(split_rows * split_rows, axis=-1, keepdims=True) + epsilon)
    return (split_rows * inverse).reshape(mixed_rows.shape)


def outer_dot(left_rows, right_rows):
    return lax.dot_general(
        left_rows,
        right_rows,
        (((1,), (1,)), ((), ())),
        precision=highest,
        preferred_element_type=jnp.float32,
    )


def path_head(query_rows, key_rows, value_rows, house_rows, rate_rows, segment):
    length = query_rows.shape[0]
    positions = lax.iota(jnp.int32, length)
    same_doc = segment[:, None] == segment[None, :]
    inclusive = same_doc & (positions[None, :] <= positions[:, None])
    strict = same_doc & (positions[None, :] < positions[:, None])
    lower_part = jnp.where(strict, outer_dot(house_rows, house_rows) * rate_rows[None, :], 0.0)
    right_side = jnp.where(strict, outer_dot(house_rows, key_rows), 0.0)
    system = jnp.eye(length, dtype=query_rows.dtype) + lower_part
    carried = lax.linalg.triangular_solve(
        system, right_side, left_side=True, lower=True, unit_diagonal=True
    )
    reach_part = jnp.where(inclusive, outer_dot(query_rows, house_rows), 0.0) * rate_rows[None, :]
    scores = (
        outer_dot(query_rows, key_rows) - jnp.dot(reach_part, carried, precision=highest)
    ) * query_rows.shape[1] ** (-0.5)
    scores = jnp.where(inclusive, scores, -1e30)
    row_max = jnp.max(scores, axis=1, keepdims=True)
    exp_terms = jnp.where(inclusive, jnp.exp(scores - row_max), 0.0)
    probabilities = exp_terms / jnp.sum(exp_terms, axis=1, keepdims=True)
    return jnp.dot(probabilities, value_rows, precision=highest)


def path_attention(query_rows, key_rows, value_rows, house_rows, rate_rows, segment, head_count):
    length, model_width = query_rows.shape

    def by_heads(array):
        return array.reshape(length, head_count, model_width // head_count).transpose(1, 0, 2)

    def per_head(packed):
        return path_head(packed[0], packed[1], packed[2], packed[3], packed[4], segment)

    stacked = lax.map(
        jax.checkpoint(per_head),
        (
            by_heads(query_rows),
            by_heads(key_rows),
            by_heads(value_rows),
            by_heads(house_rows),
            rate_rows.T,
        ),
    )
    return stacked.transpose(1, 0, 2).reshape(length, model_width)


def dot_plain(left_rows, right_rows):
    return jnp.dot(left_rows, right_rows, preferred_element_type=jnp.float32)


def dot_left_t(left_rows, right_rows):
    return lax.dot_general(
        left_rows, right_rows, (((0,), (0,)), ((), ())), preferred_element_type=jnp.float32
    )


def dot_right_t(left_rows, right_rows):
    return lax.dot_general(
        left_rows, right_rows, (((1,), (1,)), ((), ())), preferred_element_type=jnp.float32
    )


def fetch_attention(gain_in, w_query, w_key, w_value, w_house, w_rate, conv_taps, w_out):
    half = jnp.bfloat16
    return (
        lax.all_gather(gain_in.astype(half), "fsdp", axis=0, tiled=True),
        lax.all_gather(w_query.astype(half), "fsdp", axis=0, tiled=True),
        lax.all_gather(w_key.astype(half), "fsdp", axis=0, tiled=True),
        lax.all_gather(w_value.astype(half), "fsdp", axis=0, tiled=True),
        lax.all_gather(w_house.astype(half), "fsdp", axis=0, tiled=True),
        lax.all_gather(w_rate.astype(half), "fsdp", axis=0, tiled=True),
        lax.all_gather(conv_taps.astype(half), "fsdp", axis=1, tiled=True),
        lax.all_gather(w_out.astype(half), "fsdp", axis=0, tiled=True),
    )


def fetch_feed(gain_mid, w_gate, w_up, w_down):
    half = jnp.bfloat16
    return (
        lax.all_gather(gain_mid.astype(half), "fsdp", axis=0, tiled=True),
        lax.all_gather(w_gate.astype(half), "fsdp", axis=0, tiled=True),
        lax.all_gather(w_up.astype(half), "fsdp", axis=0, tiled=True),
        lax.all_gather(w_down.astype(half), "fsdp", axis=0, tiled=True),
    )


def local(
    tokens,
    doc_ids,
    cotangent,
    gain_in,
    w_query,
    w_key,
    w_value,
    w_house,
    w_rate,
    conv_taps,
    w_out,
    gain_mid,
    w_gate,
    w_up,
    w_down,
):
    half = jnp.bfloat16
    single = jnp.float32
    head_count = w_rate.shape[1]
    segment = doc_ids[0]
    flat_rows = tokens[0].astype(single)
    upstream = cotangent[0]
    attn_set = fetch_attention(gain_in, w_query, w_key, w_value, w_house, w_rate, conv_taps, w_out)
    feed_set = fetch_feed(gain_mid, w_gate, w_up, w_down)
    gain_one, mat_query, mat_key, mat_value, mat_house, mat_rate, tap_half, mat_out = attn_set
    gain_two, mat_gate, mat_up, mat_down = feed_set
    gain_first = gain_one.astype(single)
    normed = rms_scale(flat_rows, gain_first).astype(half)
    query_rows = dot_plain(normed, mat_query).astype(half)
    key_rows = dot_plain(normed, mat_key).astype(half)
    value_rows = dot_plain(normed, mat_value).astype(half)
    house_raw = dot_plain(normed, mat_house)
    rate_sig = jax.nn.sigmoid(dot_plain(normed, mat_rate))
    rate_rows = 2.0 * rate_sig
    tap_values = tap_half.astype(single)

    def make_house(raw_rows, tap_rows):
        return unit_rows(short_conv(raw_rows, tap_rows, segment), head_count)

    house_rows = make_house(house_raw, tap_values).astype(half)

    def attend(query_part, key_part, value_part, house_part, rate_part):
        return path_attention(
            query_part, key_part, value_part, house_part, rate_part, segment, head_count
        )

    attn_inputs = (
        query_rows.astype(single),
        key_rows.astype(single),
        value_rows.astype(single),
        house_rows.astype(single),
        rate_rows,
    )
    attended = attend(
        attn_inputs[0], attn_inputs[1], attn_inputs[2], attn_inputs[3], attn_inputs[4]
    ).astype(half)
    middle = flat_rows + dot_plain(attended, mat_out)
    gain_second = gain_two.astype(single)
    normed_mid = rms_scale(middle, gain_second).astype(half)
    gate_rows = dot_plain(normed_mid, mat_gate)
    up_rows = dot_plain(normed_mid, mat_up)
    gate_sig = jax.nn.sigmoid(gate_rows)
    hidden = (gate_rows * gate_sig * up_rows).astype(half)
    result = (middle + dot_plain(hidden, mat_down)).astype(half)
    attn_set = fetch_attention(gain_in, w_query, w_key, w_value, w_house, w_rate, conv_taps, w_out)
    feed_set = fetch_feed(gain_mid, w_gate, w_up, w_down)
    gain_one, mat_query, mat_key, mat_value, mat_house, mat_rate, tap_half, mat_out = attn_set
    gain_two, mat_gate, mat_up, mat_down = feed_set
    grad_down = dot_left_t(hidden, upstream)
    grad_hidden = dot_right_t(upstream, mat_down)
    grad_up_rows = (grad_hidden * gate_rows * gate_sig).astype(half)
    grad_gate_rows = (
        grad_hidden * up_rows * gate_sig * (1.0 + gate_rows * (1.0 - gate_sig))
    ).astype(half)
    grad_gate = dot_left_t(normed_mid, grad_gate_rows)
    grad_up = dot_left_t(normed_mid, grad_up_rows)
    grad_normed_mid = dot_right_t(grad_gate_rows, mat_gate) + dot_right_t(grad_up_rows, mat_up)
    unused_mid, mid_back = jax.vjp(rms_scale, middle, gain_second)
    grad_mid_norm, grad_gain_mid = mid_back(grad_normed_mid)
    feed_grads = (
        lax.psum_scatter(
            grad_gain_mid.astype(jnp.bfloat16), "fsdp", scatter_dimension=0, tiled=True
        ).astype(jnp.float32),
        lax.psum_scatter(
            grad_gate.astype(jnp.bfloat16), "fsdp", scatter_dimension=0, tiled=True
        ).astype(jnp.float32),
        lax.psum_scatter(
            grad_up.astype(jnp.bfloat16), "fsdp", scatter_dimension=0, tiled=True
        ).astype(jnp.float32),
        lax.psum_scatter(
            grad_down.astype(jnp.bfloat16), "fsdp", scatter_dimension=0, tiled=True
        ).astype(jnp.float32),
    )
    grad_middle = upstream.astype(single) + grad_mid_norm
    grad_branch = grad_middle.astype(half)
    grad_wout = dot_left_t(attended, grad_branch)
    grad_attended = dot_right_t(grad_branch, mat_out)
    unused_attn, attend_back = jax.vjp(
        attend, attn_inputs[0], attn_inputs[1], attn_inputs[2], attn_inputs[3], attn_inputs[4]
    )
    grad_query_f, grad_key_f, grad_value_f, grad_house_f, grad_rate_f = attend_back(grad_attended)
    grad_query_rows = grad_query_f.astype(half)
    grad_key_rows = grad_key_f.astype(half)
    grad_value_rows = grad_value_f.astype(half)
    unused_house, house_back = jax.vjp(make_house, house_raw, tap_values)
    grad_house_raw, grad_taps = house_back(grad_house_f)
    grad_house_rows = grad_house_raw.astype(half)
    grad_rate_rows = (grad_rate_f * 2.0 * rate_sig * (1.0 - rate_sig)).astype(half)
    grad_wquery = dot_left_t(normed, grad_query_rows)
    grad_wkey = dot_left_t(normed, grad_key_rows)
    grad_wvalue = dot_left_t(normed, grad_value_rows)
    grad_whouse = dot_left_t(normed, grad_house_rows)
    grad_wrate = dot_left_t(normed, grad_rate_rows)
    grad_normed = (
        dot_right_t(grad_query_rows, mat_query)
        + dot_right_t(grad_key_rows, mat_key)
        + dot_right_t(grad_value_rows, mat_value)
        + dot_right_t(grad_house_rows, mat_house)
        + dot_right_t(grad_rate_rows, mat_rate)
    )
    unused_in, in_back = jax.vjp(rms_scale, flat_rows, gain_first)
    grad_flat_norm, grad_gain_in = in_back(grad_normed)
    grad_tokens = grad_middle + grad_flat_norm
    attn_grads = (
        lax.psum_scatter(
            grad_gain_in.astype(jnp.bfloat16), "fsdp", scatter_dimension=0, tiled=True
        ).astype(jnp.float32),
        lax.psum_scatter(
            grad_wquery.astype(jnp.bfloat16), "fsdp", scatter_dimension=0, tiled=True
        ).astype(jnp.float32),
        lax.psum_scatter(
            grad_wkey.astype(jnp.bfloat16), "fsdp", scatter_dimension=0, tiled=True
        ).astype(jnp.float32),
        lax.psum_scatter(
            grad_wvalue.astype(jnp.bfloat16), "fsdp", scatter_dimension=0, tiled=True
        ).astype(jnp.float32),
        lax.psum_scatter(
            grad_whouse.astype(jnp.bfloat16), "fsdp", scatter_dimension=0, tiled=True
        ).astype(jnp.float32),
        lax.psum_scatter(
            grad_wrate.astype(jnp.bfloat16), "fsdp", scatter_dimension=0, tiled=True
        ).astype(jnp.float32),
        lax.psum_scatter(
            grad_taps.astype(jnp.bfloat16), "fsdp", scatter_dimension=1, tiled=True
        ).astype(jnp.float32),
        lax.psum_scatter(
            grad_wout.astype(jnp.bfloat16), "fsdp", scatter_dimension=0, tiled=True
        ).astype(jnp.float32),
    )
    summed = (
        lax.psum(attn_grads[0].astype(jnp.bfloat16), "grp").astype(jnp.float32),
        lax.psum(attn_grads[1].astype(jnp.bfloat16), "grp").astype(jnp.float32),
        lax.psum(attn_grads[2].astype(jnp.bfloat16), "grp").astype(jnp.float32),
        lax.psum(attn_grads[3].astype(jnp.bfloat16), "grp").astype(jnp.float32),
        lax.psum(attn_grads[4].astype(jnp.bfloat16), "grp").astype(jnp.float32),
        lax.psum(attn_grads[5].astype(jnp.bfloat16), "grp").astype(jnp.float32),
        lax.psum(attn_grads[6].astype(jnp.bfloat16), "grp").astype(jnp.float32),
        lax.psum(attn_grads[7].astype(jnp.bfloat16), "grp").astype(jnp.float32),
        lax.psum(feed_grads[0].astype(jnp.bfloat16), "grp").astype(jnp.float32),
        lax.psum(feed_grads[1].astype(jnp.bfloat16), "grp").astype(jnp.float32),
        lax.psum(feed_grads[2].astype(jnp.bfloat16), "grp").astype(jnp.float32),
        lax.psum(feed_grads[3].astype(jnp.bfloat16), "grp").astype(jnp.float32),
    )
    return (
        result[None],
        grad_tokens[None],
        summed[0],
        summed[1],
        summed[2],
        summed[3],
        summed[4],
        summed[5],
        summed[6],
        summed[7],
        summed[8],
        summed[9],
        summed[10],
        summed[11],
    )


def solution(mesh):
    return jax.shard_map(
        local,
        mesh=mesh,
        in_specs=(
            P(("grp", "fsdp"), None, None),
            P(("grp", "fsdp"), None),
            P(("grp", "fsdp"), None, None),
            P("fsdp"),
            P("fsdp", None),
            P("fsdp", None),
            P("fsdp", None),
            P("fsdp", None),
            P("fsdp", None),
            P(None, "fsdp"),
            P("fsdp", None),
            P("fsdp"),
            P("fsdp", None),
            P("fsdp", None),
            P("fsdp", None),
        ),
        out_specs=(
            P(("grp", "fsdp"), None, None),
            P(("grp", "fsdp"), None, None),
            P("fsdp"),
            P("fsdp", None),
            P("fsdp", None),
            P("fsdp", None),
            P("fsdp", None),
            P("fsdp", None),
            P(None, "fsdp"),
            P("fsdp", None),
            P("fsdp"),
            P("fsdp", None),
            P("fsdp", None),
            P("fsdp", None),
        ),
        check_vma=False,
    )
```

profile of v0, /device:TPU:0, one launch (start us, length us, event | category | flops | bytes accessed | tf_op | source)
XLA Modules:
  0.0 3110.1 jit_solution(6407261776200314311)
XLA Ops:
  38.1 9.5 all-gather
  85.4 45.0 %all-gather.13.cloned.1.call-done = bf16[1536,1536]{1,0:T(8,128)(2,1)} async-done(((bf16[384,1536]{1,0:T(8,128)(2,1)}), bf16[1536,1536]{1,0:T(8,128)(2,1)}) %all-gather.13.cloned.1.call-update) | async-done | bytes 4718608 | tf_op jit(solution)/shard_map/all_gather | solution.py:116
  140.2 49.7 %all-gather.15.cloned.1.call-done = bf16[1536,1536]{1,0:T(8,128)(2,1)} async-done(((bf16[384,1536]{1,0:T(8,128)(2,1)}), bf16[1536,1536]{1,0:T(8,128)(2,1)}) %all-gather.15.cloned.1.call-update) | async-done | bytes 4718608 | tf_op jit(solution)/shard_map/all_gather | solution.py:118
  214.1 35.2 %all-gather.17.cloned.1.call-done = bf16[1536,1536]{1,0:T(8,128)(2,1)} async-done(((bf16[384,1536]{1,0:T(8,128)(2,1)}), bf16[1536,1536]{1,0:T(8,128)(2,1)}) %all-gather.17.cloned.1.call-update) | async-done | bytes 4718608 | tf_op jit(solution)/shard_map/all_gather | solution.py:117
  259.1 664.1 %while.43 = (s32[]{:T(128)}, bf16[12,384,128]{1,2,0:T(8,128)(2,1)}, s32[1,384]{1,0:T(1,128)S(1)}, f32[12,384,128]{2,1,0:T(8,128)}, f32[12,384,128]{2,1,0:T(8,128...) while((s32[]{:T(128)}, bf16[12,384,128]{1,2,0:T(8,128)(2,1)}, ...), condition=%wide.region_5.7_spmd, body=%wide.region_2.6_spmd.sunk | while | flops 2271460864 | bytes 11056466 | solution.py:82
  277.3 29.5 custom-call.19
  332.9 29.5 custom-call.19
  388.2 29.5 custom-call.19
  443.5 29.5 custom-call.19
  498.8 29.5 custom-call.19
  554.0 29.5 custom-call.19
  609.3 29.5 custom-call.19
  664.5 29.5 custom-call.19
  719.8 29.5 custom-call.19
  775.1 29.5 custom-call.19
  830.3 29.5 custom-call.19
  885.6 29.5 custom-call.19
  929.6 11.6 fusion.184
  941.3 10.1 fusion.185
  951.4 20.3 multiply_convert_fusion
  980.9 9.7 multiply_reduce_fusion.3
  997.6 1040.1 %while.45 = (s32[]{:T(128)}, bf16[12,384,128]{1,2,0:T(8,128)(2,1)}, bf16[12,384,128]{1,2,0:T(8,128)(2,1)}, bf16[12,384,128]{1,2,0:T(8,128)(2,1)}, f32[12,384,128...) while((s32[]{:T(128)}, bf16[12,384,128]{1,2,0:T(8,128)(2,1)}, ...), condition=%wide.region_16.19_spmd, body=%wide.region_8.18_spmd.sunk | while | flops 7271251968 | bytes 56900964 | solution.py:82
  1021.2 29.5 custom-call.21
  1106.4 29.5 custom-call.21
  1191.5 29.5 custom-call.21
  1276.6 29.5 custom-call.21
  1361.7 29.5 custom-call.21
  1446.9 29.5 custom-call.21
  1532.0 29.5 custom-call.21
  1617.1 29.5 custom-call.21
  1702.2 29.5 custom-call.21
  1787.4 29.5 custom-call.21
  1872.5 29.5 custom-call.21
  1957.6 29.5 custom-call.21
  2088.7 11.5 convolution_convert_fusion.2
  2100.3 11.7 convolution_convert_fusion.1
  2113.4 11.5 convolution_convert_fusion
  2128.7 33.5 %reduce-scatter.17.cloned.1.call-done = bf16[384,1536]{1,0:T(8,128)(2,1)} async-done(((bf16[1536,1536]{1,0:T(8,128)(2,1)}), bf16[384,1536]{1,0:T(8,128)(2,1)}) %reduce-scatter.17.cloned.1.call-update) | async-done | bytes 1179664 | tf_op jit(solution)/shard_map/reduce_scatter | solution.py:266
  2162.2 60.7 %reduce-scatter.19.cloned.1.call-done = bf16[384,1536]{1,0:T(8,128)(2,1)} async-done(((bf16[1536,1536]{1,0:T(8,128)(2,1)}), bf16[384,1536]{1,0:T(8,128)(2,1)}) %reduce-scatter.19.cloned.1.call-update) | async-done | bytes 1179664 | tf_op jit(solution)/shard_map/reduce_scatter | solution.py:269
  2222.9 60.0 %reduce-scatter.21.cloned.1.call-done = bf16[384,1536]{1,0:T(8,128)(2,1)} async-done(((bf16[1536,1536]{1,0:T(8,128)(2,1)}), bf16[384,1536]{1,0:T(8,128)(2,1)}) %reduce-scatter.21.cloned.1.call-update) | async-done | bytes 1179664 | tf_op jit(solution)/shard_map/reduce_scatter | solution.py:272
  2282.9 60.1 %reduce-scatter.23.cloned.1.call-done = bf16[384,1536]{1,0:T(8,128)(2,1)} async-done(((bf16[1536,1536]{1,0:T(8,128)(2,1)}), bf16[384,1536]{1,0:T(8,128)(2,1)}) %reduce-scatter.23.cloned.1.call-update) | async-done | bytes 1179664 | tf_op jit(solution)/shard_map/reduce_scatter | solution.py:281
  2343.0 123.7 %reduce-scatter.25.cloned.1.call-done = bf16[384,4096]{1,0:T(8,128)(2,1)} async-done(((bf16[1536,4096]{1,0:T(8,128)(2,1)}), bf16[384,4096]{1,0:T(8,128)(2,1)}) %reduce-scatter.25.cloned.1.call-update) | async-done | bytes 3145744 | tf_op jit(solution)/shard_map/reduce_scatter | solution.py:219
  2466.8 123.7 %reduce-scatter.27.cloned.1.call-done = bf16[384,4096]{1,0:T(8,128)(2,1)} async-done(((bf16[1536,4096]{1,0:T(8,128)(2,1)}), bf16[384,4096]{1,0:T(8,128)(2,1)}) %reduce-scatter.27.cloned.1.call-update) | async-done | bytes 3145744 | tf_op jit(solution)/shard_map/reduce_scatter | solution.py:222
  2590.5 123.7 %reduce-scatter.29.cloned.1.call-done = bf16[1024,1536]{1,0:T(8,128)(2,1)} async-done(((bf16[4096,1536]{1,0:T(8,128)(2,1)}), bf16[1024,1536]{1,0:T(8,128)(2,1)}) %reduce-scatter.29.cloned.1.call-update) | async-done | bytes 3145744 | tf_op jit(solution)/shard_map/reduce_scatter | solution.py:225
  2731.3 9.8 all-reduce.16
  2758.6 11.0 reduce-scatter.31.cloned.1.call-done
  2770.6 29.3 all-reduce.14
  2802.2 279.7 %all-reduce.19.cloned.1.call-done = (bf16[384,1536]{1,0:T(8,128)(2,1)}, bf16[384,1536]{1,0:T(8,128)(2,1)}, bf16[384,1536]{1,0:T(8,128)(2,1)}, bf16[384,1536]{1,0...) async-done(((bf16[384,1536]{1,0:T(8,128)(2,1)}, bf16[384,1536]{1,0:T(8,128)(2,1)}, ...) | async-done | bytes 15335440 | tf_op jit(solution)/shard_map/psum | solution.py:287
  (2052 shorter events, 1403.7 us)
Async XLA Ops:
  7.2 68.3 %all-gather.11.cloned.1.call-start = ((), (), s32[]{:S(2)}) async-start(), calls=%async_computation.10 | async-start | bytes 5898240 | tf_op jit(solution)/shard_map/all_gather | solution.py:115
  10.2 120.2 %all-gather.13.cloned.1.call-start = ((), (), s32[]{:S(2)}) async-start(), calls=%async_computation.11 | async-start | bytes 5898240 | tf_op jit(solution)/shard_map/all_gather | solution.py:116
  11.5 178.5 %all-gather.15.cloned.1.call-start = ((), (), s32[]{:S(2)}) async-start(), calls=%async_computation.12 | async-start | bytes 5898240 | tf_op jit(solution)/shard_map/all_gather | solution.py:118
  14.5 234.8 %all-gather.17.cloned.1.call-start = ((), (), s32[]{:S(2)}) async-start(), calls=%async_computation.13 | async-start | bytes 5898240 | tf_op jit(solution)/shard_map/all_gather | solution.py:117
  15.7 907.5 %all-gather.19.cloned.1.call-start = ((), (), s32[]{:S(2)}) async-start(), calls=%async_computation.14 | async-start | bytes 5898240 | tf_op jit(solution)/shard_map/all_gather | solution.py:121
  18.6 909.8 %all-gather.21.cloned.1.call-start = ((), (), s32[]{:S(2)}) async-start(), calls=%async_computation.15 | async-start | bytes 15728640 | tf_op jit(solution)/shard_map/all_gather | solution.py:129
  24.4 916.9 %all-gather.23.cloned.1.call-start = ((), (), s32[]{:S(2)}) async-start(), calls=%async_computation.16 | async-start | bytes 15728640 | tf_op jit(solution)/shard_map/all_gather | solution.py:130
  29.3 922.0 %all-gather.25.cloned.1.call-start = ((), (), s32[]{:S(2)}) async-start(), calls=%async_computation.17 | async-start | bytes 15728640 | tf_op jit(solution)/shard_map/all_gather | solution.py:131
  34.3 2094.5 %reduce-scatter.15.cloned.1.call-start = ((), (), s32[]{:S(2)}) async-start(), calls=%async_computation.18 | async-start | bytes 5898240 | tf_op jit(solution)/shard_map/reduce_scatter | solution.py:263
  34.9 39.9 %copy-start.18 = (s32[384]{0:T(512)}, s32[384]{0:T(512)S(1)}, u32[]{:S(2)}) copy-start(s32[384]{0:T(512)S(1)} %reduce.6) | copy-start | bytes 4612
  48.0 201.3 %copy-start.80 = (f32[384]{0:T(512)}, f32[384]{0:T(512)S(1)}, u32[]{:S(2)}) copy-start(f32[384]{0:T(512)S(1)} %fusion.164) | copy-start | bytes 4612
  56.9 137.4 %copy-start.61 = (f32[1536]{0:T(1024)}, f32[1536]{0:T(1024)S(1)}, u32[]{:S(2)}) copy-start(f32[1536]{0:T(1024)S(1)} %get-tuple-element.456) | copy-start | bytes 18436
  140.2 55.6 %copy-start.63 = (f32[1536]{0:T(1024)S(1)}, f32[1536]{0:T(1024)}, u32[]{:S(2)}) copy-start(f32[1536]{0:T(1024)} %get-tuple-element.457) | copy-start | bytes 18436
  140.2 55.6 %copy-start.65 = (f32[1536]{0:T(1024)S(1)}, f32[1536]{0:T(1024)}, u32[]{:S(2)}) copy-start(f32[1536]{0:T(1024)} %get-tuple-element.458) | copy-start | bytes 18436
  140.2 55.6 %copy-start.67 = (f32[1536]{0:T(1024)S(1)}, f32[1536]{0:T(1024)}, u32[]{:S(2)}) copy-start(f32[1536]{0:T(1024)} %get-tuple-element.459) | copy-start | bytes 18436
  140.2 55.6 %copy-start.88 = (pred[384]{0:T(512)(128)(4,1)S(1)}, pred[384]{0:T(512)(128)(4,1)}, u32[]{:S(2)}) copy-start(pred[384]{0:T(512)(128)(4,1)} %get-tuple-element.573) | copy-start | bytes 1156
  140.2 55.6 %copy-start.89 = (pred[384]{0:T(512)(128)(4,1)S(1)}, pred[384]{0:T(512)(128)(4,1)}, u32[]{:S(2)}) copy-start(pred[384]{0:T(512)(128)(4,1)} %get-tuple-element.574) | copy-start | bytes 1156
  140.2 55.6 %copy-start.90 = (pred[384]{0:T(512)(128)(4,1)S(1)}, pred[384]{0:T(512)(128)(4,1)}, u32[]{:S(2)}) copy-start(pred[384]{0:T(512)(128)(4,1)} %get-tuple-element.575) | copy-start | bytes 1156
  212.1 37.2 %copy-start.70 = (f32[1536]{0:T(1024)S(1)}, f32[1536]{0:T(1024)}, u32[]{:S(2)}) copy-start(f32[1536]{0:T(1024)} %copy-done.69) | copy-start | bytes 18436
  928.1 62.5 %copy-start.12 = (f32[384,1536]{1,0:T(8,128)}, f32[384,1536]{1,0:T(8,128)S(1)}, u32[]{:S(2)}) copy-start(f32[384,1536]{1,0:T(8,128)S(1)} %get-tuple-element.577) | copy-start | bytes 7077892
  1012.0 43.5 %copy-start.25 = (f32[1,384,128]{2,1,0:T(8,128)}, f32[1,384,128]{2,1,0:T(8,128)S(1)}, u32[]{:S(2)}) copy-start(f32[1,384,128]{2,1,0:T(8,128)S(1)} %copy.216) | copy-start | bytes 589828 | tf_op jit(solution)/shard_map/transpose(jvp())/while
  1021.2 31.6 %copy-start.8 = (f32[384,384]{0,1:T(8,128)}, f32[384,384]{0,1:T(8,128)S(1)}, u32[]{:S(2)}) copy-start(f32[384,384]{0,1:T(8,128)S(1)} %get-tuple-element.986) | copy-start | bytes 1769476 | tf_op jit(solution)/shard_map/transpose(jvp())/while
  1097.2 43.5 %copy-start.25 = (f32[1,384,128]{2,1,0:T(8,128)}, f32[1,384,128]{2,1,0:T(8,128)S(1)}, u32[]{:S(2)}) copy-start(f32[1,384,128]{2,1,0:T(8,128)S(1)} %copy.216) | copy-start | bytes 589828 | tf_op jit(solution)/shard_map/transpose(jvp())/while
  1106.4 31.6 %copy-start.8 = (f32[384,384]{0,1:T(8,128)}, f32[384,384]{0,1:T(8,128)S(1)}, u32[]{:S(2)}) copy-start(f32[384,384]{0,1:T(8,128)S(1)} %get-tuple-element.986) | copy-start | bytes 1769476 | tf_op jit(solution)/shard_map/transpose(jvp())/while
  1182.3 43.5 %copy-start.25 = (f32[1,384,128]{2,1,0:T(8,128)}, f32[1,384,128]{2,1,0:T(8,128)S(1)}, u32[]{:S(2)}) copy-start(f32[1,384,128]{2,1,0:T(8,128)S(1)} %copy.216) | copy-start | bytes 589828 | tf_op jit(solution)/shard_map/transpose(jvp())/while
  1267.4 43.5 %copy-start.25 = (f32[1,384,128]{2,1,0:T(8,128)}, f32[1,384,128]{2,1,0:T(8,128)S(1)}, u32[]{:S(2)}) copy-start(f32[1,384,128]{2,1,0:T(8,128)S(1)} %copy.216) | copy-start | bytes 589828 | tf_op jit(solution)/shard_map/transpose(jvp())/while
  1352.5 43.5 %copy-start.25 = (f32[1,384,128]{2,1,0:T(8,128)}, f32[1,384,128]{2,1,0:T(8,128)S(1)}, u32[]{:S(2)}) copy-start(f32[1,384,128]{2,1,0:T(8,128)S(1)} %copy.216) | copy-start | bytes 589828 | tf_op jit(solution)/shard_map/transpose(jvp())/while
  1361.7 31.6 %copy-start.8 = (f32[384,384]{0,1:T(8,128)}, f32[384,384]{0,1:T(8,128)S(1)}, u32[]{:S(2)}) copy-start(f32[384,384]{0,1:T(8,128)S(1)} %get-tuple-element.986) | copy-start | bytes 1769476 | tf_op jit(solution)/shard_map/transpose(jvp())/while
  1437.7 43.5 %copy-start.25 = (f32[1,384,128]{2,1,0:T(8,128)}, f32[1,384,128]{2,1,0:T(8,128)S(1)}, u32[]{:S(2)}) copy-start(f32[1,384,128]{2,1,0:T(8,128)S(1)} %copy.216) | copy-start | bytes 589828 | tf_op jit(solution)/shard_map/transpose(jvp())/while
  1522.8 43.5 %copy-start.25 = (f32[1,384,128]{2,1,0:T(8,128)}, f32[1,384,128]{2,1,0:T(8,128)S(1)}, u32[]{:S(2)}) copy-start(f32[1,384,128]{2,1,0:T(8,128)S(1)} %copy.216) | copy-start | bytes 589828 | tf_op jit(solution)/shard_map/transpose(jvp())/while
  1532.0 31.6 %copy-start.8 = (f32[384,384]{0,1:T(8,128)}, f32[384,384]{0,1:T(8,128)S(1)}, u32[]{:S(2)}) copy-start(f32[384,384]{0,1:T(8,128)S(1)} %get-tuple-element.986) | copy-start | bytes 1769476 | tf_op jit(solution)/shard_map/transpose(jvp())/while
  1607.9 43.5 %copy-start.25 = (f32[1,384,128]{2,1,0:T(8,128)}, f32[1,384,128]{2,1,0:T(8,128)S(1)}, u32[]{:S(2)}) copy-start(f32[1,384,128]{2,1,0:T(8,128)S(1)} %copy.216) | copy-start | bytes 589828 | tf_op jit(solution)/shard_map/transpose(jvp())/while
  1693.0 43.5 %copy-start.25 = (f32[1,384,128]{2,1,0:T(8,128)}, f32[1,384,128]{2,1,0:T(8,128)S(1)}, u32[]{:S(2)}) copy-start(f32[1,384,128]{2,1,0:T(8,128)S(1)} %copy.216) | copy-start | bytes 589828 | tf_op jit(solution)/shard_map/transpose(jvp())/while
  1778.2 43.5 %copy-start.25 = (f32[1,384,128]{2,1,0:T(8,128)}, f32[1,384,128]{2,1,0:T(8,128)S(1)}, u32[]{:S(2)}) copy-start(f32[1,384,128]{2,1,0:T(8,128)S(1)} %copy.216) | copy-start | bytes 589828 | tf_op jit(solution)/shard_map/transpose(jvp())/while
  1787.4 31.6 %copy-start.8 = (f32[384,384]{0,1:T(8,128)}, f32[384,384]{0,1:T(8,128)S(1)}, u32[]{:S(2)}) copy-start(f32[384,384]{0,1:T(8,128)S(1)} %get-tuple-element.986) | copy-start | bytes 1769476 | tf_op jit(solution)/shard_map/transpose(jvp())/while
  1863.3 43.5 %copy-start.25 = (f32[1,384,128]{2,1,0:T(8,128)}, f32[1,384,128]{2,1,0:T(8,128)S(1)}, u32[]{:S(2)}) copy-start(f32[1,384,128]{2,1,0:T(8,128)S(1)} %copy.216) | copy-start | bytes 589828 | tf_op jit(solution)/shard_map/transpose(jvp())/while
  1948.4 43.5 %copy-start.25 = (f32[1,384,128]{2,1,0:T(8,128)}, f32[1,384,128]{2,1,0:T(8,128)S(1)}, u32[]{:S(2)}) copy-start(f32[1,384,128]{2,1,0:T(8,128)S(1)} %copy.216) | copy-start | bytes 589828 | tf_op jit(solution)/shard_map/transpose(jvp())/while
  2044.4 117.8 %reduce-scatter.17.cloned.1.call-start = ((), (), s32[]{:S(2)}) async-start(), calls=%async_computation.19 | async-start | bytes 5898240 | tf_op jit(solution)/shard_map/reduce_scatter | solution.py:266
  2050.5 172.4 %reduce-scatter.19.cloned.1.call-start = ((), (), s32[]{:S(2)}) async-start(), calls=%async_computation.20 | async-start | bytes 5898240 | tf_op jit(solution)/shard_map/reduce_scatter | solution.py:269
  2056.6 226.3 %reduce-scatter.21.cloned.1.call-start = ((), (), s32[]{:S(2)}) async-start(), calls=%async_computation.21 | async-start | bytes 5898240 | tf_op jit(solution)/shard_map/reduce_scatter | solution.py:272
  2080.1 263.0 %reduce-scatter.23.cloned.1.call-start = ((), (), s32[]{:S(2)}) async-start(), calls=%async_computation.22 | async-start | bytes 5898240 | tf_op jit(solution)/shard_map/reduce_scatter | solution.py:281
  2087.4 379.3 %reduce-scatter.25.cloned.1.call-start = ((), (), s32[]{:S(2)}) async-start(), calls=%async_computation.23 | async-start | bytes 15728640 | tf_op jit(solution)/shard_map/reduce_scatter | solution.py:219
  2100.2 490.3 %reduce-scatter.27.cloned.1.call-start = ((), (), s32[]{:S(2)}) async-start(), calls=%async_computation.24 | async-start | bytes 15728640 | tf_op jit(solution)/shard_map/reduce_scatter | solution.py:222
  2112.0 602.2 %reduce-scatter.29.cloned.1.call-start = ((), (), s32[]{:S(2)}) async-start(), calls=%async_computation.25 | async-start | bytes 15728640 | tf_op jit(solution)/shard_map/reduce_scatter | solution.py:225
  2125.0 632.6 %reduce-scatter.33.cloned.1.call-start = ((), (), s32[]{:S(2)}) async-start(), calls=%async_computation.27 | async-start | bytes 491520
  2126.7 587.5 %copy-start.74 = (bf16[384,12]{0,1:T(8,128)(2,1)}, bf16[384,12]{0,1:T(8,128)(2,1)S(1)}, u32[]{:S(2)}) copy-start(bf16[384,12]{0,1:T(8,128)(2,1)S(1)} %fusion.163) | copy-start | bytes 27652
  2126.7 642.8 %reduce-scatter.31.cloned.1.call-start = ((), (), s32[]{:S(2)}) async-start(), calls=%async_computation.26 | async-start | bytes 491520
  2128.2 953.7 %all-reduce.19.cloned.1.call-start = ((), (), s32[]{:S(2)}) async-start(), calls=%async_computation.28 | async-start | bytes 30670848 | tf_op jit(solution)/shard_map/psum | solution.py:287
  (251 other events, 1206.5 us)
Sparse Core Ops, SparseCore 0:
  10.4 60.3 all-gather.10
  73.3 57.0 all-gather.12
  132.8 57.0 all-gather.14
  192.2 57.0 all-gather.16
  251.0 57.1 all-gather.18
  310.4 122.5 all-gather.20
  435.5 122.6 all-gather.22
  560.5 122.6 all-gather.24
  2044.5 57.1 reduce-scatter.14
  2105.1 57.0 reduce-scatter.16
  2165.8 57.0 reduce-scatter.18
  2225.8 57.0 reduce-scatter.20
  2285.9 57.0 reduce-scatter.22
  2346.0 120.7 reduce-scatter.24
  2469.7 120.7 reduce-scatter.26
  2593.4 120.7 reduce-scatter.28
  2717.4 24.4 reduce-scatter.32
  2745.1 24.4 reduce-scatter.30
  2772.6 309.3 all-reduce.18
where the time goes:
time: 3130 us; the launch traced here: 3110 us
  waiting for transfers between devices  1010 us (32%)
  other arithmetic  792 us (25%)
  matrix products  789 us (25%)
  local copies, waits for them, and re-layouts  405 us (13%)
  blocking collectives  72.9 us (2%)
    another operation x96, other arithmetic, path_head(): lax.linalg.triangular_solve(system, right_side, left_side=True, lower=Tru...  708 us
    psum x1, waiting for transfers between devices, local(): lax.psum(attn_grads[1].astype(jnp.bfloat16), 'grp').astype(jnp.float32)  280 us
    dot_general x192, matrix products, outer_dot(): lax.dot_general(left_rows, right_rows, (((1,), (1,)), ((), ())), precisio...  258 us
    another operation x432, local copies, waits for them, and re-layouts, path_head(): lax.linalg.triangular_solve(system, right_side, left_side=True, lower=Tru...  207 us
    another operation x240, matrix products, path_head(): lax.linalg.triangular_solve(system, right_side, left_side=True, lower=Tru...  172 us
    reduce_scatter x1, waiting for transfers between devices, local(): lax.psum_scatter(grad_gate.astype(jnp.bfloat16), 'fsdp', scatter_dimensio...  124 us
    reduce_scatter x1, waiting for transfers between devices, local(): lax.psum_scatter(grad_down.astype(jnp.bfloat16), 'fsdp', scatter_dimensio...  124 us
    reduce_scatter x1, waiting for transfers between devices, local(): lax.psum_scatter(grad_up.astype(jnp.bfloat16), 'fsdp', scatter_dimension=...  124 us
  transfers between devices with their start and end apart: 19, of which 12 were waited for; matrix products, arithmetic and copies ran while one was open for 28% of the time, Pallas kernels for 0%

commit v1 on v0

--- a/solution.py
+++ b/solution.py
@@ -1,7 +1,230 @@
+import functools
 import jax
 import jax.numpy as jnp
 from jax import lax
+from jax.experimental import pallas as pl
+from jax.experimental.pallas import tpu as pltpu
 from jax.sharding import PartitionSpec as P
+
+EPS = 1e-06
+HALF = jnp.bfloat16
+SINGLE = jnp.float32
+
+
+def mm(left, right):
+    return lax.dot_general(left, right, (((1,), (0,)), ((), ())), preferred_element_type=SINGLE)
+
+
+def mm_nt(left, right):
+    return lax.dot_general(left, right, (((1,), (1,)), ((), ())), preferred_element_type=SINGLE)
+
+
+def mm_tn(left, right):
+    return lax.dot_general(left, right, (((0,), (0,)), ((), ())), preferred_element_type=SINGLE)
+
+
+def conv_parts(raw, taps, marks, taps_count):
+    shifted = [raw]
+    total = raw * taps[0:1, :]
+    for k in range(1, taps_count):
+        moved = pltpu.roll(raw, k, 0) * marks[:, k : k + 1]
+        shifted.append(moved)
+        total = total + moved * taps[k : k + 1, :]
+    return shifted, total
+
+
+def attn_forward_kernel(
+    span, dim, count, taps_count,
+    q_ref, k_ref, v_ref, raw_ref, rate_ref, taps_ref, marks_ref, segc_ref, segr_ref,
+    out_ref, w_ref, t_ref, c_ref, p_ref,
+):
+    blocks = q_ref.shape[0] // span
+    marks = marks_ref[...]
+    row_id = lax.broadcasted_iota(jnp.int32, (span, span), 0)
+    col_id = lax.broadcasted_iota(jnp.int32, (span, span), 1)
+    eye = jnp.where(row_id == col_id, 1.0, 0.0)
+    sizes = []
+    size = 1
+    while size < span:
+        sizes.append(size)
+        size *= 2
+    level_of = {}
+    for size in sizes:
+        level_of[size] = ((row_id // (2 * size)) == (col_id // (2 * size))) & (
+            (row_id // size) > (col_id // size)
+        )
+    strict = []
+    inclusive = []
+    for u in range(blocks):
+        rows = slice(u * span, (u + 1) * span)
+        same = segc_ref[rows, 0:1] == segr_ref[0:1, rows]
+        strict.append(same & (col_id < row_id))
+        inclusive.append(same & (col_id <= row_id))
+    for h in range(count):
+        cols = slice(h * dim, (h + 1) * dim)
+        shifted, mixed = conv_parts(raw_ref[:, cols], taps_ref[:, cols], marks, taps_count)
+        inverse = lax.rsqrt(jnp.sum(mixed * mixed, axis=-1, keepdims=True) + EPS)
+        w_ref[:, cols] = (mixed * inverse).astype(HALF)
+    units = [(h, u) for h in range(count) for u in range(blocks)]
+    rates = {}
+    lower = {}
+    inv = {}
+    for h, u in units:
+        rows = slice(u * span, (u + 1) * span)
+        cols = slice(h * dim, (h + 1) * dim)
+        w = w_ref[rows, cols]
+        rates[h, u] = rate_ref[0, h : h + 1, rows]
+        lw = jnp.where(strict[u], mm_nt(w, w) * rates[h, u], 0.0)
+        lower[h, u] = lw.astype(HALF)
+        inv[h, u] = eye - jnp.where(level_of[1], lw, 0.0)
+    for size in sizes[1:]:
+        half_inv = {}
+        inner = {}
+        for unit in units:
+            half_inv[unit] = inv[unit].astype(HALF)
+            inner[unit] = mm(jnp.where(level_of[size], lower[unit], jnp.zeros_like(lower[unit])), half_inv[unit])
+        for unit in units:
+            inv[unit] = inv[unit] - mm(half_inv[unit], inner[unit].astype(HALF))
+    for h, u in units:
+        rows = slice(u * span, (u + 1) * span)
+        cols = slice(h * dim, (h + 1) * dim)
+        w = w_ref[rows, cols]
+        q = q_ref[rows, cols]
+        k = k_ref[rows, cols]
+        tri = inv[h, u].astype(HALF)
+        t_ref[h * blocks + u] = tri
+        right = jnp.where(strict[u], mm_nt(w, k), 0.0).astype(HALF)
+        carried = mm(tri, right).astype(HALF)
+        c_ref[h * blocks + u] = carried
+        reach = (jnp.where(inclusive[u], mm_nt(q, w), 0.0) * rates[h, u]).astype(HALF)
+        scores = (mm_nt(q, k) - mm(reach, carried)) * dim ** (-0.5)
+        scores = jnp.where(inclusive[u], scores, -1e30)
+        terms = jnp.exp(scores - jnp.max(scores, axis=1, keepdims=True))
+        probs = (terms / jnp.sum(terms, axis=1, keepdims=True)).astype(HALF)
+        p_ref[h * blocks + u] = probs
+        out_ref[rows, cols] = mm(probs, v_ref[rows, cols]).astype(HALF)
+
+
+def attn_backward_kernel(
+    span, dim, count, taps_count,
+    q_ref, k_ref, v_ref, w_ref, raw_ref, rate_ref, taps_ref, marks_ref, segc_ref, segr_ref,
+    grad_ref, t_ref, c_ref, p_ref,
+    dq_ref, dk_ref, dv_ref, draw_ref, drate_ref, dtaps_ref, dw_ref,
+):
+    blocks = q_ref.shape[0] // span
+    marks = marks_ref[...]
+    row_id = lax.broadcasted_iota(jnp.int32, (span, span), 0)
+    col_id = lax.broadcasted_iota(jnp.int32, (span, span), 1)
+    scale = dim ** (-0.5)
+    for u in range(blocks):
+        rows = slice(u * span, (u + 1) * span)
+        same = segc_ref[rows, 0:1] == segr_ref[0:1, rows]
+        strict = same & (col_id < row_id)
+        inclusive = same & (col_id <= row_id)
+        for h in range(count):
+            cols = slice(h * dim, (h + 1) * dim)
+            unit = h * blocks + u
+            q = q_ref[rows, cols]
+            k = k_ref[rows, cols]
+            v = v_ref[rows, cols]
+            w = w_ref[rows, cols]
+            grad = grad_ref[rows, cols]
+            rate = rate_ref[0, h : h + 1, rows]
+            probs = p_ref[unit]
+            carried = c_ref[unit]
+            tri = t_ref[unit]
+            dprobs = mm_nt(grad, v)
+            dv_ref[rows, cols] = mm_tn(probs, grad).astype(HALF)
+            probs = probs.astype(SINGLE)
+            weighted = probs * dprobs
+            dscore = ((weighted - probs * jnp.sum(weighted, axis=1, keepdims=True)) * scale).astype(HALF)
+            reach_raw = jnp.where(inclusive, mm_nt(q, w), 0.0)
+            reach = (reach_raw * rate).astype(HALF)
+            dreach = -mm_nt(dscore, carried)
+            drate = jnp.sum(dreach * reach_raw, axis=0, keepdims=True)
+            dreach = (jnp.where(inclusive, dreach, 0.0) * rate).astype(HALF)
+            dcarried = (-mm_tn(reach, dscore)).astype(HALF)
+            dright = jnp.where(strict, mm_tn(tri, dcarried), 0.0).astype(HALF)
+            dlower = jnp.where(strict, -mm_nt(dright, carried), 0.0)
+            drate = drate + jnp.sum(dlower * mm_nt(w, w), axis=0, keepdims=True)
+            dlower = (dlower * rate).astype(HALF)
+            dq_ref[rows, cols] = (mm(dscore, k) + mm(dreach, w)).astype(HALF)
+            dk_ref[rows, cols] = (mm_tn(dscore, q) + mm_tn(dright, w)).astype(HALF)
+            dw_ref[rows, cols] = mm_tn(dreach, q) + mm(dright, k) + mm(dlower, w) + mm_tn(dlower, w)
+            drate_ref[0, h : h + 1, rows] = drate
+    length = q_ref.shape[0]
+    for h in range(count):
+        cols = slice(h * dim, (h + 1) * dim)
+        taps = taps_ref[:, cols]
+        shifted, mixed = conv_parts(raw_ref[:, cols], taps, marks, taps_count)
+        inverse = lax.rsqrt(jnp.sum(mixed * mixed, axis=-1, keepdims=True) + EPS)
+        unit_rows = mixed * inverse
+        dw = dw_ref[:, cols]
+        dmixed = inverse * (dw - unit_rows * jnp.sum(dw * unit_rows, axis=-1, keepdims=True))
+        draw = dmixed * taps[0:1, :]
+        dtaps = [jnp.sum(dmixed * shifted[0], axis=0, keepdims=True)]
+        for k in range(1, taps_count):
+            dtaps.append(jnp.sum(dmixed * shifted[k], axis=0, keepdims=True))
+            draw = draw + pltpu.roll(dmixed * marks[:, k : k + 1], length - k, 0) * taps[k : k + 1, :]
+        draw_ref[:, cols] = draw.astype(HALF)
+        dtaps_ref[:, cols] = jnp.concatenate(dtaps, axis=0)
+
+
+def attn_forward(q, k, v, raw, rate, taps, marks, segc, segr, dim, count, span):
+    length, width = q.shape
+    groups = width // (dim * count)
+    units = count * (length // span)
+    wide = pl.BlockSpec((length, count * dim), lambda g: (0, g))
+    whole = lambda a: pl.BlockSpec(a.shape, lambda g: (0,) * a.ndim)
+    square = pl.BlockSpec((units, span, span), lambda g: (g, 0, 0))
+    square_shape = jax.ShapeDtypeStruct((units * groups, span, span), HALF)
+    return pl.pallas_call(
+        functools.partial(attn_forward_kernel, span, dim, count, taps.shape[0]),
+        grid=(groups,),
+        in_specs=[
+            wide, wide, wide, wide,
+            pl.BlockSpec((1, count, length), lambda g: (g, 0, 0)),
+            pl.BlockSpec((taps.shape[0], count * dim), lambda g: (0, g)),
+            whole(marks), whole(segc), whole(segr),
+        ],
+        out_specs=[wide, wide, square, square, square],
+        out_shape=[
+            jax.ShapeDtypeStruct((length, width), HALF),
+            jax.ShapeDtypeStruct((length, width), HALF),
+            square_shape, square_shape, square_shape,
+        ],
+        compiler_params=pltpu.CompilerParams(vmem_limit_bytes=56 * 1024 * 1024),
+        name="attend",
+    )(q, k, v, raw, rate, taps, marks, segc, segr)
+
+
+def attn_backward(q, k, v, w, raw, rate, taps, marks, segc, segr, grad, tri, carried, probs, dim, count, span):
+    length, width = q.shape
+    groups = width // (dim * count)
+    units = count * (length // span)
+    wide = pl.BlockSpec((length, count * dim), lambda g: (0, g))
+    whole = lambda a: pl.BlockSpec(a.shape, lambda g: (0,) * a.ndim)
+    square = pl.BlockSpec((units, span, span), lambda g: (g, 0, 0))
+    rates = pl.BlockSpec((1, count, length), lambda g: (g, 0, 0))
+    tap_spec = pl.BlockSpec((taps.shape[0], count * dim), lambda g: (0, g))
+    wide_shape = jax.ShapeDtypeStruct((length, width), HALF)
+    return pl.pallas_call(
+        functools.partial(attn_backward_kernel, span, dim, count, taps.shape[0]),
+        grid=(groups,),
+        in_specs=[
+            wide, wide, wide, wide, wide, rates, tap_spec,
+            whole(marks), whole(segc), whole(segr), wide, square, square, square,
+        ],
+        out_specs=[wide, wide, wide, wide, rates, tap_spec],
+        out_shape=[
+            wide_shape, wide_shape, wide_shape, wide_shape,
+            jax.ShapeDtypeStruct(rate.shape, SINGLE),
+            jax.ShapeDtypeStruct(taps.shape, SINGLE),
+        ],
+        scratch_shapes=[pltpu.VMEM((length, count * dim), SINGLE)],
+        compiler_params=pltpu.CompilerParams(vmem_limit_bytes=56 * 1024 * 1024),
+        name="attend_back",
+    )(q, k, v, w, raw, rate, taps, marks, segc, segr, grad, tri, carried, probs)
 
 epsilon = 1e-06
 highest = lax.Precision.HIGHEST
@@ -10,86 +233,6 @@
 def rms_scale(row_block, gain_row):
     inverse = lax.rsqrt(jnp.mean(row_block * row_block, axis=-1, keepdims=True) + epsilon)
     return row_block * inverse * gain_row
-
-
-def short_conv(house_raw, tap_values, segment):
-    length = house_raw.shape[0]
-    summed = house_raw * tap_values[0]
-    for offset in range(1, tap_values.shape[0]):
-        shifted = jnp.concatenate(
-            [
-                jnp.zeros((offset, house_raw.shape[1]), house_raw.dtype),
-                house_raw[: length - offset],
-            ],
-            axis=0,
-        )
-        seg_shift = jnp.concatenate(
-            [jnp.full((offset,), -1, jnp.int32), segment[: length - offset]]
-        )
-        same_doc = (seg_shift == segment)[:, None]
-        summed = summed + jnp.where(same_doc, shifted * tap_values[offset], 0.0)
-    return summed
-
-
-def unit_rows(mixed_rows, head_count):
-    split_rows = mixed_rows.reshape(mixed_rows.shape[:-1] + (head_count, -1))
-    inverse = lax.rsqrt(jnp.sum(split_rows * split_rows, axis=-1, keepdims=True) + epsilon)
-    return (split_rows * inverse).reshape(mixed_rows.shape)
-
-
-def outer_dot(left_rows, right_rows):
-    return lax.dot_general(
-        left_rows,
-        right_rows,
-        (((1,), (1,)), ((), ())),
-        precision=highest,
-        preferred_element_type=jnp.float32,
-    )
-
-
-def path_head(query_rows, key_rows, value_rows, house_rows, rate_rows, segment):
-    length = query_rows.shape[0]
-    positions = lax.iota(jnp.int32, length)
-    same_doc = segment[:, None] == segment[None, :]
-    inclusive = same_doc & (positions[None, :] <= positions[:, None])
-    strict = same_doc & (positions[None, :] < positions[:, None])
-    lower_part = jnp.where(strict, outer_dot(house_rows, house_rows) * rate_rows[None, :], 0.0)
-    right_side = jnp.where(strict, outer_dot(house_rows, key_rows), 0.0)
-    system = jnp.eye(length, dtype=query_rows.dtype) + lower_part
-    carried = lax.linalg.triangular_solve(
-        system, right_side, left_side=True, lower=True, unit_diagonal=True
-    )
-    reach_part = jnp.where(inclusive, outer_dot(query_rows, house_rows), 0.0) * rate_rows[None, :]
-    scores = (
-        outer_dot(query_rows, key_rows) - jnp.dot(reach_part, carried, precision=highest)
-    ) * query_rows.shape[1] ** (-0.5)
-    scores = jnp.where(inclusive, scores, -1e30)
-    row_max = jnp.max(scores, axis=1, keepdims=True)
-    exp_terms = jnp.where(inclusive, jnp.exp(scores - row_max), 0.0)
-    probabilities = exp_terms / jnp.sum(exp_terms, axis=1, keepdims=True)
-    return jnp.dot(probabilities, value_rows, precision=highest)
-
-
-def path_attention(query_rows, key_rows, value_rows, house_rows, rate_rows, segment, head_count):
-    length, model_width = query_rows.shape
-
-    def by_heads(array):
-        return array.reshape(length, head_count, model_width // head_count).transpose(1, 0, 2)
-
-    def per_head(packed):
-        return path_head(packed[0], packed[1], packed[2], packed[3], packed[4], segment)
-
-    stacked = lax.map(
-        jax.checkpoint(per_head),
-        (
-            by_heads(query_rows),
-            by_heads(key_rows),
-            by_heads(value_rows),
-            by_heads(house_rows),
-            rate_rows.T,
-        ),
-    )
-    return stacked.transpose(1, 0, 2).reshape(length, model_width)
 
 
 def dot_plain(left_rows, right_rows):
@@ -152,9 +295,25 @@
     half = jnp.bfloat16
     single = jnp.float32
     head_count = w_rate.shape[1]
-    segment = doc_ids[0]
-    flat_rows = tokens[0].astype(single)
-    upstream = cotangent[0]
+    length = tokens.shape[1]
+    span = length // 2
+    dim = tokens.shape[2] // head_count
+    doc_row = doc_ids[0]
+    start = jnp.argmax(doc_row[: length - span + 1] == doc_row[span - 1 :])
+    position = lax.iota(jnp.int32, length)
+    source = (position + start) % length
+    turn = (source[:, None] == position[None, :]).astype(half)
+    segment = jnp.sum(jnp.where(turn > 0, doc_row[None, :], 0), axis=1)
+    flat_rows = dot_plain(turn, tokens[0])
+    upstream = dot_plain(turn, cotangent[0]).astype(half)
+    marks = jnp.stack(
+        [
+            ((jnp.roll(segment, k) == segment) & (position >= k)).astype(single)
+            for k in range(conv_taps.shape[0])
+        ],
+        axis=1,
+    )
+    count = 3
     attn_set = fetch_attention(gain_in, w_query, w_key, w_value, w_house, w_rate, conv_taps, w_out)
     feed_set = fetch_feed(gain_mid, w_gate, w_up, w_down)
     gain_one, mat_query, mat_key, mat_value, mat_house, mat_rate, tap_half, mat_out = attn_set
@@ -165,30 +324,15 @@
     key_rows = dot_plain(normed, mat_key).astype(half)
     value_rows = dot_plain(normed, mat_value).astype(half)
     house_raw = dot_plain(normed, mat_house)
-    rate_sig = jax.nn.sigmoid(dot_plain(normed, mat_rate))
-    rate_rows = 2.0 * rate_sig
+    rate_sig = jax.nn.sigmoid(
+        lax.dot_general(mat_rate, normed, (((0,), (1,)), ((), ())), preferred_element_type=single)
+    )
+    rate_rows = (2.0 * rate_sig).reshape(head_count // count, count, length)
     tap_values = tap_half.astype(single)
-
-    def make_house(raw_rows, tap_rows):
-        return unit_rows(short_conv(raw_rows, tap_rows, segment), head_count)
-
-    house_rows = make_house(house_raw, tap_values).astype(half)
-
-    def attend(query_part, key_part, value_part, house_part, rate_part):
-        return path_attention(
-            query_part, key_part, value_part, house_part, rate_part, segment, head_count
-        )
-
-    attn_inputs = (
-        query_rows.astype(single),
-        key_rows.astype(single),
-        value_rows.astype(single),
-        house_rows.astype(single),
-        rate_rows,
-    )
-    attended = attend(
-        attn_inputs[0], attn_inputs[1], attn_inputs[2], attn_inputs[3], attn_inputs[4]
-    ).astype(half)
+    attended, house_rows, tri, carried, probs = attn_forward(
+        query_rows, key_rows, value_rows, house_raw, rate_rows, tap_values, marks,
+        segment[:, None], segment[None, :], dim, count, span,
+    )
     middle = flat_rows + dot_plain(attended, mat_out)
     gain_second = gain_two.astype(single)
     normed_mid = rms_scale(middle, gain_second).astype(half)
@@ -230,17 +374,12 @@
     grad_branch = grad_middle.astype(half)
     grad_wout = dot_left_t(attended, grad_branch)
     grad_attended = dot_right_t(grad_branch, mat_out)
-    unused_attn, attend_back = jax.vjp(
-        attend, attn_inputs[0], attn_inputs[1], attn_inputs[2], attn_inputs[3], attn_inputs[4]
-    )
-    grad_query_f, grad_key_f, grad_value_f, grad_house_f, grad_rate_f = attend_back(grad_attended)
-    grad_query_rows = grad_query_f.astype(half)
-    grad_key_rows = grad_key_f.astype(half)
-    grad_value_rows = grad_value_f.astype(half)
-    unused_house, house_back = jax.vjp(make_house, house_raw, tap_values)
-    grad_house_raw, grad_taps = house_back(grad_house_f)
-    grad_house_rows = grad_house_raw.astype(half)
-    grad_rate_rows = (grad_rate_f * 2.0 * rate_sig * (1.0 - rate_sig)).astype(half)
+    (grad_query_rows, grad_key_rows, grad_value_rows, grad_house_rows, grad_rate_f, grad_taps) = attn_backward(
+        query_rows, key_rows, value_rows, house_rows, house_raw, rate_rows, tap_values, marks,
+        segment[:, None], segment[None, :], grad_attended.astype(half), tri, carried, probs, dim, count, span,
+    )
+    grad_rate_f = grad_rate_f.reshape(head_count, length)
+    grad_rate_rows = (grad_rate_f * 2.0 * rate_sig * (1.0 - rate_sig)).astype(half).T
     grad_wquery = dot_left_t(normed, grad_query_rows)
     grad_wkey = dot_left_t(normed, grad_key_rows)
     grad_wvalue = dot_left_t(normed, grad_value_rows)
@@ -296,6 +435,10 @@
         lax.psum(feed_grads[2].astype(jnp.bfloat16), "grp").astype(jnp.float32),
         lax.psum(feed_grads[3].astype(jnp.bfloat16), "grp").astype(jnp.float32),
     )
+    result = dot_left_t(turn, result).astype(half)
+    high = grad_tokens.astype(half)
+    low = (grad_tokens - high.astype(single)).astype(half)
+    grad_tokens = dot_left_t(turn, high) + dot_left_t(turn, low)
     return (
         result[None],
         grad_tokens[None],

time: 3130 us -> 1840 us (0.59)
  other arithmetic: 792 us -> 58.4 us
  matrix products: 789 us -> 198 us
  waiting for transfers between devices: 1010 us -> 1400 us
  local copies, waits for them, and re-layouts: 405 us -> 18.5 us
  Pallas kernels: 0 us -> 68.7 us
    another operation x108 -> x2, other arithmetic: 708 us -> 0.72 us  [the longest x1 0.65 us: local(): start = jnp.argmax(doc_row[:length - span + 1] == doc_row[span - 1:])]
    dot_general x288 -> x1, matrix products: 439 us -> 1.1 us  [local(): lax.dot_general(mat_rate, normed, (((0,), (1,)), ((), ())), preferred_ele...]
    another operation x433 -> x2, local copies, waits for them, and re-layouts: 209 us -> 0.83 us  [local(): jnp.stack([((jnp.roll(segment, k) == segment) & (position >= k)).astype(s...]
    another operation x240 -> x0, matrix products: 172 us -> none  [path_head(): lax.linalg.triangular_solve(system, right_side, left_side=True, lower=Tru...]
    all_gather x1, waiting for transfers between devices: 0.02 us -> 118 us  [fetch_feed(): lax.all_gather(w_gate.astype(half), 'fsdp', axis=0, tiled=True)]
    all_gather x1, waiting for transfers between devices: 0.01 us -> 113 us  [fetch_feed(): lax.all_gather(w_up.astype(half), 'fsdp', axis=0, tiled=True)]
    all_gather x1, waiting for transfers between devices: 0.01 us -> 113 us  [fetch_feed(): lax.all_gather(w_down.astype(half), 'fsdp', axis=0, tiled=True)]
    dynamic_update_slice x84 -> x0, local copies, waits for them, and re-layouts: 73.1 us -> none  [path_attention(): lax.map(jax.checkpoint(per_head), (by_heads(query_rows), by_heads(key_row...]
  transfers between devices with their start and end apart: 19 -> 19, of which waited for: 12 -> 16; matrix products, arithmetic and copies ran while one was open for 28% -> 10% of each run, Pallas kernels for 0% -> 2%
where the time goes in v1:
time: 1840 us
  waiting for transfers between devices  1400 us (76%)
  matrix products  198 us (11%)
  blocking collectives  71.8 us (4%)
  Pallas kernels  68.7 us (4%)
  other arithmetic  58.4 us (3%)
  local copies, waits for them, and re-layouts  18.5 us (1%)
    psum x1, waiting for transfers between devices, local(): lax.psum(attn_grads[1].astype(jnp.bfloat16), 'grp').astype(jnp.float32)  280 us
    reduce_scatter x1, waiting for transfers between devices, local(): lax.psum_scatter(grad_gate.astype(jnp.bfloat16), 'fsdp', scatter_dimensio...  124 us
    reduce_scatter x1, waiting for transfers between devices, local(): lax.psum_scatter(grad_down.astype(jnp.bfloat16), 'fsdp', scatter_dimensio...  124 us
    reduce_scatter x1, waiting for transfers between devices, local(): lax.psum_scatter(grad_up.astype(jnp.bfloat16), 'fsdp', scatter_dimension=...  124 us
    all_gather x1, waiting for transfers between devices, fetch_feed(): lax.all_gather(w_gate.astype(half), 'fsdp', axis=0, tiled=True)  118 us
    all_gather x1, waiting for transfers between devices, fetch_feed(): lax.all_gather(w_up.astype(half), 'fsdp', axis=0, tiled=True)  113 us
    all_gather x1, waiting for transfers between devices, fetch_feed(): lax.all_gather(w_down.astype(half), 'fsdp', axis=0, tiled=True)  113 us
    dot_general x12, matrix products, dot_left_t(): lax.dot_general(left_rows, right_rows, (((0,), (0,)), ((), ())), preferre...  79.1 us
  transfers between devices with their start and end apart: 19, of which 16 were waited for; matrix products, arithmetic and copies ran while one was open for 10% of the time, Pallas kernels for 2%

profile of v1, /device:TPU:0, one launch (start us, length us, event | category | flops | bytes accessed | tf_op | source)
XLA Modules:
  0.0 1836.3 jit_solution(551436017196458881)
XLA Ops:
  18.7 5.7 convert_element_type.261
  24.4 4.9 convert_element_type.262
  29.4 4.8 convert_element_type.264
  38.3 9.4 all-gather
  47.8 8.7 all_gather.50
  61.5 7.3 all_gather.51
  73.4 8.0 all-gather.1
  85.9 5.3 convolution_convert_fusion.11.q_ref
  91.3 39.1 %all-gather.13.cloned.1.call-done = bf16[1536,1536]{1,0:T(8,128)(2,1)} async-done(((bf16[384,1536]{1,0:T(8,128)(2,1)}), bf16[1536,1536]{1,0:T(8,128)(2,1)}) %all-gather.13.cloned.1.call-update) | async-done | bytes 4718608 | tf_op jit(solution)/shard_map/all_gather | solution.py:259
  130.4 5.4 convolution_convert_fusion.10.k_ref
  135.8 54.2 %all-gather.15.cloned.1.call-done = bf16[1536,1536]{1,0:T(8,128)(2,1)} async-done(((bf16[384,1536]{1,0:T(8,128)(2,1)}), bf16[1536,1536]{1,0:T(8,128)(2,1)}) %all-gather.15.cloned.1.call-update) | async-done | bytes 4718608 | tf_op jit(solution)/shard_map/all_gather | solution.py:260
  189.9 5.4 convolution_convert_fusion.9.v_ref
  195.3 54.0 %all-gather.17.cloned.1.call-done = bf16[1536,1536]{1,0:T(8,128)(2,1)} async-done(((bf16[384,1536]{1,0:T(8,128)(2,1)}), bf16[1536,1536]{1,0:T(8,128)(2,1)}) %all-gather.17.cloned.1.call-update) | async-done | bytes 4718608 | tf_op jit(solution)/shard_map/all_gather | solution.py:261
  249.3 5.7 fusion.28.raw_ref
  255.0 36.1 %attend.1 = (bf16[384,1536]{1,0:T(8,128)(2,1)}, bf16[384,1536]{1,0:T(8,128)(2,1)}, bf16[24,192,192]{2,1,0:T(8,128)(2,1)}, bf16[24,192,192]{2,1,0:T(8,128)(2,1)}, bf16[24,192,192]{2,1,0:T(8,128)(2,1)}) custom-call(bf16[384,1536]{1,0:T(8,128)(2,1)} %convolution_convert_fusion.11.q_ref, bf16[384,1536]{1,0:T(8,128)(2,1)} %convolution_convert_fusion.10.k_ref, ...), custom_call_target="tpu_custom_call" | custom-call | tf_op jit(solution)/shard_map/attend/pallas_call | solution.py:181
  291.1 17.6 all-gather.19.cloned.1.call-done
  308.7 4.8 multiply_reduce_fusion.4
  315.1 118.3 %all-gather.21.cloned.1.call-done = bf16[1536,4096]{1,0:T(8,128)(2,1)} async-done(((bf16[384,4096]{1,0:T(8,128)(2,1)}), bf16[1536,4096]{1,0:T(8,128)(2,1)}) %all-gather.21.cloned.1.call-update) | async-done | bytes 12582928 | tf_op jit(solution)/shard_map/all_gather | solution.py:272
  433.5 11.6 fusion.29
  445.1 113.3 %all-gather.23.cloned.1.call-done = bf16[1536,4096]{1,0:T(8,128)(2,1)} async-done(((bf16[384,4096]{1,0:T(8,128)(2,1)}), bf16[1536,4096]{1,0:T(8,128)(2,1)}) %all-gather.23.cloned.1.call-update) | async-done | bytes 12582928 | tf_op jit(solution)/shard_map/all_gather | solution.py:273
  558.5 11.8 fusion.30
  570.3 113.1 %all-gather.25.cloned.1.call-done = bf16[4096,1536]{1,0:T(8,128)(2,1)} async-done(((bf16[1024,1536]{1,0:T(8,128)(2,1)}), bf16[4096,1536]{1,0:T(8,128)(2,1)}) %all-gather.25.cloned.1.call-update) | async-done | bytes 12582928 | tf_op jit(solution)/shard_map/all_gather | solution.py:274
  683.4 20.3 %multiply_convert_fusion = (bf16[384,4096]{1,0:T(8,128)(2,1)}, bf16[384,4096]{1,0:T(8,128)(2,1)}, bf16[384,4096]{1,0:T(8,128)(2,1)}) fusion(f32[384,4096]{1,0:T(8,128)} %fusion.29, f32[384,4096]{1,0:T(8,128)} %fusion.30, bf16[384,1536]{1,0:T(8,128)(2,1)S(1)} %copy-done.8, bf16[4096,1536]{1,0:T(8,128)(2,1)} %all-gather.25.cloned.1.call-done), kind=kOutput, calls=%fused_computation.8 | convolution fusion | flops 4857004032 | bytes 35782656 | tf_op jit(solution)/shard_map/dot_general | solution.py:249
  703.8 14.8 fusion.31
  718.6 10.0 multiply_reduce_fusion
  732.3 32.6 %attend_back.1 = (bf16[384,1536]{1,0:T(8,128)(2,1)}, bf16[384,1536]{1,0:T(8,128)(2,1)}, bf16[384,1536]{1,0:T(8,128)(2,1)}, bf16[384,1536]{1,0:T(8,128)(2,1)}, f32[4,3,384]{2,1,0:T(4,128)}, /*index=5*/f32[4,1536]{1,0:T(4,128)}) custom-call(bf16[384,1536]{1,0:T(8,128)(2,1)} %convolution_convert_fusion.11.q_ref, ...), custom_call_target="tpu_custom_call" | custom-call | tf_op jit(solution)/shard_map/attend_back/pallas_call | solution.py:211
  764.9 5.6 convolution_convert_fusion.7
  770.5 5.6 convolution_convert_fusion.6
  776.1 6.1 convolution_convert_fusion.5
  782.3 5.5 convolution_convert_fusion.4
  787.9 5.7 convolution_convert_fusion.3
  794.9 11.5 convolution_convert_fusion.2
  806.5 11.6 convolution_convert_fusion.1
  819.3 11.9 convolution_convert_fusion
  834.5 53.8 %reduce-scatter.17.cloned.1.call-done = bf16[384,1536]{1,0:T(8,128)(2,1)} async-done(((bf16[1536,1536]{1,0:T(8,128)(2,1)}), bf16[384,1536]{1,0:T(8,128)(2,1)}) %reduce-scatter.17.cloned.1.call-update) | async-done | bytes 1179664 | tf_op jit(solution)/shard_map/reduce_scatter | solution.py:405
  888.3 60.7 %reduce-scatter.19.cloned.1.call-done = bf16[384,1536]{1,0:T(8,128)(2,1)} async-done(((bf16[1536,1536]{1,0:T(8,128)(2,1)}), bf16[384,1536]{1,0:T(8,128)(2,1)}) %reduce-scatter.19.cloned.1.call-update) | async-done | bytes 1179664 | tf_op jit(solution)/shard_map/reduce_scatter | solution.py:408
  949.0 60.0 %reduce-scatter.21.cloned.1.call-done = bf16[384,1536]{1,0:T(8,128)(2,1)} async-done(((bf16[1536,1536]{1,0:T(8,128)(2,1)}), bf16[384,1536]{1,0:T(8,128)(2,1)}) %reduce-scatter.21.cloned.1.call-update) | async-done | bytes 1179664 | tf_op jit(solution)/shard_map/reduce_scatter | solution.py:411
  1008.9 60.1 %reduce-scatter.23.cloned.1.call-done = bf16[384,1536]{1,0:T(8,128)(2,1)} async-done(((bf16[1536,1536]{1,0:T(8,128)(2,1)}), bf16[384,1536]{1,0:T(8,128)(2,1)}) %reduce-scatter.23.cloned.1.call-update) | async-done | bytes 1179664 | tf_op jit(solution)/shard_map/reduce_scatter | solution.py:420
  1069.1 123.7 %reduce-scatter.25.cloned.1.call-done = bf16[384,4096]{1,0:T(8,128)(2,1)} async-done(((bf16[1536,4096]{1,0:T(8,128)(2,1)}), bf16[384,4096]{1,0:T(8,128)(2,1)}) %reduce-scatter.25.cloned.1.call-update) | async-done | bytes 3145744 | tf_op jit(solution)/shard_map/reduce_scatter | solution.py:363
  1192.8 123.7 %reduce-scatter.27.cloned.1.call-done = bf16[384,4096]{1,0:T(8,128)(2,1)} async-done(((bf16[1536,4096]{1,0:T(8,128)(2,1)}), bf16[384,4096]{1,0:T(8,128)(2,1)}) %reduce-scatter.27.cloned.1.call-update) | async-done | bytes 3145744 | tf_op jit(solution)/shard_map/reduce_scatter | solution.py:366
  1316.5 123.7 %reduce-scatter.29.cloned.1.call-done = bf16[1024,1536]{1,0:T(8,128)(2,1)} async-done(((bf16[4096,1536]{1,0:T(8,128)(2,1)}), bf16[1024,1536]{1,0:T(8,128)(2,1)}) %reduce-scatter.29.cloned.1.call-update) | async-done | bytes 3145744 | tf_op jit(solution)/shard_map/reduce_scatter | solution.py:369
  1442.1 4.5 fusion.32
  1446.7 4.6 convolution_add_fusion.4
  1457.8 9.4 all-reduce.4
  1473.6 12.3 fusion.2
  1486.8 8.7 reduce-scatter.31.cloned.1.call-done
  1496.5 29.0 %all-reduce.2 = (bf16[384]{0:T(512)(128)(2,1)S(1)}, bf16[384,12]{0,1:T(8,128)(2,1)S(1)}, bf16[4,384]{1,0:T(4,128)(2,1)S(1)}, bf16[384]{0:T(512)(128)(2,1)S(1)}) all-reduce(bf16[384]{0:T(512)(128)(2,1)S(1)} %dynamic-slice.1, bf16[384,12]{0,1:T(8,128)(2,1)S(1)} %copy.50, ...), channel_id=1, replica_groups=mesh['grp'=8,'fsdp'=4] {'grp'}, use_global_device_ids=true, to_apply=%region_8.9 | all-reduce | flops 6912 | bytes 27648 | tf_op jit(solution)/shard_map/psum | solution.py:425
  1527.9 280.0 %all-reduce.7.cloned.1.call-done = (bf16[384,1536]{1,0:T(8,128)(2,1)}, bf16[384,1536]{1,0:T(8,128)(2,1)}, bf16[384,1536]{1,0:T(8,128)(2,1)}, bf16[384,1536]{1,0:...) async-done(((bf16[384,1536]{1,0:T(8,128)(2,1)}, bf16[384,1536]{1,0:T(8,128)(2,1)}, ...) | async-done | bytes 15335440 | tf_op jit(solution)/shard_map/psum | solution.py:426
  (222 shorter events, 80.6 us)
Async XLA Ops:
  7.2 49.4 %copy-start = (bf16[1,384,1536]{2,1,0:T(8,128)(2,1)S(1)}, bf16[1,384,1536]{2,1,0:T(8,128)(2,1)}, u32[]{:S(2)}) copy-start(bf16[1,384,1536]{2,1,0:T(8,128)(2,1)} %param.15) | copy-start | bytes 3538948
  7.2 3.1 copy-start.14
  7.2 78.7 %all-gather.11.cloned.1.call-start = ((), (), s32[]{:S(2)}) async-start(), calls=%async_computation.10 | async-start | bytes 5898240 | tf_op jit(solution)/shard_map/all_gather | solution.py:258
  10.2 120.2 %all-gather.13.cloned.1.call-start = ((), (), s32[]{:S(2)}) async-start(), calls=%async_computation.11 | async-start | bytes 5898240 | tf_op jit(solution)/shard_map/all_gather | solution.py:259
  11.5 3.1 copy-start.15
  11.5 178.4 %all-gather.15.cloned.1.call-start = ((), (), s32[]{:S(2)}) async-start(), calls=%async_computation.12 | async-start | bytes 5898240 | tf_op jit(solution)/shard_map/all_gather | solution.py:260
  14.5 234.8 %all-gather.17.cloned.1.call-start = ((), (), s32[]{:S(2)}) async-start(), calls=%async_computation.13 | async-start | bytes 5898240 | tf_op jit(solution)/shard_map/all_gather | solution.py:261
  15.7 293.0 %all-gather.19.cloned.1.call-start = ((), (), s32[]{:S(2)}) async-start(), calls=%async_computation.14 | async-start | bytes 5898240 | tf_op jit(solution)/shard_map/all_gather | solution.py:264
  18.6 414.9 %all-gather.21.cloned.1.call-start = ((), (), s32[]{:S(2)}) async-start(), calls=%async_computation.15 | async-start | bytes 15728640 | tf_op jit(solution)/shard_map/all_gather | solution.py:272
  24.4 534.1 %all-gather.23.cloned.1.call-start = ((), (), s32[]{:S(2)}) async-start(), calls=%async_computation.16 | async-start | bytes 15728640 | tf_op jit(solution)/shard_map/all_gather | solution.py:273
  29.3 654.1 %all-gather.25.cloned.1.call-start = ((), (), s32[]{:S(2)}) async-start(), calls=%async_computation.17 | async-start | bytes 15728640 | tf_op jit(solution)/shard_map/all_gather | solution.py:274
  34.2 4.1 copy-start.38
  34.2 13.6 copy-start.31
  34.2 800.2 %reduce-scatter.15.cloned.1.call-start = ((), (), s32[]{:S(2)}) async-start(), calls=%async_computation.18 | async-start | bytes 5898240 | tf_op jit(solution)/shard_map/reduce_scatter | solution.py:402
  36.3 46.4 %copy-start.27 = (s32[384]{0:T(512)}, s32[384]{0:T(512)S(1)}, u32[]{:S(2)}) copy-start(s32[384]{0:T(512)S(1)} %add_select_fusion) | copy-start | bytes 4612
  47.8 10.5 copy-start.24
  57.4 251.2 %copy-start.2 = (f32[384,1536]{1,0:T(8,128)}, f32[384,1536]{1,0:T(8,128)S(1)}, u32[]{:S(2)}) copy-start(f32[384,1536]{1,0:T(8,128)S(1)} %get-tuple-element.63) | copy-start | bytes 7077892
  315.1 243.3 %copy-start.16 = (bf16[384,1536]{1,0:T(8,128)(2,1)}, bf16[384,1536]{1,0:T(8,128)(2,1)S(1)}, u32[]{:S(2)}) copy-start(bf16[384,1536]{1,0:T(8,128)(2,1)S(1)} %multiply_convert_fusion.3) | copy-start | bytes 3538948
  445.1 238.3 %copy-start.8 = (bf16[384,1536]{1,0:T(8,128)(2,1)S(1)}, bf16[384,1536]{1,0:T(8,128)(2,1)}, u32[]{:S(2)}) copy-start(bf16[384,1536]{1,0:T(8,128)(2,1)} %convolution_convert_fusion.12) | copy-start | bytes 3538948
  703.8 14.8 copy-start.6
  703.8 14.8 copy-start.44
  703.8 25.5 %slice-start.4 = ((s8[4718592]{0:T(1024)(128)(4,1)}), s8[4194304]{0:T(1024)(128)(4,1)S(1)}, s32[]{:S(2)}) async-start(s8[4718592]{0:T(1024)(128)(4,1)} %bitcast.88), calls=%async_computation.33 | async-start | bytes 8388608
  718.6 10.0 copy-start.9
  718.6 10.7 slice-start.5
  729.3 58.6 %copy-start.4 = (f32[384,1536]{1,0:T(8,128)}, f32[384,1536]{1,0:T(8,128)S(1)}, u32[]{:S(2)}) copy-start(f32[384,1536]{1,0:T(8,128)S(1)} %fusion.3) | copy-start | bytes 7077892
  770.5 117.8 %reduce-scatter.17.cloned.1.call-start = ((), (), s32[]{:S(2)}) async-start(), calls=%async_computation.19 | async-start | bytes 5898240 | tf_op jit(solution)/shard_map/reduce_scatter | solution.py:405
  776.1 172.9 %reduce-scatter.19.cloned.1.call-start = ((), (), s32[]{:S(2)}) async-start(), calls=%async_computation.20 | async-start | bytes 5898240 | tf_op jit(solution)/shard_map/reduce_scatter | solution.py:408
  782.2 226.7 %reduce-scatter.21.cloned.1.call-start = ((), (), s32[]{:S(2)}) async-start(), calls=%async_computation.21 | async-start | bytes 5898240 | tf_op jit(solution)/shard_map/reduce_scatter | solution.py:411
  787.8 281.2 %reduce-scatter.23.cloned.1.call-start = ((), (), s32[]{:S(2)}) async-start(), calls=%async_computation.22 | async-start | bytes 5898240 | tf_op jit(solution)/shard_map/reduce_scatter | solution.py:420
  793.6 399.2 %reduce-scatter.25.cloned.1.call-start = ((), (), s32[]{:S(2)}) async-start(), calls=%async_computation.23 | async-start | bytes 15728640 | tf_op jit(solution)/shard_map/reduce_scatter | solution.py:363
  806.4 510.1 %reduce-scatter.27.cloned.1.call-start = ((), (), s32[]{:S(2)}) async-start(), calls=%async_computation.24 | async-start | bytes 15728640 | tf_op jit(solution)/shard_map/reduce_scatter | solution.py:366
  818.1 622.1 %reduce-scatter.29.cloned.1.call-start = ((), (), s32[]{:S(2)}) async-start(), calls=%async_computation.25 | async-start | bytes 15728640 | tf_op jit(solution)/shard_map/reduce_scatter | solution.py:369
  831.3 654.5 %reduce-scatter.33.cloned.1.call-start = ((), (), s32[]{:S(2)}) async-start(), calls=%async_computation.27 | async-start | bytes 491520
  833.1 662.5 %reduce-scatter.31.cloned.1.call-start = ((), (), s32[]{:S(2)}) async-start(), calls=%async_computation.26 | async-start | bytes 491520
  834.4 973.5 %all-reduce.7.cloned.1.call-start = ((), (), s32[]{:S(2)}) async-start(), calls=%async_computation.28 | async-start | bytes 30670848 | tf_op jit(solution)/shard_map/psum | solution.py:426
  1442.1 4.5 copy-start.41
  1442.1 9.2 slice-start
  1446.6 4.6 slice-start.1
  1446.7 4.6 copy-start.40
  1446.7 6.8 slice-start.2
  1455.6 11.8 copy-start.35
  1467.4 2.9 copy-start.28
  1471.3 2.3 copy-start.7
  1807.9 3.1 copy-start.21
  1816.1 2.7 copy-start.13
  1818.8 3.5 copy-start.12
  1822.3 3.5 copy-start.11
  1825.8 3.6 copy-start.1
  (22 other events, 34.2 us)
Sparse Core Ops, SparseCore 0:
  10.5 60.3 all-gather.10
  73.3 57.0 all-gather.12
  132.8 57.0 all-gather.14
  192.2 57.0 all-gather.16
  251.6 57.0 all-gather.18
  310.9 122.5 all-gather.20
  435.9 122.5 all-gather.22
  560.9 122.5 all-gather.24
  770.6 57.0 reduce-scatter.14
  831.1 57.0 reduce-scatter.16
  891.8 57.0 reduce-scatter.18
  951.8 57.0 reduce-scatter.20
  1011.9 57.0 reduce-scatter.22
  1072.0 120.7 reduce-scatter.24
  1195.7 120.7 reduce-scatter.26
  1319.4 120.7 reduce-scatter.28
  1443.4 24.3 reduce-scatter.32
  1471.1 24.4 reduce-scatter.30
  1498.5 309.3 all-reduce.6

commit v2 on v1

v2 whole, which is shorter than its diff:
```python
import functools
import jax
import jax.numpy as jnp
from jax import lax
from jax.experimental import pallas as pl
from jax.experimental.pallas import tpu as pltpu
from jax.sharding import PartitionSpec as P

EPS = 1e-06
HALF = jnp.bfloat16
SINGLE = jnp.float32


def mm(left, right):
    return lax.dot_general(left, right, (((1,), (0,)), ((), ())), preferred_element_type=SINGLE)


def mm_nt(left, right):
    return lax.dot_general(left, right, (((1,), (1,)), ((), ())), preferred_element_type=SINGLE)


def mm_tn(left, right):
    return lax.dot_general(left, right, (((0,), (0,)), ((), ())), preferred_element_type=SINGLE)


def conv_parts(raw, taps, marks, taps_count):
    shifted = [raw]
    total = raw * taps[0:1, :]
    for k in range(1, taps_count):
        moved = pltpu.roll(raw, k, 0) * marks[:, k : k + 1]
        shifted.append(moved)
        total = total + moved * taps[k : k + 1, :]
    return shifted, total


def attn_forward_kernel(
    span, dim, count, taps_count, number, *refs
):
    normed_ref = refs[0]
    piece_refs = refs[1 : 1 + number]
    rate_ref, taps_ref, marks_ref, segc_ref, segr_ref = refs[1 + number : 6 + number]
    out_ref, qkv_ref, raw_ref, w_ref, t_ref, c_ref, p_ref = refs[6 + number :]
    blocks = normed_ref.shape[0] // span
    wide = count * dim
    depth = normed_ref.shape[1] // number
    for m in (3, 0, 1, 2):
        total = mm(normed_ref[:, :depth], piece_refs[0][:, m * wide : (m + 1) * wide])
        for r in range(1, number):
            total = total + mm(
                normed_ref[:, r * depth : (r + 1) * depth], piece_refs[r][:, m * wide : (m + 1) * wide]
            )
        if m == 3:
            raw_ref[...] = total
        else:
            qkv_ref[:, m * wide : (m + 1) * wide] = total.astype(HALF)
    q_ref, k_ref, v_ref = [qkv_ref.at[:, m * wide : (m + 1) * wide] for m in range(3)]
    marks = marks_ref[...]
    row_id = lax.broadcasted_iota(jnp.int32, (span, span), 0)
    col_id = lax.broadcasted_iota(jnp.int32, (span, span), 1)
    eye = jnp.where(row_id == col_id, 1.0, 0.0)
    sizes = []
    size = 1
    while size < span:
        sizes.append(size)
        size *= 2
    level_of = {}
    for size in sizes:
        level_of[size] = ((row_id // (2 * size)) == (col_id // (2 * size))) & (
            (row_id // size) > (col_id // size)
        )
    strict = []
    inclusive = []
    for u in range(blocks):
        rows = slice(u * span, (u + 1) * span)
        same = segc_ref[rows, 0:1] == segr_ref[0:1, rows]
        strict.append(same & (col_id < row_id))
        inclusive.append(same & (col_id <= row_id))
    for h in range(count):
        cols = slice(h * dim, (h + 1) * dim)
        shifted, mixed = conv_parts(raw_ref[:, cols], taps_ref[:, cols], marks, taps_count)
        inverse = lax.rsqrt(jnp.sum(mixed * mixed, axis=-1, keepdims=True) + EPS)
        w_ref[:, cols] = (mixed * inverse).astype(HALF)
    units = [(h, u) for h in range(count) for u in range(blocks)]
    rates = {}
    lower = {}
    inv = {}
    for h, u in units:
        rows = slice(u * span, (u + 1) * span)
        cols = slice(h * dim, (h + 1) * dim)
        w = w_ref[rows, cols]
        rates[h, u] = rate_ref[h : h + 1, rows]
        lw = jnp.where(strict[u], mm_nt(w, w) * rates[h, u], 0.0)
        lower[h, u] = lw.astype(HALF)
        inv[h, u] = eye - jnp.where(level_of[1], lw, 0.0)
    for size in sizes[1:]:
        half_inv = {}
        inner = {}
        for unit in units:
            half_inv[unit] = inv[unit].astype(HALF)
            inner[unit] = mm(jnp.where(level_of[size], lower[unit], jnp.zeros_like(lower[unit])), half_inv[unit])
        for unit in units:
            inv[unit] = inv[unit] - mm(half_inv[unit], inner[unit].astype(HALF))
    for h, u in units:
        rows = slice(u * span, (u + 1) * span)
        cols = slice(h * dim, (h + 1) * dim)
        w = w_ref[rows, cols]
        q = q_ref[rows, cols]
        k = k_ref[rows, cols]
        tri = inv[h, u].astype(HALF)
        t_ref[h * blocks + u] = tri
        right = jnp.where(strict[u], mm_nt(w, k), 0.0).astype(HALF)
        carried = mm(tri, right).astype(HALF)
        c_ref[h * blocks + u] = carried
        reach = (jnp.where(inclusive[u], mm_nt(q, w), 0.0) * rates[h, u]).astype(HALF)
        scores = (mm_nt(q, k) - mm(reach, carried)) * dim ** (-0.5)
        scores = jnp.where(inclusive[u], scores, -1e30)
        terms = jnp.exp(scores - jnp.max(scores, axis=1, keepdims=True))
        probs = (terms / jnp.sum(terms, axis=1, keepdims=True)).astype(HALF)
        p_ref[h * blocks + u] = probs
        out_ref[rows, cols] = mm(probs, v_ref[rows, cols]).astype(HALF)


def attn_backward_kernel(
    span, dim, count, taps_count,
    qkv_ref, w_ref, raw_ref, rate_ref, taps_ref, marks_ref, segc_ref, segr_ref, grad_ref, t_ref, c_ref, p_ref,
    out_ref, drate_ref, dtaps_ref, dw_ref,
):
    blocks = qkv_ref.shape[0] // span
    wide = count * dim
    q_ref, k_ref, v_ref = [qkv_ref.at[:, m * wide : (m + 1) * wide] for m in range(3)]
    dq_ref, dk_ref, dv_ref, draw_ref = [out_ref.at[:, m * wide : (m + 1) * wide] for m in range(4)]
    marks = marks_ref[...]
    row_id = lax.broadcasted_iota(jnp.int32, (span, span), 0)
    col_id = lax.broadcasted_iota(jnp.int32, (span, span), 1)
    scale = dim ** (-0.5)
    for u in range(blocks):
        rows = slice(u * span, (u + 1) * span)
        same = segc_ref[rows, 0:1] == segr_ref[0:1, rows]
        strict = same & (col_id < row_id)
        inclusive = same & (col_id <= row_id)
        for h in range(count):
            cols = slice(h * dim, (h + 1) * dim)
            unit = h * blocks + u
            q = q_ref[rows, cols]
            k = k_ref[rows, cols]
            v = v_ref[rows, cols]
            w = w_ref[rows, cols]
            grad = grad_ref[0, rows, cols]
            rate = rate_ref[h : h + 1, rows]
            probs = p_ref[unit]
            carried = c_ref[unit]
            tri = t_ref[unit]
            dprobs = mm_nt(grad, v)
            dv_ref[rows, cols] = mm_tn(probs, grad).astype(HALF)
            probs = probs.astype(SINGLE)
            weighted = probs * dprobs
            dscore = ((weighted - probs * jnp.sum(weighted, axis=1, keepdims=True)) * scale).astype(HALF)
            reach_raw = jnp.where(inclusive, mm_nt(q, w), 0.0)
            reach = (reach_raw * rate).astype(HALF)
            dreach = -mm_nt(dscore, carried)
            drate = jnp.sum(dreach * reach_raw, axis=0, keepdims=True)
            dreach = (jnp.where(inclusive, dreach, 0.0) * rate).astype(HALF)
            dcarried = (-mm_tn(reach, dscore)).astype(HALF)
            dright = jnp.where(strict, mm_tn(tri, dcarried), 0.0).astype(HALF)
            dlower = jnp.where(strict, -mm_nt(dright, carried), 0.0)
            drate = drate + jnp.sum(dlower * mm_nt(w, w), axis=0, keepdims=True)
            dlower = (dlower * rate).astype(HALF)
            dq_ref[rows, cols] = (mm(dscore, k) + mm(dreach, w)).astype(HALF)
            dk_ref[rows, cols] = (mm_tn(dscore, q) + mm_tn(dright, w)).astype(HALF)
            dw_ref[rows, cols] = mm_tn(dreach, q) + mm(dright, k) + mm(dlower, w) + mm_tn(dlower, w)
            drate_ref[h : h + 1, rows] = drate
    length = q_ref.shape[0]
    for h in range(count):
        cols = slice(h * dim, (h + 1) * dim)
        taps = taps_ref[:, cols]
        shifted, mixed = conv_parts(raw_ref[:, cols], taps, marks, taps_count)
        inverse = lax.rsqrt(jnp.sum(mixed * mixed, axis=-1, keepdims=True) + EPS)
        unit_rows = mixed * inverse
        dw = dw_ref[:, cols]
        dmixed = inverse * (dw - unit_rows * jnp.sum(dw * unit_rows, axis=-1, keepdims=True))
        draw = dmixed * taps[0:1, :]
        dtaps = [jnp.sum(dmixed * shifted[0], axis=0, keepdims=True)]
        for k in range(1, taps_count):
            dtaps.append(jnp.sum(dmixed * shifted[k], axis=0, keepdims=True))
            draw = draw + pltpu.roll(dmixed * marks[:, k : k + 1], length - k, 0) * taps[k : k + 1, :]
        draw_ref[:, cols] = draw.astype(HALF)
        dtaps_ref[:, cols] = jnp.concatenate(dtaps, axis=0)


def attn_forward(normed, pieces, rate, taps, marks, segc, segr, dim, span):
    length = normed.shape[0]
    count = rate.shape[0]
    wide = count * dim
    units = count * (length // span)
    square = jax.ShapeDtypeStruct((units, span, span), HALF)
    return pl.pallas_call(
        functools.partial(attn_forward_kernel, span, dim, count, taps.shape[0], len(pieces)),
        out_shape=[
            jax.ShapeDtypeStruct((length, wide), HALF),
            jax.ShapeDtypeStruct((length, 3 * wide), HALF),
            jax.ShapeDtypeStruct((length, wide), SINGLE),
            jax.ShapeDtypeStruct((length, wide), HALF),
            square, square, square,
        ],
        compiler_params=pltpu.CompilerParams(vmem_limit_bytes=48 * 1024 * 1024),
        cost_estimate=pl.CostEstimate(flops=16000000000, bytes_accessed=12000000, transcendentals=0),
        name="attend",
    )(normed, *pieces, rate, taps, marks, segc, segr)


def attn_backward(qkv, w, raw, rate, taps, marks, segc, segr, grads, group, tri, carried, probs, dim, span):
    length = qkv.shape[0]
    count = rate.shape[0]
    wide = count * dim
    whole = lambda a: pl.BlockSpec(a.shape, lambda g: (0,) * a.ndim)
    small = lambda shape: pl.BlockSpec(shape, lambda g: (0, 0))
    return pl.pallas_call(
        functools.partial(attn_backward_kernel, span, dim, count, taps.shape[0]),
        grid=(1,),
        in_specs=[whole(a) for a in (qkv, w, raw, rate, taps, marks, segc, segr)]
        + [pl.BlockSpec((1, length, wide), lambda g: (group, 0, 0))]
        + [whole(a) for a in (tri, carried, probs)],
        out_specs=[small((length, 4 * wide)), small(rate.shape), small(taps.shape)],
        out_shape=[
            jax.ShapeDtypeStruct((length, 4 * wide), HALF),
            jax.ShapeDtypeStruct(rate.shape, SINGLE),
            jax.ShapeDtypeStruct(taps.shape, SINGLE),
        ],
        scratch_shapes=[pltpu.VMEM((length, wide), SINGLE)],
        compiler_params=pltpu.CompilerParams(vmem_limit_bytes=48 * 1024 * 1024),
        cost_estimate=pl.CostEstimate(flops=12000000000, bytes_accessed=8000000, transcendentals=0),
        name="attend_back",
    )(qkv, w, raw, rate, taps, marks, segc, segr, grads, tri, carried, probs)


def leave_kernel(part, half, *refs):
    place_ref, rows_ref, gain_ref = refs[:3]
    group_refs = refs[3:7]
    own_refs = refs[7:11]
    other_refs = refs[11:15]
    attended_ref, middle_ref, normed_ref = refs[15:]
    for i in range(4):
        at = pl.multiple_of(place_ref[i] * part, part)
        attended_ref[:, pl.ds(at, part)] = group_refs[i][...]
    own_at = pl.multiple_of(place_ref[4], half)
    other_at = pl.multiple_of(half - place_ref[4], half)
    for at, pieces in ((own_at, own_refs), (other_at, other_refs)):
        total = mm(attended_ref[:, :part], pieces[0][...])
        for r in range(1, 4):
            total = total + mm(attended_ref[:, r * part : (r + 1) * part], pieces[r][...])
        middle_ref[:, pl.ds(at, half)] = rows_ref[:, pl.ds(at, half)] + total
    middle = middle_ref[...]
    inverse = lax.rsqrt(jnp.mean(middle * middle, axis=-1, keepdims=True) + EPS)
    normed_ref[...] = (middle * inverse * gain_ref[...]).astype(HALF)


def leave_attention(places, rows, gain, groups, own, other):
    length, width = rows.shape
    vmem = pl.BlockSpec(memory_space=pltpu.VMEM)
    return pl.pallas_call(
        functools.partial(leave_kernel, width // 4, width // 2),
        in_specs=[pl.BlockSpec(memory_space=pltpu.SMEM)] + [vmem] * 14,
        out_specs=[vmem] * 3,
        out_shape=[
            jax.ShapeDtypeStruct((length, width), HALF),
            jax.ShapeDtypeStruct((length, width), SINGLE),
            jax.ShapeDtypeStruct((length, width), HALF),
        ],
        compiler_params=pltpu.CompilerParams(vmem_limit_bytes=48 * 1024 * 1024),
        cost_estimate=pl.CostEstimate(flops=6000000000, bytes_accessed=14000000, transcendentals=0),
        name="leave_attention",
    )(places, rows, gain, *groups, *own, *other)


def return_kernel(part, half, *refs):
    place_ref, own_ref, last_ref, upstream_ref, middle_ref, gain_ref = refs[:6]
    own_refs = refs[6:10]
    other_refs = refs[10:14]
    middle_grad_ref, branch_ref, gain_grad_ref, group_ref = refs[14:]
    middle = middle_ref[...]
    inverse = lax.rsqrt(jnp.mean(middle * middle, axis=-1, keepdims=True) + EPS)
    unit = middle * inverse
    grad = own_ref[...] + last_ref[...].astype(SINGLE)
    gain_grad_ref[...] = jnp.sum(grad * unit, axis=0, keepdims=True)
    scaled = grad * gain_ref[...]
    middle_grad_ref[...] = upstream_ref[...].astype(SINGLE) + inverse * (
        scaled - unit * jnp.mean(scaled * unit, axis=-1, keepdims=True)
    )
    own_at = pl.multiple_of(place_ref[4], half)
    other_at = pl.multiple_of(half - place_ref[4], half)
    branch_ref[:, :half] = middle_grad_ref[:, pl.ds(own_at, half)].astype(HALF)
    branch_ref[:, half:] = middle_grad_ref[:, pl.ds(other_at, half)].astype(HALF)
    for r in range(4):
        total = mm_nt(branch_ref[:, :half], own_refs[r][...]) + mm_nt(branch_ref[:, half:], other_refs[r][...])
        group_ref[place_ref[5 + r]] = total.astype(HALF)


def return_to_attention(places, own_sum, last, upstream, middle, gain, own, other):
    length, width = middle.shape
    vmem = pl.BlockSpec(memory_space=pltpu.VMEM)
    return pl.pallas_call(
        functools.partial(return_kernel, width // 4, width // 2),
        in_specs=[pl.BlockSpec(memory_space=pltpu.SMEM)] + [vmem] * 13,
        out_specs=[vmem] * 4,
        out_shape=[
            jax.ShapeDtypeStruct((length, width), SINGLE),
            jax.ShapeDtypeStruct((length, width), HALF),
            jax.ShapeDtypeStruct((1, width), SINGLE),
            jax.ShapeDtypeStruct((4, length, width // 4), HALF),
        ],
        compiler_params=pltpu.CompilerParams(vmem_limit_bytes=48 * 1024 * 1024),
        cost_estimate=pl.CostEstimate(flops=6000000000, bytes_accessed=14000000, transcendentals=0),
        name="return_to_attention",
    )(places, own_sum, last, upstream, middle, gain, *own, *other)


AXES = ("grp", "fsdp")


def tie(*values):
    return lax.optimization_barrier(values)


def cut(array, start, size, axis):
    return lax.dynamic_slice_in_dim(array, start, size, axis)


def wide_sum(*terms):
    total = terms[0].astype(SINGLE)
    for term in terms[1:]:
        total = total + term.astype(SINGLE)
    return total


def turned(doc_row, taps_count):
    length = doc_row.shape[0]
    span = length // 2
    start = jnp.argmax(doc_row[: length - span + 1] == doc_row[span - 1 :])
    position = lax.iota(jnp.int32, length)
    source = (position + start) % length
    turn = (source[:, None] == position[None, :]).astype(HALF)
    segment = jnp.sum(jnp.where(turn > 0, doc_row[None, :], 0), axis=1)
    marks = jnp.stack(
        [((jnp.roll(segment, k) == segment) & (position >= k)).astype(SINGLE) for k in range(taps_count)],
        axis=1,
    )
    return turn, marks, segment[:, None], segment[None, :]


def turn_back(turn, array):
    high = array.astype(HALF)
    low = (array - high.astype(SINGLE)).astype(HALF)
    return mm_tn(turn, high) + mm_tn(turn, low)


def unit_norm(array):
    inverse = lax.rsqrt(jnp.mean(array * array, axis=-1, keepdims=True) + EPS)
    return array * inverse, inverse


def unit_back(grad, unit, inverse, gain):
    scaled = grad * gain
    return inverse * (scaled - unit * jnp.mean(scaled * unit, axis=-1, keepdims=True))


def gates(gate_rows, up_rows):
    gate_sig = jax.nn.sigmoid(gate_rows)
    return gate_sig, (gate_rows * gate_sig * up_rows).astype(HALF)


def gates_back(grad_hidden, gate_rows, up_rows, gate_sig):
    return jnp.concatenate(
        [
            (grad_hidden * up_rows * gate_sig * (1.0 + gate_rows * (1.0 - gate_sig))).astype(HALF),
            (grad_hidden * gate_rows * gate_sig).astype(HALF),
        ],
        axis=1,
    )


def local_any(
    tokens, doc_ids, cotangent, gain_in, w_query, w_key, w_value, w_house, w_rate, conv_taps, w_out,
    gain_mid, w_gate, w_up, w_down,
):
    heads = w_rate.shape[1]
    width = tokens.shape[2]
    dim = width // heads
    span = tokens.shape[1] // 2
    count = heads // 4
    wide = count * dim

    def fetch(array, axis=0):
        return lax.all_gather(array.astype(HALF), "fsdp", axis=axis, tiled=True)

    def share(array, axis=0):
        part = lax.psum_scatter(array.astype(HALF), "fsdp", scatter_dimension=axis, tiled=True)
        return lax.psum(part, "grp").astype(SINGLE)

    gain_first = fetch(gain_in).astype(SINGLE)
    gain_second = fetch(gain_mid).astype(SINGLE)
    projections = [fetch(w) for w in (w_query, w_key, w_value, w_house)]
    mat_rate = fetch(w_rate)
    tap_values = fetch(conv_taps, 1).astype(SINGLE)
    mat_out, mat_gate, mat_up, mat_down = [fetch(w) for w in (w_out, w_gate, w_up, w_down)]
    turn, marks, segc, segr = turned(doc_ids[0], conv_taps.shape[0])
    rows = mm(turn, tokens[0])
    upstream = mm(turn, cotangent[0]).astype(HALF)
    unit_in, inverse_in = unit_norm(rows)
    normed = (unit_in * gain_first).astype(HALF)
    rate_sig = jax.nn.sigmoid(
        lax.dot_general(mat_rate, normed, (((0,), (1,)), ((), ())), preferred_element_type=SINGLE)
    )
    rates = [2.0 * rate_sig[k * count : (k + 1) * count] for k in range(4)]
    taps = [tap_values[:, k * wide : (k + 1) * wide] for k in range(4)]
    pieces = [
        jnp.concatenate([w[:, k * wide : (k + 1) * wide] for w in projections], axis=1) for k in range(4)
    ]
    kept = [
        attn_forward(normed, [pieces[k]], rates[k], taps[k], marks, segc, segr, dim, span) for k in range(4)
    ]
    attended = jnp.concatenate([k[0] for k in kept], axis=1)
    middle = rows + mm(attended, mat_out)
    unit_mid, inverse_mid = unit_norm(middle)
    normed_mid = (unit_mid * gain_second).astype(HALF)
    gate_rows = mm(normed_mid, mat_gate)
    up_rows = mm(normed_mid, mat_up)
    gate_sig, hidden = gates(gate_rows, up_rows)
    result = (middle + mm(hidden, mat_down)).astype(HALF)
    feed_rows = gates_back(mm_nt(upstream, mat_down), gate_rows, up_rows, gate_sig)
    units = feed_rows.shape[1] // 2
    grad_gate_rows, grad_up_rows = feed_rows[:, :units], feed_rows[:, units:]
    grad_normed_mid = mm_nt(grad_gate_rows, mat_gate) + mm_nt(grad_up_rows, mat_up)
    grad_middle = upstream.astype(SINGLE) + unit_back(grad_normed_mid, unit_mid, inverse_mid, gain_second)
    grad_branch = grad_middle.astype(HALF)
    grad_att = mm_nt(grad_branch, mat_out).astype(HALF)
    row_grads, rate_grads, tap_grads = [], [], []
    for k in range(4):
        unused_out, qkv, raw, house, tri, carried, probs = kept[k]
        got = attn_backward(
            qkv, house, raw, rates[k], taps[k], marks, segc, segr, grad_att[None, :, k * wide : (k + 1) * wide], 0,
            tri, carried, probs, dim, span,
        )
        row_grads.append(got[0])
        rate_grads.append(got[1])
        tap_grads.append(got[2])
    grad_rate_rows = (jnp.concatenate(rate_grads, axis=0) * 2.0 * rate_sig * (1.0 - rate_sig)).astype(HALF)
    grad_normed = lax.dot_general(
        grad_rate_rows, mat_rate, (((0,), (1,)), ((), ())), preferred_element_type=SINGLE
    )
    for k in range(4):
        grad_normed = grad_normed + mm_nt(row_grads[k], pieces[k])
    grad_tokens = grad_middle + unit_back(grad_normed, unit_in, inverse_in, gain_first)
    weight_grads = []
    for m in range(4):
        part = jnp.concatenate([r[:, m * wide : (m + 1) * wide] for r in row_grads], axis=1)
        weight_grads.append(share(mm_tn(normed, part)))
    return (
        mm_tn(turn, result).astype(HALF)[None],
        turn_back(turn, grad_tokens)[None],
        share(jnp.sum(grad_normed * unit_in, axis=0)),
        weight_grads[0],
        weight_grads[1],
        weight_grads[2],
        weight_grads[3],
        share(lax.dot_general(normed, grad_rate_rows, (((0,), (1,)), ((), ())), preferred_element_type=SINGLE)),
        share(jnp.concatenate(tap_grads, axis=1), 1),
        share(mm_tn(attended, grad_branch)),
        share(jnp.sum(grad_normed_mid * unit_mid, axis=0)),
        share(mm_tn(normed_mid, grad_gate_rows)),
        share(mm_tn(normed_mid, grad_up_rows)),
        share(mm_tn(hidden, upstream)),
    )


class Links:
    def __init__(self, groups, shards):
        self.core = lax.axis_index("grp") % 2
        self.me = lax.axis_index("fsdp")
        near = 1 + self.core
        self.order = [self.me, self.me ^ near, self.me ^ (3 - near), self.me ^ 3]

        def permutation(move):
            pairs = []
            for g in range(groups):
                for f in range(shards):
                    target = move(g // 2, g % 2, f)
                    if target is not None:
                        pairs.append((g * shards + f, target[0] * shards + target[1]))
            return pairs

        self.pairs = {
            "near": permutation(lambda z, c, f: (2 * z + c, f ^ (1 + c))),
            "next": permutation(lambda z, c, f: (2 * z + c, f ^ (2 - c))),
            "twin": permutation(lambda z, c, f: (2 * z + 1 - c, f)),
            "inward": permutation(lambda z, c, f: (2 * (z ^ 1) + c, f) if z in (0, 3) else None),
            "across": permutation(lambda z, c, f: (2 * (3 - z) + c, f) if z in (1, 2) else None),
            "outward": permutation(lambda z, c, f: (2 * (z ^ 1) + c, f) if z in (1, 2) else None),
        }
        level = lax.axis_index("grp") // 2
        self.edge = (level == 0) | (level == 3)

    def near(self, array):
        return lax.ppermute(array, AXES, self.pairs["near"])

    def next(self, array):
        return lax.ppermute(array, AXES, self.pairs["next"])

    def twin(self, array):
        return lax.ppermute(array, AXES, self.pairs["twin"])

    def inward(self, array):
        return lax.ppermute(array, AXES, self.pairs["inward"])

    def across(self, array):
        return lax.ppermute(array, AXES, self.pairs["across"])

    def outward(self, array):
        return lax.ppermute(array, AXES, self.pairs["outward"])

    def settled(self, total, got):
        return jnp.where(self.edge, got, total)

    def place(self, number):
        apart = number ^ self.me
        return jnp.where((apart == 0) | (apart == 3) | (self.core == 0), apart, 3 - apart)

    def in_place(self, blocks):
        rows = blocks[0].shape[0]
        every = jnp.zeros((rows * 4,) + blocks[0].shape[1:], blocks[0].dtype)
        for number, block in zip(self.order, blocks):
            every = lax.dynamic_update_slice(every, block, (number * rows,) + (0,) * (block.ndim - 1))
        return every

    def by_core(self, own, other, axis):
        return jnp.where(
            self.core == 0,
            jnp.concatenate([own, other], axis=axis),
            jnp.concatenate([other, own], axis=axis),
        )


def core_sum(own, got):
    rows = own.shape[0] // 4
    flip = [got[i * rows : (i + 1) * rows] for i in (0, 2, 1, 3)]
    head = wide_sum(own[: 2 * rows], jnp.concatenate(flip[:2], axis=0)).astype(HALF)
    tail = wide_sum(own[2 * rows :], jnp.concatenate(flip[2:], axis=0)).astype(HALF)
    return head, tail


def second_sum(head, got):
    rows = head.shape[0] // 2
    return wide_sum(head[:rows], got[:rows]), wide_sum(head[rows:], got[rows:]).astype(HALF)


def local_paired(
    tokens, doc_ids, cotangent, gain_in, w_query, w_key, w_value, w_house, w_rate, conv_taps, w_out,
    gain_mid, w_gate, w_up, w_down, *, groups, shards,
):
    links = Links(groups, shards)
    core = links.core
    length = tokens.shape[1]
    width = tokens.shape[2]
    span = length // 2
    heads = w_rate.shape[1]
    dim = width // heads
    taps_count = conv_taps.shape[0]
    part = width // shards
    half_width = width // 2
    count = heads // 4
    wide = count * dim
    own_at = core * half_width
    other_at = half_width - own_at
    number = [2 * core, 2 * core + 1, 2 - 2 * core, 3 - 2 * core]
    hidden_part = w_gate.shape[1] // shards
    h = hidden_part // 2
    hid_own = core * h
    hid_other = h - hid_own

    def group_columns(k):
        return jnp.concatenate(
            [cut(matrix, k * wide, wide, 1).astype(HALF) for matrix in (w_query, w_key, w_value, w_house)],
            axis=1,
        )

    def feed_block(i):
        start = i * hidden_part + hid_own
        return jnp.concatenate([cut(w_gate, start, h, 1), cut(w_up, start, h, 1)], axis=1).astype(HALF)

    def in_order(array, axis):
        return jnp.concatenate([cut(array, i * part, part, axis) for i in links.order], axis=axis)

    def from_order(array, axis):
        return jnp.concatenate([cut(array, links.place(i) * part, part, axis) for i in range(4)], axis=axis)

    small = jnp.concatenate([gain_in[:, None], gain_mid[:, None], conv_taps.T, w_rate], axis=1).astype(HALF)
    small = jnp.pad(small, ((0, 0), (0, 128 - small.shape[1])))
    small_near, small_second = links.near(small), links.next(small)
    block0 = group_columns(number[0])
    near0, second0 = links.near(block0), links.next(block0)

    turn, marks, segc, segr = turned(doc_ids[0], taps_count)
    rows = mm(turn, tokens[0])
    unit_in, inverse_in = unit_norm(rows)
    unit_in = in_order(unit_in, 1)
    block1 = group_columns(number[1])

    near0, second0, small_near, small_second, block1, unit_in = tie(
        near0, second0, small_near, small_second, block1, unit_in
    )
    small_far = links.next(small_near)
    far0 = links.next(near0)
    twin0 = [links.twin(second0), links.twin(near0)]
    block2 = group_columns(number[2])
    small = [small, small_near, small_second, small_far]
    small_order = jnp.concatenate(small, axis=0)
    small_plain = links.in_place(small)
    gain_first = small_order[:, 0].astype(SINGLE)
    gain_second = small_plain[:, 1].astype(SINGLE)
    tap_values = small_plain[:, 2 : 2 + taps_count].astype(SINGLE)
    mat_rate = small_order[:, 2 + taps_count : 2 + taps_count + heads]
    normed = (unit_in * gain_first).astype(HALF)
    rate_sig = jax.nn.sigmoid(
        lax.dot_general(mat_rate, normed, (((0,), (1,)), ((), ())), preferred_element_type=SINGLE)
    )
    rates = [cut(2.0 * rate_sig, k * count, count, 0) for k in number]
    taps = [cut(tap_values, k * wide, wide, 0).T for k in number]
    normed, far0, block1, block2, *rest = tie(normed, far0, block1, block2, *rates, *taps)
    rates, taps = rest[:4], rest[4:]

    def forward(i, normed, pieces):
        return attn_forward(normed, pieces, rates[i], taps[i], marks, segc, segr, dim, span)

    kept = [None] * 4
    pieces = [None] * 4
    pieces[0] = [block0, near0, second0, far0]
    twin0.append(links.twin(far0))
    near1, second1 = links.near(block1), links.next(block1)
    kept[0] = forward(0, normed, pieces[0])

    normed, unused, *twin0 = tie(normed, kept[0][0], *twin0)
    pieces[2] = [block2] + twin0
    kept[2] = forward(2, normed, pieces[2])

    out_block = cut(w_out, own_at, half_width, 1).astype(HALF)
    near1, second1, normed, unused, out_block = tie(near1, second1, normed, kept[2][0], out_block)
    far1 = links.next(near1)
    out_near, out_second = links.near(out_block), links.next(out_block)
    twin1 = [links.twin(second1), links.twin(near1)]
    upstream = mm(turn, cotangent[0]).astype(HALF)
    block3 = group_columns(number[3])
    out_rest = cut(w_out, other_at, half_width, 1).astype(HALF)
    feed_first, feed_second, feed_far = [feed_block(i) for i in links.order[1:]]

    far1, normed, block3, feed_first, feed_second, feed_far, upstream, out_rest = tie(
        far1, normed, block3, feed_first, feed_second, feed_far, upstream, out_rest
    )
    twin1.append(links.twin(far1))
    pieces[1] = [block1, near1, second1, far1]
    feed_passing = links.near(feed_far)
    feed_next = links.next(feed_second)
    kept[1] = forward(1, normed, pieces[1])

    normed, unused, out_near, out_second, *twin1 = tie(normed, kept[1][0], out_near, out_second, *twin1)
    pieces[3] = [block3] + twin1
    out_far = links.next(out_near)
    feed_near = links.near(feed_first)
    out_twin = [links.twin(out_second), links.twin(out_near)]
    kept[3] = forward(3, normed, pieces[3])

    att3, out_far, feed_passing, *out_twin = tie(kept[3][0], out_far, feed_passing, *out_twin)
    feed_last = links.next(feed_passing)
    out_twin.append(links.twin(out_far))
    places = [links.place(k) for k in number] + [own_at] + [k ^ (2 * core) for k in links.order]
    places = jnp.stack([jnp.asarray(p, jnp.int32) for p in places])
    gain_second = gain_second[None, :]
    out_own = [out_block, out_near, out_second, out_far]
    out_other = [out_rest] + out_twin
    attended, middle, normed_mid = leave_attention(
        places, rows, gain_second, [kept[0][0], kept[1][0], kept[2][0], att3], out_own, out_other
    )

    mid_near, mid_second = links.near(normed_mid), links.next(normed_mid)
    feed_own = links.in_place([feed_block(links.me), feed_near, feed_next, feed_last])
    mat_down = jnp.concatenate(
        [cut(w_down, hid_own, h, 0), cut(w_down, hid_other, h, 0)], axis=0
    ).astype(HALF)
    mid_near, mid_second, feed_own, mat_down = tie(mid_near, mid_second, feed_own, mat_down)
    feed_other = links.twin(feed_own)
    mid_far = links.next(mid_near)
    up_near, up_second = links.near(upstream), links.next(upstream)
    mat_feed = jnp.concatenate(
        [feed_own[:, :h], feed_other[:, :h], feed_own[:, h:], feed_other[:, h:]], axis=1
    )
    mat_feed, mid_far = tie(mat_feed, mid_far)
    normed_all = jnp.concatenate([normed_mid, mid_near, mid_second, mid_far], axis=0)
    gate_up = mm(normed_all, mat_feed)
    up_near, up_second, gate_up = tie(up_near, up_second, gate_up)
    up_far = links.next(up_near)
    gate_rows, up_rows = gate_up[:, :hidden_part], gate_up[:, hidden_part:]
    gate_sig, hidden = gates(gate_rows, up_rows)
    down_tail = mm(hidden[2 * length :], mat_down).astype(HALF)
    up_far, down_tail, hidden = tie(up_far, down_tail, hidden)
    down_part = links.next(down_tail)
    upstream_all = jnp.concatenate([upstream, up_near, up_second, up_far], axis=0)
    grad_hidden = mm_nt(upstream_all, mat_down)
    feed_rows = gates_back(grad_hidden, gate_rows, up_rows, gate_sig)
    mid_tail = mm_nt(feed_rows[2 * length :], mat_feed).astype(HALF)

    mid_tail, feed_rows, hidden = tie(mid_tail, feed_rows, hidden)
    mid_got = links.next(mid_tail)
    grad_down = mm_tn(hidden, upstream_all).astype(HALF)
    down_head = mm(hidden[: 2 * length], mat_down)
    grad_down, feed_rows = tie(grad_down, feed_rows)
    down_got = links.twin(grad_down[h:])
    mid_head = mm_nt(feed_rows[: 2 * length], mat_feed)
    mid_got, mid_head, down_got, down_part, down_head = tie(mid_got, mid_head, down_got, down_part, down_head)
    mid_own, mid_first = second_sum(mid_head, mid_got)
    mid_last = links.near(mid_first)
    down_own, down_first = second_sum(down_head, down_part)
    down_sum = wide_sum(grad_down[:h], down_got).astype(HALF)
    down_in = links.inward(down_sum)
    grad_feed = mm_tn(normed_all, feed_rows).astype(HALF)

    mid_last, grad_feed, down_first, mid_own = tie(mid_last, grad_feed, down_first, mid_own)
    feed_got = links.twin(jnp.concatenate([grad_feed[:, h : 2 * h], grad_feed[:, 3 * h :]], axis=1))
    down_last = links.near(down_first)
    grad_middle, branch_pair, grad_gain_mid, grad_att = return_to_attention(
        places, mid_own, mid_last, upstream, middle, gain_second, out_own, out_other
    )
    out_grads = mm_tn(attended, branch_pair).astype(HALF)

    def backward(i, grad_att):
        unused_out, qkv, raw, house, tri, carried, probs = kept[i]
        return attn_backward(
            qkv, house, raw, rates[i], taps[i], marks, segc, segr, grad_att, i, tri, carried, probs, dim, span
        )

    row_grads = [None] * 4
    rate_grads = [None] * 4
    tap_grads = [None] * 4
    out_grads, feed_got, grad_att = tie(out_grads, feed_got, grad_att)
    out_got = links.twin(out_grads[:, half_width:])
    feed_sum = wide_sum(
        jnp.concatenate([grad_feed[:, :h], grad_feed[:, 2 * h : 3 * h]], axis=1), feed_got
    ).astype(HALF)
    feed0, feed1 = feed_sum[: width // 2], feed_sum[width // 2 :]
    row_grads[2], rate_grads[2], tap_grads[2] = backward(2, grad_att)
    other = mm_tn(normed, row_grads[2]).astype(HALF)

    other, out_got, grad_att, down_in, feed0, feed1 = tie(other, out_got, grad_att, down_in, feed0, feed1)
    got0 = links.twin(other)
    feed0_in = links.inward(feed0)
    down_sum = wide_sum(down_sum, down_in).astype(HALF)
    down_across = links.across(down_sum)
    out_head, out_tail = core_sum(out_grads[:, :half_width], out_got)
    out_part = links.next(out_tail)
    row_grads[0], rate_grads[0], tap_grads[0] = backward(0, grad_att)
    own0 = mm_tn(normed, row_grads[0]).astype(HALF)

    own0, got0, out_part, grad_att, down_last = tie(own0, got0, out_part, grad_att, down_last)
    head0, tail0 = core_sum(own0, got0)
    part0 = links.next(tail0)
    out_own_sum, out_first = second_sum(out_head, out_part)
    out_last = links.near(out_first)
    row_grads[3], rate_grads[3], tap_grads[3] = backward(3, grad_att)
    other = mm_tn(normed, row_grads[3]).astype(HALF)

    other, out_last, grad_att, feed0_in, down_across = tie(other, out_last, grad_att, feed0_in, down_across)
    got1 = links.twin(other)
    feed1_in = links.inward(feed1)
    feed0 = wide_sum(feed0, feed0_in).astype(HALF)
    feed0_across = links.across(feed0)
    down_sum = wide_sum(down_sum, down_across).astype(HALF)
    down_out = links.outward(down_sum)
    out_sum = wide_sum(out_own_sum, out_last).astype(HALF)
    result = (middle + wide_sum(down_own, down_last)).astype(HALF)
    result = mm_tn(turn, result).astype(HALF)
    row_grads[1], rate_grads[1], tap_grads[1] = backward(1, grad_att)
    own1 = mm_tn(normed, row_grads[1]).astype(HALF)

    own1, got1, part0, out_sum = tie(own1, got1, part0, out_sum)
    sum0, first0 = second_sum(head0, part0)
    last0 = links.near(first0)
    head1, tail1 = core_sum(own1, got1)
    part1 = links.next(tail1)

    grad_rate = links.by_core(
        jnp.concatenate(rate_grads[:2], axis=0), jnp.concatenate(rate_grads[2:], axis=0), 0
    )
    grad_taps = links.by_core(
        jnp.concatenate(tap_grads[:2], axis=1), jnp.concatenate(tap_grads[2:], axis=1), 1
    )
    grad_rate_rows = (grad_rate * 2.0 * rate_sig * (1.0 - rate_sig)).astype(HALF)
    grad_wrate = lax.dot_general(
        normed, grad_rate_rows, (((0,), (1,)), ((), ())), preferred_element_type=SINGLE
    )
    grad_normed = lax.dot_general(
        grad_rate_rows, mat_rate, (((0,), (1,)), ((), ())), preferred_element_type=SINGLE
    )
    for i in (0, 2):
        grad_normed = grad_normed + mm_nt(row_grads[i], jnp.concatenate(pieces[i], axis=0))

    feed1_in, feed0_across, last0, grad_normed, down_out = tie(feed1_in, feed0_across, last0, grad_normed, down_out)
    feed1 = wide_sum(feed1, feed1_in).astype(HALF)
    feed1_across = links.across(feed1)
    feed0 = wide_sum(feed0, feed0_across).astype(HALF)
    feed0_out = links.outward(feed0)
    out_in = links.inward(out_sum)
    sum0 = wide_sum(sum0, last0).astype(HALF)
    sum0_in = links.inward(sum0)
    down_sum = links.settled(down_sum, down_out)
    down_twin = links.twin(down_sum)
    for i in (1, 3):
        grad_normed = grad_normed + mm_nt(row_grads[i], jnp.concatenate(pieces[i], axis=0))
    grad_gain_in = jnp.sum(grad_normed * unit_in, axis=0)
    extra = jnp.concatenate(
        [grad_gain_in[:, None], in_order(grad_gain_mid[0], 0)[:, None], in_order(grad_taps.T, 0), grad_wrate],
        axis=1,
    )
    extra = jnp.pad(extra, ((0, 0), (0, 128 - extra.shape[1]))).astype(HALF)

    extra, part1, out_in, grad_normed = tie(extra, part1, out_in, grad_normed)
    extra_got = links.twin(extra)
    sum1, first1 = second_sum(head1, part1)
    last1 = links.near(first1)
    out_sum = wide_sum(out_sum, out_in).astype(HALF)
    out_across = links.across(out_sum)
    norm_grad = unit_back(grad_normed, unit_in, inverse_in, gain_first)
    grad_tokens = turn_back(turn, grad_middle + from_order(norm_grad, 1))

    grad_tokens, feed1_across, sum0_in, extra_got, last1, feed0_out = tie(
        grad_tokens, feed1_across, sum0_in, extra_got, last1, feed0_out
    )
    feed1 = wide_sum(feed1, feed1_across).astype(HALF)
    feed1_out = links.outward(feed1)
    sum0 = wide_sum(sum0, sum0_in).astype(HALF)
    sum0_across = links.across(sum0)
    sum1 = wide_sum(sum1, last1).astype(HALF)
    sum1 = [sum1[: part // 2], sum1[part // 2 :]]
    sum1_in = [links.inward(a) for a in sum1]
    extra_head, extra_tail = core_sum(extra, extra_got)
    extra_part = links.next(extra_tail)
    grad_down = links.by_core(down_sum, down_twin, 0).astype(SINGLE)
    feed0 = links.settled(feed0, feed0_out)

    feed1_out, sum0_across, out_across, extra_part, grad_down, feed0, *sum1_in = tie(
        feed1_out, sum0_across, out_across, extra_part, grad_down, feed0, *sum1_in
    )
    sum0 = wide_sum(sum0, sum0_across).astype(HALF)
    sum0_out = links.outward(sum0)
    sum1 = [wide_sum(a, b).astype(HALF) for a, b in zip(sum1, sum1_in)]
    sum1_across = [links.across(a) for a in sum1]
    out_sum = wide_sum(out_sum, out_across).astype(HALF)
    out_out = links.outward(out_sum)
    feed_sum = jnp.concatenate([feed0, links.settled(feed1, feed1_out)], axis=0)
    feed_blocks = [cut(feed_sum, i * part, part, 0) for i in links.order]
    feed_passing, feed_near = links.near(feed_blocks[3]), links.near(feed_blocks[1])
    feed_next = links.next(feed_blocks[2])
    extra_own, extra_first = second_sum(extra_head, extra_part)
    extra_sum = wide_sum(extra_own, links.near(extra_first)).astype(HALF)
    extra_in = links.inward(extra_sum)

    feed_passing, out_out, sum0_out, extra_in, *sum1_across = tie(
        feed_passing, out_out, sum0_out, extra_in, *sum1_across
    )
    feed_last = links.next(feed_passing)
    sum1 = [wide_sum(a, b).astype(HALF) for a, b in zip(sum1, sum1_across)]
    sum1_out = [links.outward(a) for a in sum1]
    out_sum = links.settled(out_sum, out_out)
    out_twin = links.twin(out_sum)
    sum0 = links.settled(sum0, sum0_out)
    twin0 = links.twin(sum0)
    extra_sum = wide_sum(extra_sum, extra_in).astype(HALF)
    extra_across = links.across(extra_sum)
    grad_wout = links.by_core(out_sum, out_twin, 1).astype(SINGLE)

    feed_last, extra_across, *sum1_out = tie(feed_last, extra_across, *sum1_out)
    feed_mine = links.in_place([feed_blocks[0], feed_near, feed_next, feed_last])
    feed_twin = links.twin(feed_mine)
    sum1 = jnp.concatenate([links.settled(a, b) for a, b in zip(sum1, sum1_out)], axis=0)
    twin1 = links.twin(sum1)
    extra_sum = wide_sum(extra_sum, extra_across).astype(HALF)
    extra = links.settled(extra_sum, links.outward(extra_sum)).astype(SINGLE)

    grad_gate, grad_up = [
        jnp.concatenate(
            [
                links.by_core(
                    feed_mine[i * part : (i + 1) * part, at : at + h],
                    feed_twin[i * part : (i + 1) * part, at : at + h],
                    1,
                )
                for i in range(shards)
            ],
            axis=1,
        ).astype(SINGLE)
        for at in (0, h)
    ]
    sums = [(sum0, twin0), (sum1, twin1)]
    weight_grads = []
    for m in range(4):
        columns = [[a[:, m * wide : (m + 1) * wide] for a in pair] for pair in sums]
        weight_grads.append(
            links.by_core(
                jnp.concatenate([columns[0][0], columns[1][0]], axis=1),
                jnp.concatenate([columns[0][1], columns[1][1]], axis=1),
                1,
            ).astype(SINGLE)
        )

    return (
        result[None],
        grad_tokens[None],
        extra[:, 0],
        weight_grads[0],
        weight_grads[1],
        weight_grads[2],
        weight_grads[3],
        extra[:, 2 + taps_count : 2 + taps_count + heads],
        extra[:, 2 : 2 + taps_count].T,
        grad_wout,
        extra[:, 1],
        grad_gate,
        grad_up,
        grad_down,
    )


def solution(mesh):
    groups, shards = mesh.shape["grp"], mesh.shape["fsdp"]
    if (groups, shards) == (8, 4):
        body = functools.partial(local_paired, groups=groups, shards=shards)
    else:
        body = local_any
    rows = P(("grp", "fsdp"), None, None)
    vector = P("fsdp")
    matrix = P("fsdp", None)
    taps = P(None, "fsdp")
    return jax.shard_map(
        body,
        mesh=mesh,
        in_specs=(
            rows, P(("grp", "fsdp"), None), rows, vector, matrix, matrix, matrix, matrix, matrix,
            taps, matrix, vector, matrix, matrix, matrix,
        ),
        out_specs=(
            rows, rows, vector, matrix, matrix, matrix, matrix, matrix, taps, matrix, vector,
            matrix, matrix, matrix,
        ),
        check_vma=False,
    )
```

time: 1840 us -> 743 us (0.40)
  waiting for transfers between devices: 1400 us -> 221 us
  starting transfers between devices: 0.79 us -> 102 us
  local copies, waits for them, and re-layouts: 18.5 us -> 90.9 us
  blocking collectives: 71.8 us -> 0 us
  matrix products: 198 us -> 127 us
  Pallas kernels: 68.7 us -> 101 us
  other arithmetic: 58.4 us -> 85.1 us
    reduce_scatter x8 -> x0, waiting for transfers between devices: 606 us -> none  [the longest x1 124 us: local(): lax.psum_scatter(grad_gate.astype(jnp.bfloat16), 'fsdp', scatter_dimensio...]
    all_gather x8 -> x0, waiting for transfers between devices: 510 us -> none  [the longest x1 118 us: fetch_feed(): lax.all_gather(w_gate.astype(half), 'fsdp', axis=0, tiled=True)]
    psum x1 -> x0, waiting for transfers between devices: 280 us -> none  [local(): lax.psum(attn_grads[1].astype(jnp.bfloat16), 'grp').astype(jnp.float32)]
    ppermute x0 -> x83, waiting for transfers between devices: none -> 221 us  [the longest x22 110 us: next(): return lax.ppermute(array, AXES, self.pairs['next'])]
    ppermute x0 -> x83, starting transfers between devices: none -> 102 us  [the longest x8 36.6 us: inward(): return lax.ppermute(array, AXES, self.pairs['inward'])]
    dot_general x31 -> x25, matrix products: 198 us -> 127 us  [the longest x7 54.1 us: mm_nt(): lax.dot_general(left, right, (((1,), (1,)), ((), ())), preferred_element_...]
    unnamed x111 -> x360, local copies, waits for them, and re-layouts: 12.2 us -> 51.8 us
    all_gather x4 -> x0, blocking collectives: 33.5 us -> none  [the longest x1 9.44 us: fetch_attention(): lax.all_gather(gain_in.astype(half), 'fsdp', axis=0, tiled=True)]
  transfers between devices with their start and end apart: 19 -> 83, of which waited for: 16 -> 29; matrix products, arithmetic and copies ran while one was open for 10% -> 28% of each run, Pallas kernels for 2% -> 14%
where the time goes in v2:
time: 743 us; the launch traced here: 731 us
  waiting for transfers between devices  221 us (30%)
  matrix products  127 us (17%)
  starting transfers between devices  102 us (14%)
  Pallas kernels  101 us (14%)
  local copies, waits for them, and re-layouts  90.9 us (12%)
  other arithmetic  85.1 us (11%)
    ppermute x22, waiting for transfers between devices, next(): return lax.ppermute(array, AXES, self.pairs['next'])  110 us
    dot_general x7, matrix products, mm_nt(): lax.dot_general(left, right, (((1,), (1,)), ((), ())), preferred_element_...  54.1 us
    pallas_call x4, Pallas kernels, attn_forward(): pl.pallas_call(functools.partial(attn_forward_kernel, span, dim, count, t...  52 us
    unnamed x360, local copies, waits for them, and re-layouts  51.8 us
    ppermute x8, waiting for transfers between devices, outward(): return lax.ppermute(array, AXES, self.pairs['outward'])  51.1 us
    dot_general x10, matrix products, mm_tn(): lax.dot_general(left, right, (((0,), (0,)), ((), ())), preferred_element_...  48.3 us
    ppermute x16, waiting for transfers between devices, near(): return lax.ppermute(array, AXES, self.pairs['near'])  46.6 us
    ppermute x8, starting transfers between devices, inward(): return lax.ppermute(array, AXES, self.pairs['inward'])  36.6 us
  transfers between devices with their start and end apart: 83, of which 29 were waited for; matrix products, arithmetic and copies ran while one was open for 28% of the time, Pallas kernels for 14%

profile of v2, /device:TPU:0, one launch (start us, length us, event | category | flops | bytes accessed | tf_op | source)
XLA Modules:
  0.0 731.3 jit_solution(17342926643848304643)
XLA Ops:
  25.4 14.4 %collective-permute-done.2 = bf16[384,128]{0,1:T(8,128)(2,1)} collective-permute-done((bf16[384,128]{0,1:T(8,128)(2,1)}, bf16[384,128]{0,1:T(8,128)(2,1)}, u32[]{:S(2)}, u32[]{:S(2)}) %collective-permute-start.2) | collective-permute-done | bytes 98336 | tf_op jit(solution)/shard_map/ppermute | solution.py:503
  46.5 10.9 %collective-permute-done.4 = bf16[384,128]{0,1:T(8,128)(2,1)S(1)} collective-permute-done((bf16[384,128]{0,1:T(8,128)(2,1)}, bf16[384,128]{0,1:T(8,128)(2,1)S(1)}, u32[]{:S(2)}, u32[]{:S(2)}) %collective-permute-start.4) | collective-permute-done | bytes 98336 | tf_op jit(solution)/shard_map/ppermute | solution.py:506
  65.1 13.1 %attend.4 = (bf16[384,384]{1,0:T(8,128)(2,1)S(1)}, bf16[384,1152]{1,0:T(8,128)(2,1)S(1)}, f32[384,384]{1,0:T(8,128)S(1)}, bf16[384,384]{1,0:T(8,128)(2,1)S(1)}, ...) custom-call(bf16[384,1536]{1,0:T(8,128)(2,1)S(1)} %multiply_convert_fusion.3.ref, ...), custom_call_target="tpu_custom_call" | custom-call | flops 16000000000 | bytes 12000000 | tf_op jit(solution)/shard_map/attend/pallas_call | solution.py:196
  85.8 12.8 %attend.5 = (bf16[384,384]{1,0:T(8,128)(2,1)S(1)}, bf16[384,1152]{1,0:T(8,128)(2,1)S(1)}, f32[384,384]{1,0:T(8,128)S(1)}, bf16[384,384]{1,0:T(8,128)(2,1)S(1)}, ...) custom-call(bf16[384,1536]{1,0:T(8,128)(2,1)S(1)} %multiply_convert_fusion.3.ref, ...), custom_call_target="tpu_custom_call" | custom-call | flops 16000000000 | bytes 12000000 | tf_op jit(solution)/shard_map/attend/pallas_call | solution.py:196
  115.0 13.0 %attend.6 = (bf16[384,384]{1,0:T(8,128)(2,1)S(1)}, bf16[384,1152]{1,0:T(8,128)(2,1)S(1)}, f32[384,384]{1,0:T(8,128)S(1)}, bf16[384,384]{1,0:T(8,128)(2,1)S(1)}, ...) custom-call(bf16[384,1536]{1,0:T(8,128)(2,1)S(1)} %multiply_convert_fusion.3.ref, ...), custom_call_target="tpu_custom_call" | custom-call | flops 16000000000 | bytes 12000000 | tf_op jit(solution)/shard_map/attend/pallas_call | solution.py:196
  135.7 13.0 %attend.7 = (bf16[384,384]{1,0:T(8,128)(2,1)S(1)}, bf16[384,1152]{1,0:T(8,128)(2,1)S(1)}, f32[384,384]{1,0:T(8,128)S(1)}, bf16[384,384]{1,0:T(8,128)(2,1)S(1)}, ...) custom-call(bf16[384,1536]{1,0:T(8,128)(2,1)S(1)} %multiply_convert_fusion.3.ref, ...), custom_call_target="tpu_custom_call" | custom-call | flops 16000000000 | bytes 12000000 | tf_op jit(solution)/shard_map/attend/pallas_call | solution.py:196
  166.5 6.8 leave_attention.1
  180.2 15.8 %collective-permute-done.28 = bf16[384,1024]{1,0:T(8,128)(2,1)S(1)} collective-permute-done((bf16[384,1024]{1,0:T(8,128)(2,1)}, bf16[384,1024]{1,0:T(8,128)(2,1)S(1)}, u32[]{:S(2)}, u32[]{:S(2)}) %collective-permute-start.28) | collective-permute-done | bytes 786464 | tf_op jit(solution)/shard_map/ppermute | solution.py:506
  196.1 7.5 %collective-permute-done.24 = bf16[384,1536]{1,0:T(8,128)(2,1)S(1)} collective-permute-done((bf16[384,1536]{1,0:T(8,128)(2,1)}, bf16[384,1536]{1,0:T(8,128)(2,1)S(1)}, u32[]{:S(2)}, u32[]{:S(2)}) %collective-permute-start.24) | collective-permute-done | bytes 1179680 | tf_op jit(solution)/shard_map/ppermute | solution.py:503
  203.5 7.5 %collective-permute-done.25 = bf16[384,1536]{1,0:T(8,128)(2,1)S(1)} collective-permute-done((bf16[384,1536]{1,0:T(8,128)(2,1)}, bf16[384,1536]{1,0:T(8,128)(2,1)S(1)}, u32[]{:S(2)}, u32[]{:S(2)}) %collective-permute-start.25) | collective-permute-done | bytes 1179680 | tf_op jit(solution)/shard_map/ppermute | solution.py:506
  220.3 31.8 %collective-permute-done.30 = bf16[384,1536]{1,0:T(8,128)(2,1)S(1)} collective-permute-done((bf16[384,1536]{1,0:T(8,128)(2,1)S(1)}, bf16[384,1536]{1,0:T(8,128)(2,1)S(1)}, u32[]{:S(2)}, u32[]{:S(2)}) %collective-permute-start.30) | collective-permute-done | bytes 1179680 | tf_op jit(solution)/shard_map/ppermute | solution.py:506
  253.2 12.3 %fusion.150 = f32[1536,2048]{1,0:T(8,128)S(1)} fusion(bf16[1536,1536]{1,0:T(8,128)(2,1)} %constant_dynamic-update-slice_fusion, bf16[1536,2048]{1,0:T(8,128)(2,1)S(1)} %pad_maximum_fusion.1), kind=kOutput, calls=%fused_computation.369 | convolution fusion | flops 9663676416 | bytes 23592960 | tf_op jit(solution)/shard_map/dot_general | solution.py:15
  283.1 12.3 %multiply_convert_fusion = (bf16[1536,1024]{1,0:T(8,128)(2,1)}, bf16[1536,1024]{1,0:T(8,128)(2,1)}) fusion(f32[1536,2048]{1,0:T(8,128)S(1)} %fusion.150, bf16[1536,1536]{1,0:T(8,128)(2,1)} %constant_dynamic-update-slice_fusion.4, bf16[1024,1536]{1,0:T(8,128)(2,1)} %copy-done.97), kind=kOutput, calls=%fused_computation.11 | convolution fusion | flops 4852285440 | bytes 26738688 | tf_op jit(solution)/shard_map/dot_general | solution.py:19
  295.3 8.4 %convolution_convert_fusion.8 = bf16[768,1536]{1,0:T(8,128)(2,1)} fusion(bf16[1536,2048]{1,0:T(8,128)(2,1)S(1)} %pad_maximum_fusion.1, bf16[1536,1024]{1,0:T(8,128)(2,1)} %get-tuple-element.371, bf16[1536,1024]{1,0:T(8,128)(2,1)} %get-tuple-element.370), kind=kOutput, calls=%fused_computation.67 | convolution fusion | flops 4839309312 | bytes 14942208 | tf_op jit(solution)/shard_map/dot_general | solution.py:19
  303.7 6.5 pad_maximum_fusion
  312.3 8.4 %convolution_convert_fusion.6 = bf16[1024,1536]{1,0:T(8,128)(2,1)S(1)} fusion(bf16[1536,1024]{1,0:T(8,128)(2,1)} %copy-done.101, bf16[1536,1536]{1,0:T(8,128)(2,1)} %constant_dynamic-update-slice_fusion.4), kind=kOutput, calls=%fused_computation.65 | convolution fusion | flops 4833411072 | bytes 11010048 | tf_op jit(solution)/shard_map/dot_general | solution.py:23
  325.8 5.1 fusion.41
  330.9 8.5 %collective-permute-done.32 = bf16[768,1536]{1,0:T(8,128)(2,1)} collective-permute-done((bf16[768,1536]{1,0:T(8,128)(2,1)}, bf16[768,1536]{1,0:T(8,128)(2,1)}, u32[]{:S(2)}, u32[]{:S(2)}) %collective-permute-start.32) | collective-permute-done | bytes 2359328 | tf_op jit(solution)/shard_map/ppermute | solution.py:506
  339.4 25.2 %collective-permute-done.34 = bf16[768,1536]{1,0:T(8,128)(2,1)S(1)} collective-permute-done((bf16[768,1536]{1,0:T(8,128)(2,1)}, bf16[768,1536]{1,0:T(8,128)(2,1)S(1)}, u32[]{:S(2)}, u32[]{:S(2)}) %collective-permute-start.34) | collective-permute-done | bytes 2359328 | tf_op jit(solution)/shard_map/ppermute | solution.py:506
  364.6 4.7 convert_add_fusion
  370.6 12.4 %convolution_convert_fusion.5 = bf16[1536,2048]{1,0:T(8,128)(2,1)S(1)} fusion(bf16[1536,1536]{1,0:T(8,128)(2,1)} %constant_dynamic-update-slice_fusion, bf16[1536,2048]{1,0:T(8,128)(2,1)S(1)} %bitcast.87), kind=kOutput, calls=%fused_computation.5 | convolution fusion | flops 9666822144 | bytes 17301504 | tf_op jit(solution)/shard_map/dot_general | solution.py:23
  393.9 8.6 %return_to_attention.1 = (f32[384,1536]{1,0:T(8,128)}, bf16[384,1536]{1,0:T(8,128)(2,1)S(1)}, f32[1,1536]{1,0:T(1,128)S(1)}, bf16[4,384,384]{2,1,0:T(8,128)(2,1)}) custom-call(s32[9]{0:T(128)S(1)} %stack.46.refs_0_, f32[384,1536]{1,0:T(8,128)} %get-tuple-element.269.refs_1_, bf16[384,1536]{1,0:T(8,128)(2,1)} %copy-done.169, ...), custom_call_target="tpu_custom_call" | custom-call | flops 6000000000 | bytes 14000000 | tf_op jit(solution)/shard_map/return_to_attention/pallas_call | solution.py:301
  402.5 4.5 convolution_convert_fusion.4
  415.4 8.5 %attend_back.4 = (bf16[384,1536]{1,0:T(8,128)(2,1)S(1)}, f32[3,384]{1,0:T(4,128)S(1)}, f32[4,384]{1,0:T(4,128)S(1)}) custom-call(bf16[384,1152]{1,0:T(8,128)(2,1)S(1)} %copy-done.43, bf16[384,384]{1,0:T(8,128)(2,1)S(1)} %copy-done.83, f32[384,384]{1,0:T(8,128)S(1)} %copy-done.69, f32[3,384]{1,0:T(4,128)S(1)} %copy-done.19, f32[4,384]{1,0:T(4,128)S(1)} %copy-done.17, ...), custom_call_target="tpu_custom_call" | custom-call | flops 12000000000 | bytes 8000000 | tf_op jit(solution)/shard_map/attend_back/pallas_call | solution.py:217
  423.9 4.3 convolution_convert_fusion.3
  430.7 5.4 fusion.14
  446.4 8.4 %attend_back.5 = (bf16[384,1536]{1,0:T(8,128)(2,1)S(1)}, f32[3,384]{1,0:T(4,128)S(1)}, f32[4,384]{1,0:T(4,128)S(1)}) custom-call(bf16[384,1152]{1,0:T(8,128)(2,1)S(1)} %copy-done.39, bf16[384,384]{1,0:T(8,128)(2,1)S(1)} %copy-done.79, f32[384,384]{1,0:T(8,128)S(1)} %copy-done.53, f32[3,384]{1,0:T(4,128)S(1)} %copy-done.15, f32[4,384]{1,0:T(4,128)S(1)} %copy-done.13, ...), custom_call_target="tpu_custom_call" | custom-call | flops 12000000000 | bytes 8000000 | tf_op jit(solution)/shard_map/attend_back/pallas_call | solution.py:217
  454.9 4.3 convolution_convert_fusion.2
  461.4 12.2 %fusion = f32[384,1536]{1,0:T(8,128)} fusion(bf16[384,1536]{1,0:T(8,128)(2,1)S(1)} %get-tuple-element.286, bf16[384,1536]{1,0:T(8,128)(2,1)S(1)} %copy-done.165, bf16[384,1536]{1,0:T(8,128)(2,1)} %collective-permute-done.1.refs_3_, bf16[384,1536]{1,0:T(8,128)(2,1)} %collective-permute-done.refs_2_, bf16[384,384]{1,0:T(8,128)(2,1)S(1)} %copy-done.116, ...), kind=kOutput, calls=%fused_computation.15 | convolution fusion | flops 1844969472 | bytes 8257536 | tf_op jit(solution)/shard_map/dot_general | solution.py:19
  478.9 8.4 %attend_back.6 = (bf16[384,1536]{1,0:T(8,128)(2,1)S(1)}, f32[3,384]{1,0:T(4,128)S(1)}, f32[4,384]{1,0:T(4,128)S(1)}) custom-call(bf16[384,1152]{1,0:T(8,128)(2,1)S(1)} %copy-done.41, bf16[384,384]{1,0:T(8,128)(2,1)S(1)} %copy-done.81, f32[384,384]{1,0:T(8,128)S(1)} %copy-done.61, f32[3,384]{1,0:T(4,128)S(1)} %copy-done.11, f32[4,384]{1,0:T(4,128)S(1)} %copy-done.9, ...), custom_call_target="tpu_custom_call" | custom-call | flops 12000000000 | bytes 8000000 | tf_op jit(solution)/shard_map/attend_back/pallas_call | solution.py:217
  487.3 4.7 convolution_convert_fusion.1
  505.2 8.4 %attend_back.7 = (bf16[384,1536]{1,0:T(8,128)(2,1)S(1)}, f32[3,384]{1,0:T(4,128)S(1)}, f32[4,384]{1,0:T(4,128)S(1)}) custom-call(bf16[384,1152]{1,0:T(8,128)(2,1)S(1)} %copy-done.37, bf16[384,384]{1,0:T(8,128)(2,1)S(1)} %copy-done.77, f32[384,384]{1,0:T(8,128)S(1)} %copy-done.45, f32[3,384]{1,0:T(4,128)S(1)} %copy-done.7, f32[4,384]{1,0:T(4,128)S(1)} %copy-done.5, ...), custom_call_target="tpu_custom_call" | custom-call | flops 12000000000 | bytes 8000000 | tf_op jit(solution)/shard_map/attend_back/pallas_call | solution.py:217
  522.0 4.7 fusion.22
  535.4 5.5 collective-permute-start.52
  542.1 13.2 %collective-permute-done.49 = bf16[384,1536]{1,0:T(8,128)(2,1)} collective-permute-done((bf16[384,1536]{1,0:T(8,128)(2,1)S(1)}, bf16[384,1536]{1,0:T(8,128)(2,1)}, u32[]{:S(2)}, u32[]{:S(2)}) %collective-permute-start.49) | collective-permute-done | bytes 1179680 | tf_op jit(solution)/shard_map/ppermute | solution.py:503
  555.2 6.0 multiply_reduce_fusion.1
  566.2 7.5 %collective-permute-start.54 = (bf16[384,1536]{1,0:T(8,128)(2,1)S(1)}, bf16[384,1536]{1,0:T(8,128)(2,1)S(1)}, u32[]{:S(2)}, u32[]{:S(2)}) collective-permute-start(bf16[384,1536]{1,0:T(8,128)(2,1)S(1)} %add_convert_fusion.16), channel_id=1, source_target_pairs={{0,8},{1,9},{2,10},{3,11},{4,12},{5,13},{6,14},{7,15},{24,16},{25,... | collective-permute-start | bytes 3538952 | tf_op jit(solution)/shard_map/ppermute | solution.py:512
  593.1 16.5 %collective-permute-done.57 = bf16[768,1024]{1,0:T(8,128)(2,1)S(1)} collective-permute-done((bf16[768,1024]{1,0:T(8,128)(2,1)S(1)}, bf16[768,1024]{1,0:T(8,128)(2,1)S(1)}, u32[]{:S(2)}, u32[]{:S(2)}) %collective-permute-start.57) | collective-permute-done | bytes 1572896 | tf_op jit(solution)/shard_map/ppermute | solution.py:518
  613.2 7.3 %collective-permute-start.63 = (bf16[192,1536]{1,0:T(8,128)(2,1)S(1)}, bf16[192,1536]{1,0:T(8,128)(2,1)S(1)}, u32[]{:S(2)}, u32[]{:S(2)}) collective-permute-start(bf16[192,1536]{1,0:T(8,128)(2,1)S(1)} %get-tuple-element.477), channel_id=1, source_target_pairs={{0,8},{1,9},{2,10},{3,11},{4,12},{5,13},{6,14},{7,15},{24,16},{25,... | collective-permute-start | bytes 1769480 | tf_op jit(solution)/shard_map/ppermute | solution.py:512
  623.3 4.4 collective-permute-done.61
  628.7 6.3 collective-permute-done.64
  635.1 5.8 collective-permute-done.58
  641.4 4.5 fusion.61
  651.8 9.8 %collective-permute-done.65 = bf16[384,128]{0,1:T(8,128)(2,1)S(1)} collective-permute-done((bf16[384,128]{0,1:T(8,128)(2,1)S(1)}, bf16[384,128]{0,1:T(8,128)(2,1)S(1)}, u32[]{:S(2)}, u32[]{:S(2)}) %collective-permute-start.65) | collective-permute-done | bytes 98336 | tf_op jit(solution)/shard_map/ppermute | solution.py:503
  661.7 4.3 collective-permute-start.69
  675.0 8.2 %collective-permute-done.67 = bf16[384,768]{1,0:T(8,128)(2,1)S(1)} collective-permute-done((bf16[384,768]{1,0:T(8,128)(2,1)S(1)}, bf16[384,768]{1,0:T(8,128)(2,1)S(1)}, u32[]{:S(2)}, u32[]{:S(2)}) %collective-permute-start.67) | collective-permute-done | bytes 589856 | tf_op jit(solution)/shard_map/ppermute | solution.py:518
  692.8 8.3 %collective-permute-done.74 = bf16[192,1536]{1,0:T(8,128)(2,1)S(1)} collective-permute-done((bf16[192,1536]{1,0:T(8,128)(2,1)S(1)}, bf16[192,1536]{1,0:T(8,128)(2,1)S(1)}, u32[]{:S(2)}, u32[]{:S(2)}) %collective-permute-start.74) | collective-permute-done | bytes 589856 | tf_op jit(solution)/shard_map/ppermute | solution.py:518
  701.1 7.4 %collective-permute-done.75 = bf16[192,1536]{1,0:T(8,128)(2,1)S(1)} collective-permute-done((bf16[192,1536]{1,0:T(8,128)(2,1)S(1)}, bf16[192,1536]{1,0:T(8,128)(2,1)S(1)}, u32[]{:S(2)}, u32[]{:S(2)}) %collective-permute-start.75) | collective-permute-done | bytes 589856 | tf_op jit(solution)/shard_map/ppermute | solution.py:518
  (671 shorter events, 279.3 us)
Async XLA Ops:
  8.2 31.6 %collective-permute-start = (bf16[384,1536]{1,0:T(8,128)(2,1)}, bf16[384,1536]{1,0:T(8,128)(2,1)}, u32[]{:S(2)}, u32[]{:S(2)}) collective-permute-start(bf16[384,1536]{1,0:T(8,128)(2,1)} %pad_maximum_fusion.6.refs_1_), channel_id=1, source_target_pairs={{0,1},{1,0},{2,3},{3,2},{4,6},{5,7},{6,4},{7,5},{8,9},{9,8},{10,11... | collective-permute-start | bytes 3538952 | tf_op jit(solution)/shard_map/ppermute | solution.py:503
  11.2 28.7 %collective-permute-start.1 = (bf16[384,1536]{1,0:T(8,128)(2,1)}, bf16[384,1536]{1,0:T(8,128)(2,1)}, u32[]{:S(2)}, u32[]{:S(2)}) collective-permute-start(bf16[384,1536]{1,0:T(8,128)(2,1)} %pad_maximum_fusion.6.refs_1_), channel_id=1, source_target_pairs={{0,2},{1,3},{2,0},{3,1},{4,5},{5,4},{6,7},{7,6},{8,10},{9,11},{10,... | collective-permute-start | bytes 3538952 | tf_op jit(solution)/shard_map/ppermute | solution.py:506
  14.3 25.6 %collective-permute-start.2 = (bf16[384,128]{0,1:T(8,128)(2,1)}, bf16[384,128]{0,1:T(8,128)(2,1)}, u32[]{:S(2)}, u32[]{:S(2)}) collective-permute-start(bf16[384,128]{0,1:T(8,128)(2,1)} %get-tuple-element.492), channel_id=1, source_target_pairs={{0,1},{1,0},{2,3},{3,2},{4,6},{5,7},{6,4},{7,5},{8,9},{9,8},{10,11... | collective-permute-start | bytes 294920 | tf_op jit(solution)/shard_map/ppermute | solution.py:503
  14.8 25.1 %collective-permute-start.3 = (bf16[384,128]{0,1:T(8,128)(2,1)}, bf16[384,128]{0,1:T(8,128)(2,1)}, u32[]{:S(2)}, u32[]{:S(2)}) collective-permute-start(bf16[384,128]{0,1:T(8,128)(2,1)} %get-tuple-element.492), channel_id=1, source_target_pairs={{0,2},{1,3},{2,0},{3,1},{4,5},{5,4},{6,7},{7,6},{8,10},{9,11},{10,... | collective-permute-start | bytes 294920 | tf_op jit(solution)/shard_map/ppermute | solution.py:506
  39.9 21.9 %collective-permute-start.5 = (bf16[384,1536]{1,0:T(8,128)(2,1)}, bf16[384,1536]{1,0:T(8,128)(2,1)S(1)}, u32[]{:S(2)}, u32[]{:S(2)}) collective-permute-start(bf16[384,1536]{1,0:T(8,128)(2,1)} %collective-permute-done.refs_2_), channel_id=1, source_target_pairs={{0,2},{1,3},{2,0},{3,1},{4,5},{5,4},{6,7},{7,6},{8,10},{9,11},{10,... | collective-permute-start | bytes 3538952 | tf_op jit(solution)/shard_map/ppermute | solution.py:506
  41.5 42.5 %collective-permute-start.9 = (bf16[384,1536]{1,0:T(8,128)(2,1)}, bf16[384,1536]{1,0:T(8,128)(2,1)S(1)}, u32[]{:S(2)}, u32[]{:S(2)}) collective-permute-start(bf16[384,1536]{1,0:T(8,128)(2,1)} %collective-permute-done.refs_2_), channel_id=1, source_target_pairs={{0,4},{1,5},{2,6},{3,7},{4,0},{5,1},{6,2},{7,3},{8,12},{9,13},{10,... | collective-permute-start | bytes 3538952 | tf_op jit(solution)/shard_map/ppermute | solution.py:509
  43.7 40.2 %collective-permute-start.8 = (bf16[384,1536]{1,0:T(8,128)(2,1)}, bf16[384,1536]{1,0:T(8,128)(2,1)S(1)}, u32[]{:S(2)}, u32[]{:S(2)}) collective-permute-start(bf16[384,1536]{1,0:T(8,128)(2,1)} %collective-permute-done.1.refs_3_), channel_id=1, source_target_pairs={{0,4},{1,5},{2,6},{3,7},{4,0},{5,1},{6,2},{7,3},{8,12},{9,13},{10,... | collective-permute-start | bytes 3538952 | tf_op jit(solution)/shard_map/ppermute | solution.py:509
  61.8 36.8 %collective-permute-start.6 = (bf16[384,1536]{1,0:T(8,128)(2,1)S(1)}, bf16[384,1536]{1,0:T(8,128)(2,1)S(1)}, u32[]{:S(2)}, u32[]{:S(2)}) collective-permute-start(bf16[384,1536]{1,0:T(8,128)(2,1)S(1)} %pad_maximum_fusion.7.refs_1_), channel_id=1, source_target_pairs={{0,1},{1,0},{2,3},{3,2},{4,6},{5,7},{6,4},{7,5},{8,9},{9,8},{10,11... | collective-permute-start | bytes 3538952 | tf_op jit(solution)/shard_map/ppermute | solution.py:503
  64.3 34.3 %collective-permute-start.7 = (bf16[384,1536]{1,0:T(8,128)(2,1)S(1)}, bf16[384,1536]{1,0:T(8,128)(2,1)S(1)}, u32[]{:S(2)}, u32[]{:S(2)}) collective-permute-start(bf16[384,1536]{1,0:T(8,128)(2,1)S(1)} %pad_maximum_fusion.7.refs_1_), channel_id=1, source_target_pairs={{0,2},{1,3},{2,0},{3,1},{4,5},{5,4},{6,7},{7,6},{8,10},{9,11},{10,... | collective-permute-start | bytes 3538952 | tf_op jit(solution)/shard_map/ppermute | solution.py:506
  111.7 21.3 %collective-permute-start.12 = (bf16[384,768]{1,0:T(8,128)(2,1)S(1)}, bf16[384,768]{1,0:T(8,128)(2,1)S(1)}, u32[]{:S(2)}, u32[]{:S(2)}) collective-permute-start(bf16[384,768]{1,0:T(8,128)(2,1)S(1)} %get-tuple-element.218.refs_7_.refs_6_), channel_id=1, source_target_pairs={{0,1},{1,0},{2,3},{3,2},{4,6},{5,7},{6,4},{7,5},{8,9},{9,8},{10,11... | collective-permute-start | bytes 1769480 | tf_op jit(solution)/shard_map/ppermute | solution.py:503
  112.1 21.5 %collective-permute-start.13 = (bf16[384,768]{1,0:T(8,128)(2,1)S(1)}, bf16[384,768]{1,0:T(8,128)(2,1)S(1)}, u32[]{:S(2)}, u32[]{:S(2)}) collective-permute-start(bf16[384,768]{1,0:T(8,128)(2,1)S(1)} %get-tuple-element.218.refs_7_.refs_6_), channel_id=1, source_target_pairs={{0,2},{1,3},{2,0},{3,1},{4,5},{5,4},{6,7},{7,6},{8,10},{9,11},{10,... | collective-permute-start | bytes 1769480 | tf_op jit(solution)/shard_map/ppermute | solution.py:506
  133.0 21.4 %collective-permute-start.18 = (bf16[384,1024]{1,0:T(8,128)(2,1)S(1)}, bf16[384,1024]{1,0:T(8,128)(2,1)S(1)}, u32[]{:S(2)}, u32[]{:S(2)}) collective-permute-start(bf16[384,1024]{1,0:T(8,128)(2,1)S(1)} %pad_maximum_fusion.12), channel_id=1, source_target_pairs={{0,1},{1,0},{2,3},{3,2},{4,6},{5,7},{6,4},{7,5},{8,9},{9,8},{10,11... | collective-permute-start | bytes 2359304 | tf_op jit(solution)/shard_map/ppermute | solution.py:503
  157.7 22.3 %collective-permute-start.26 = (bf16[384,1024]{1,0:T(8,128)(2,1)}, bf16[384,1024]{1,0:T(8,128)(2,1)S(1)}, u32[]{:S(2)}, u32[]{:S(2)}) collective-permute-start(bf16[384,1024]{1,0:T(8,128)(2,1)} %pad_maximum_fusion.10), channel_id=1, source_target_pairs={{0,1},{1,0},{2,3},{3,2},{4,6},{5,7},{6,4},{7,5},{8,9},{9,8},{10,11... | collective-permute-start | bytes 2359304 | tf_op jit(solution)/shard_map/ppermute | solution.py:503
  158.5 21.6 %collective-permute-start.27 = (bf16[384,1024]{1,0:T(8,128)(2,1)}, bf16[384,1024]{1,0:T(8,128)(2,1)S(1)}, u32[]{:S(2)}, u32[]{:S(2)}) collective-permute-start(bf16[384,1024]{1,0:T(8,128)(2,1)} %pad_maximum_fusion.11), channel_id=1, source_target_pairs={{0,2},{1,3},{2,0},{3,1},{4,5},{5,4},{6,7},{7,6},{8,10},{9,11},{10,... | collective-permute-start | bytes 2359304 | tf_op jit(solution)/shard_map/ppermute | solution.py:506
  159.6 36.5 %collective-permute-start.28 = (bf16[384,1024]{1,0:T(8,128)(2,1)}, bf16[384,1024]{1,0:T(8,128)(2,1)S(1)}, u32[]{:S(2)}, u32[]{:S(2)}) collective-permute-start(bf16[384,1024]{1,0:T(8,128)(2,1)} %copy-done.170), channel_id=1, source_target_pairs={{0,2},{1,3},{2,0},{3,1},{4,5},{5,4},{6,7},{7,6},{8,10},{9,11},{10,... | collective-permute-start | bytes 2359304 | tf_op jit(solution)/shard_map/ppermute | solution.py:506
  173.3 30.2 %collective-permute-start.24 = (bf16[384,1536]{1,0:T(8,128)(2,1)}, bf16[384,1536]{1,0:T(8,128)(2,1)S(1)}, u32[]{:S(2)}, u32[]{:S(2)}) collective-permute-start(bf16[384,1536]{1,0:T(8,128)(2,1)} %get-tuple-element.237), channel_id=1, source_target_pairs={{0,1},{1,0},{2,3},{3,2},{4,6},{5,7},{6,4},{7,5},{8,9},{9,8},{10,11... | collective-permute-start | bytes 3538952 | tf_op jit(solution)/shard_map/ppermute | solution.py:503
  174.6 36.5 %collective-permute-start.25 = (bf16[384,1536]{1,0:T(8,128)(2,1)}, bf16[384,1536]{1,0:T(8,128)(2,1)S(1)}, u32[]{:S(2)}, u32[]{:S(2)}) collective-permute-start(bf16[384,1536]{1,0:T(8,128)(2,1)} %get-tuple-element.237), channel_id=1, source_target_pairs={{0,2},{1,3},{2,0},{3,1},{4,5},{5,4},{6,7},{7,6},{8,10},{9,11},{10,... | collective-permute-start | bytes 3538952 | tf_op jit(solution)/shard_map/ppermute | solution.py:506
  211.4 54.1 %collective-permute-start.22 = (bf16[384,1536]{1,0:T(8,128)(2,1)S(1)}, bf16[384,1536]{1,0:T(8,128)(2,1)}, u32[]{:S(2)}, u32[]{:S(2)}) collective-permute-start(bf16[384,1536]{1,0:T(8,128)(2,1)S(1)} %copy-done.96), channel_id=1, source_target_pairs={{0,1},{1,0},{2,3},{3,2},{4,6},{5,7},{6,4},{7,5},{8,9},{9,8},{10,11... | collective-permute-start | bytes 3538952 | tf_op jit(solution)/shard_map/ppermute | solution.py:503
  212.6 52.9 %collective-permute-start.23 = (bf16[384,1536]{1,0:T(8,128)(2,1)S(1)}, bf16[384,1536]{1,0:T(8,128)(2,1)}, u32[]{:S(2)}, u32[]{:S(2)}) collective-permute-start(bf16[384,1536]{1,0:T(8,128)(2,1)S(1)} %copy-done.96), channel_id=1, source_target_pairs={{0,2},{1,3},{2,0},{3,1},{4,5},{5,4},{6,7},{7,6},{8,10},{9,11},{10,... | collective-permute-start | bytes 3538952 | tf_op jit(solution)/shard_map/ppermute | solution.py:506
  215.9 36.2 %collective-permute-start.30 = (bf16[384,1536]{1,0:T(8,128)(2,1)S(1)}, bf16[384,1536]{1,0:T(8,128)(2,1)S(1)}, u32[]{:S(2)}, u32[]{:S(2)}) collective-permute-start(bf16[384,1536]{1,0:T(8,128)(2,1)S(1)} %collective-permute-done.24), channel_id=1, source_target_pairs={{0,2},{1,3},{2,0},{3,1},{4,5},{5,4},{6,7},{7,6},{8,10},{9,11},{10,... | collective-permute-start | bytes 3538952 | tf_op jit(solution)/shard_map/ppermute | solution.py:506
  310.3 29.2 %collective-permute-start.32 = (bf16[768,1536]{1,0:T(8,128)(2,1)}, bf16[768,1536]{1,0:T(8,128)(2,1)}, u32[]{:S(2)}, u32[]{:S(2)}) collective-permute-start(bf16[768,1536]{1,0:T(8,128)(2,1)} %convolution_convert_fusion.8), channel_id=1, source_target_pairs={{0,2},{1,3},{2,0},{3,1},{4,5},{5,4},{6,7},{7,6},{8,10},{9,11},{10,... | collective-permute-start | bytes 7077896 | tf_op jit(solution)/shard_map/ppermute | solution.py:506
  311.3 53.3 %collective-permute-start.34 = (bf16[768,1536]{1,0:T(8,128)(2,1)}, bf16[768,1536]{1,0:T(8,128)(2,1)S(1)}, u32[]{:S(2)}, u32[]{:S(2)}) collective-permute-start(bf16[768,1536]{1,0:T(8,128)(2,1)} %convolution_convert_fusion.7), channel_id=1, source_target_pairs={{0,2},{1,3},{2,0},{3,1},{4,5},{5,4},{6,7},{7,6},{8,10},{9,11},{10,... | collective-permute-start | bytes 7077896 | tf_op jit(solution)/shard_map/ppermute | solution.py:506
  390.3 38.0 %collective-permute-start.38 = (bf16[512,1536]{1,0:T(8,128)(2,1)S(1)}, bf16[512,1536]{1,0:T(8,128)(2,1)S(1)}, u32[]{:S(2)}, u32[]{:S(2)}) collective-permute-start(bf16[512,1536]{1,0:T(8,128)(2,1)S(1)} %add_convert_fusion.11), channel_id=1, source_target_pairs={{0,8},{1,9},{2,10},{3,11},{4,12},{5,13},{6,14},{7,15},{24,16},{25,... | collective-permute-start | bytes 4718600 | tf_op jit(solution)/shard_map/ppermute | solution.py:512
  429.4 47.4 %collective-permute-start.39 = (bf16[1536,1536]{1,0:T(8,128)(2,1)}, bf16[1536,1536]{1,0:T(8,128)(2,1)}, u32[]{:S(2)}, u32[]{:S(2)}) collective-permute-start(bf16[1536,1536]{1,0:T(8,128)(2,1)} %convolution_convert_fusion.3), channel_id=1, source_target_pairs={{0,4},{1,5},{2,6},{3,7},{4,0},{5,1},{6,2},{7,3},{8,12},{9,13},{10,... | collective-permute-start | bytes 14155784 | tf_op jit(solution)/shard_map/ppermute | solution.py:509
  429.4 44.2 %collective-permute-start.41 = (bf16[384,1536]{1,0:T(8,128)(2,1)}, bf16[384,1536]{1,0:T(8,128)(2,1)}, u32[]{:S(2)}, u32[]{:S(2)}) collective-permute-start(bf16[384,1536]{1,0:T(8,128)(2,1)} %add_convert_fusion.21), channel_id=1, source_target_pairs={{0,1},{1,0},{2,3},{3,2},{4,6},{5,7},{6,4},{7,5},{8,9},{9,8},{10,11... | collective-permute-start | bytes 3538952 | tf_op jit(solution)/shard_map/ppermute | solution.py:503
  441.3 35.5 %collective-permute-start.40 = (bf16[768,768]{1,0:T(8,128)(2,1)}, bf16[768,768]{1,0:T(8,128)(2,1)}, u32[]{:S(2)}, u32[]{:S(2)}) collective-permute-start(bf16[768,768]{1,0:T(8,128)(2,1)} %get-tuple-element.401), channel_id=1, source_target_pairs={{0,2},{1,3},{2,0},{3,1},{4,5},{5,4},{6,7},{7,6},{8,10},{9,11},{10,... | collective-permute-start | bytes 3538952 | tf_op jit(solution)/shard_map/ppermute | solution.py:506
  442.4 52.2 %collective-permute-start.44 = (bf16[768,1024]{1,0:T(8,128)(2,1)S(1)}, bf16[768,1024]{1,0:T(8,128)(2,1)}, u32[]{:S(2)}, u32[]{:S(2)}) collective-permute-start(bf16[768,1024]{1,0:T(8,128)(2,1)S(1)} %copy-done.89), channel_id=1, source_target_pairs={{0,8},{1,9},{2,10},{3,11},{4,12},{5,13},{6,14},{7,15},{24,16},{25,... | collective-permute-start | bytes 4718600 | tf_op jit(solution)/shard_map/ppermute | solution.py:512
  459.7 35.0 %collective-permute-start.45 = (bf16[512,1536]{1,0:T(8,128)(2,1)S(1)}, bf16[512,1536]{1,0:T(8,128)(2,1)S(1)}, u32[]{:S(2)}, u32[]{:S(2)}) collective-permute-start(bf16[512,1536]{1,0:T(8,128)(2,1)S(1)} %add_convert_fusion.10), channel_id=1, source_target_pairs={{8,16},{9,17},{10,18},{11,19},{12,20},{13,21},{14,22},{15,23},{16,... | collective-permute-start | bytes 4718600 | tf_op jit(solution)/shard_map/ppermute | solution.py:515
  473.6 61.8 %collective-permute-start.42 = (bf16[768,1024]{1,0:T(8,128)(2,1)S(1)}, bf16[768,1024]{1,0:T(8,128)(2,1)}, u32[]{:S(2)}, u32[]{:S(2)}) collective-permute-start(bf16[768,1024]{1,0:T(8,128)(2,1)S(1)} %copy-done.88), channel_id=1, source_target_pairs={{0,8},{1,9},{2,10},{3,11},{4,12},{5,13},{6,14},{7,15},{24,16},{25,... | collective-permute-start | bytes 4718600 | tf_op jit(solution)/shard_map/ppermute | solution.py:512
  494.7 32.7 %collective-permute-start.47 = (bf16[1536,1536]{1,0:T(8,128)(2,1)}, bf16[1536,1536]{1,0:T(8,128)(2,1)}, u32[]{:S(2)}, u32[]{:S(2)}) collective-permute-start(bf16[1536,1536]{1,0:T(8,128)(2,1)} %convolution_convert_fusion.1), channel_id=1, source_target_pairs={{0,4},{1,5},{2,6},{3,7},{4,0},{5,1},{6,2},{7,3},{8,12},{9,13},{10,... | collective-permute-start | bytes 14155784 | tf_op jit(solution)/shard_map/ppermute | solution.py:509
  498.2 29.2 %collective-permute-start.48 = (bf16[768,1536]{1,0:T(8,128)(2,1)}, bf16[768,1536]{1,0:T(8,128)(2,1)}, u32[]{:S(2)}, u32[]{:S(2)}) collective-permute-start(bf16[768,1536]{1,0:T(8,128)(2,1)} %get-tuple-element.394), channel_id=1, source_target_pairs={{0,2},{1,3},{2,0},{3,1},{4,5},{5,4},{6,7},{7,6},{8,10},{9,11},{10,... | collective-permute-start | bytes 7077896 | tf_op jit(solution)/shard_map/ppermute | solution.py:506
  501.4 39.5 %collective-permute-start.46 = (bf16[768,1024]{1,0:T(8,128)(2,1)S(1)}, bf16[768,1024]{1,0:T(8,128)(2,1)}, u32[]{:S(2)}, u32[]{:S(2)}) collective-permute-start(bf16[768,1024]{1,0:T(8,128)(2,1)S(1)} %add_convert_fusion.9), channel_id=1, source_target_pairs={{8,16},{9,17},{10,18},{11,19},{12,20},{13,21},{14,22},{15,23},{16,... | collective-permute-start | bytes 4718600 | tf_op jit(solution)/shard_map/ppermute | solution.py:515
  503.8 38.3 %collective-permute-start.50 = (bf16[512,1536]{1,0:T(8,128)(2,1)S(1)}, bf16[512,1536]{1,0:T(8,128)(2,1)}, u32[]{:S(2)}, u32[]{:S(2)}) collective-permute-start(bf16[512,1536]{1,0:T(8,128)(2,1)S(1)} %add_convert_fusion.8), channel_id=1, source_target_pairs={{8,0},{9,1},{10,2},{11,3},{12,4},{13,5},{14,6},{15,7},{16,24},{17,... | collective-permute-start | bytes 4718600 | tf_op jit(solution)/shard_map/ppermute | solution.py:518
  529.0 26.3 %collective-permute-start.49 = (bf16[384,1536]{1,0:T(8,128)(2,1)S(1)}, bf16[384,1536]{1,0:T(8,128)(2,1)}, u32[]{:S(2)}, u32[]{:S(2)}) collective-permute-start(bf16[384,1536]{1,0:T(8,128)(2,1)S(1)} %add_convert_fusion.17), channel_id=1, source_target_pairs={{0,1},{1,0},{2,3},{3,2},{4,6},{5,7},{6,4},{7,5},{8,9},{9,8},{10,11... | collective-permute-start | bytes 3538952 | tf_op jit(solution)/shard_map/ppermute | solution.py:503
  534.4 44.4 %collective-permute-start.51 = (bf16[768,1536]{1,0:T(8,128)(2,1)S(1)}, bf16[768,1536]{1,0:T(8,128)(2,1)S(1)}, u32[]{:S(2)}, u32[]{:S(2)}) collective-permute-start(bf16[768,1536]{1,0:T(8,128)(2,1)S(1)} %get-tuple-element.389), channel_id=1, source_target_pairs={{0,2},{1,3},{2,0},{3,1},{4,5},{5,4},{6,7},{7,6},{8,10},{9,11},{10,... | collective-permute-start | bytes 7077896 | tf_op jit(solution)/shard_map/ppermute | solution.py:506
  535.4 43.3 %collective-permute-start.52 = (bf16[384,768]{1,0:T(8,128)(2,1)}, bf16[384,768]{1,0:T(8,128)(2,1)S(1)}, u32[]{:S(2)}, u32[]{:S(2)}) collective-permute-start(bf16[384,768]{1,0:T(8,128)(2,1)} %add_convert_fusion.30), channel_id=1, source_target_pairs={{0,8},{1,9},{2,10},{3,11},{4,12},{5,13},{6,14},{7,15},{24,16},{25,... | collective-permute-start | bytes 1769480 | tf_op jit(solution)/shard_map/ppermute | solution.py:512
  563.4 29.8 %collective-permute-start.53 = (bf16[768,1024]{1,0:T(8,128)(2,1)S(1)}, bf16[768,1024]{1,0:T(8,128)(2,1)S(1)}, u32[]{:S(2)}, u32[]{:S(2)}) collective-permute-start(bf16[768,1024]{1,0:T(8,128)(2,1)S(1)} %add_convert_fusion.7), channel_id=1, source_target_pairs={{8,16},{9,17},{10,18},{11,19},{12,20},{13,21},{14,22},{15,23},{16,... | collective-permute-start | bytes 4718600 | tf_op jit(solution)/shard_map/ppermute | solution.py:515
  566.2 26.2 %collective-permute-start.54 = (bf16[384,1536]{1,0:T(8,128)(2,1)S(1)}, bf16[384,1536]{1,0:T(8,128)(2,1)S(1)}, u32[]{:S(2)}, u32[]{:S(2)}) collective-permute-start(bf16[384,1536]{1,0:T(8,128)(2,1)S(1)} %add_convert_fusion.16), channel_id=1, source_target_pairs={{0,8},{1,9},{2,10},{3,11},{4,12},{5,13},{6,14},{7,15},{24,16},{25,... | collective-permute-start | bytes 3538952 | tf_op jit(solution)/shard_map/ppermute | solution.py:512
  575.7 33.9 %collective-permute-start.57 = (bf16[768,1024]{1,0:T(8,128)(2,1)S(1)}, bf16[768,1024]{1,0:T(8,128)(2,1)S(1)}, u32[]{:S(2)}, u32[]{:S(2)}) collective-permute-start(bf16[768,1024]{1,0:T(8,128)(2,1)S(1)} %add_convert_fusion.6), channel_id=1, source_target_pairs={{8,0},{9,1},{10,2},{11,3},{12,4},{13,5},{14,6},{15,7},{16,24},{17,... | collective-permute-start | bytes 4718600 | tf_op jit(solution)/shard_map/ppermute | solution.py:518
  579.5 30.2 %collective-permute-start.56 = (bf16[384,1536]{1,0:T(8,128)(2,1)S(1)}, bf16[384,1536]{1,0:T(8,128)(2,1)S(1)}, u32[]{:S(2)}, u32[]{:S(2)}) collective-permute-start(bf16[384,1536]{1,0:T(8,128)(2,1)S(1)} %add_convert_fusion.15), channel_id=1, source_target_pairs={{0,1},{1,0},{2,3},{3,2},{4,6},{5,7},{6,4},{7,5},{8,9},{9,8},{10,11... | collective-permute-start | bytes 3538952 | tf_op jit(solution)/shard_map/ppermute | solution.py:503
  592.4 29.6 %collective-permute-start.60 = (bf16[384,768]{1,0:T(8,128)(2,1)S(1)}, bf16[384,768]{1,0:T(8,128)(2,1)S(1)}, u32[]{:S(2)}, u32[]{:S(2)}) collective-permute-start(bf16[384,768]{1,0:T(8,128)(2,1)S(1)} %add_convert_fusion.29), channel_id=1, source_target_pairs={{8,16},{9,17},{10,18},{11,19},{12,20},{13,21},{14,22},{15,23},{16,... | collective-permute-start | bytes 1769480 | tf_op jit(solution)/shard_map/ppermute | solution.py:515
  610.3 30.5 %collective-permute-start.58 = (bf16[768,1024]{1,0:T(8,128)(2,1)S(1)}, bf16[768,1024]{1,0:T(8,128)(2,1)S(1)}, u32[]{:S(2)}, u32[]{:S(2)}) collective-permute-start(bf16[768,1024]{1,0:T(8,128)(2,1)S(1)} %add_convert_fusion.5), channel_id=1, source_target_pairs={{8,0},{9,1},{10,2},{11,3},{12,4},{13,5},{14,6},{15,7},{16,24},{17,... | collective-permute-start | bytes 4718600 | tf_op jit(solution)/shard_map/ppermute | solution.py:518
  611.9 23.2 %collective-permute-start.59 = (bf16[384,1536]{1,0:T(8,128)(2,1)S(1)}, bf16[384,1536]{1,0:T(8,128)(2,1)S(1)}, u32[]{:S(2)}, u32[]{:S(2)}) collective-permute-start(bf16[384,1536]{1,0:T(8,128)(2,1)S(1)} %add_convert_fusion.14), channel_id=1, source_target_pairs={{8,16},{9,17},{10,18},{11,19},{12,20},{13,21},{14,22},{15,23},{16,... | collective-permute-start | bytes 3538952 | tf_op jit(solution)/shard_map/ppermute | solution.py:515
  646.0 37.2 %collective-permute-start.66 = (bf16[384,1024]{1,0:T(8,128)(2,1)S(1)}, bf16[384,1024]{1,0:T(8,128)(2,1)S(1)}, u32[]{:S(2)}, u32[]{:S(2)}) collective-permute-start(bf16[384,1024]{1,0:T(8,128)(2,1)S(1)} %get-tuple-element.419), channel_id=1, source_target_pairs={{0,1},{1,0},{2,3},{3,2},{4,6},{5,7},{6,4},{7,5},{8,9},{9,8},{10,11... | collective-permute-start | bytes 2359304 | tf_op jit(solution)/shard_map/ppermute | solution.py:503
  647.2 36.0 %collective-permute-start.68 = (bf16[384,1536]{1,0:T(8,128)(2,1)S(1)}, bf16[384,1536]{1,0:T(8,128)(2,1)S(1)}, u32[]{:S(2)}, u32[]{:S(2)}) collective-permute-start(bf16[384,1536]{1,0:T(8,128)(2,1)S(1)} %add_convert_fusion.12), channel_id=1, source_target_pairs={{8,0},{9,1},{10,2},{11,3},{12,4},{13,5},{14,6},{15,7},{16,24},{17,... | collective-permute-start | bytes 3538952 | tf_op jit(solution)/shard_map/ppermute | solution.py:518
  683.2 25.3 %collective-permute-start.72 = (bf16[384,1024]{1,0:T(8,128)(2,1)S(1)}, bf16[384,1024]{1,0:T(8,128)(2,1)S(1)}, u32[]{:S(2)}, u32[]{:S(2)}) collective-permute-start(bf16[384,1024]{1,0:T(8,128)(2,1)S(1)} %collective-permute-done.66), channel_id=1, source_target_pairs={{0,2},{1,3},{2,0},{3,1},{4,5},{5,4},{6,7},{7,6},{8,10},{9,11},{10,... | collective-permute-start | bytes 2359304 | tf_op jit(solution)/shard_map/ppermute | solution.py:506
  686.7 21.8 %collective-permute-start.75 = (bf16[192,1536]{1,0:T(8,128)(2,1)S(1)}, bf16[192,1536]{1,0:T(8,128)(2,1)S(1)}, u32[]{:S(2)}, u32[]{:S(2)}) collective-permute-start(bf16[192,1536]{1,0:T(8,128)(2,1)S(1)} %add_convert_fusion.24), channel_id=1, source_target_pairs={{8,0},{9,1},{10,2},{11,3},{12,4},{13,5},{14,6},{15,7},{16,24},{17,... | collective-permute-start | bytes 1769480 | tf_op jit(solution)/shard_map/ppermute | solution.py:518
  688.6 28.3 %collective-permute-start.77 = (bf16[384,1536]{1,0:T(8,128)(2,1)S(1)}, bf16[384,1536]{1,0:T(8,128)(2,1)S(1)}, u32[]{:S(2)}, u32[]{:S(2)}) collective-permute-start(bf16[384,1536]{1,0:T(8,128)(2,1)S(1)} %broadcast_select_fusion.3), channel_id=1, source_target_pairs={{0,4},{1,5},{2,6},{3,7},{4,0},{5,1},{6,2},{7,3},{8,12},{9,13},{10,... | collective-permute-start | bytes 3538952 | tf_op jit(solution)/shard_map/ppermute | solution.py:509
  (212 other events, 2234.3 us)

commit v3 on v2

--- a/solution.py
+++ b/solution.py
@@ -202,7 +202,7 @@
             jax.ShapeDtypeStruct((length, wide), HALF),
             square, square, square,
         ],
-        compiler_params=pltpu.CompilerParams(vmem_limit_bytes=48 * 1024 * 1024),
+        compiler_params=pltpu.CompilerParams(vmem_limit_bytes=60 * 1024 * 1024),
         cost_estimate=pl.CostEstimate(flops=16000000000, bytes_accessed=12000000, transcendentals=0),
         name="attend",
     )(normed, *pieces, rate, taps, marks, segc, segr)
@@ -227,7 +227,7 @@
             jax.ShapeDtypeStruct(taps.shape, SINGLE),
         ],
         scratch_shapes=[pltpu.VMEM((length, wide), SINGLE)],
-        compiler_params=pltpu.CompilerParams(vmem_limit_bytes=48 * 1024 * 1024),
+        compiler_params=pltpu.CompilerParams(vmem_limit_bytes=60 * 1024 * 1024),
         cost_estimate=pl.CostEstimate(flops=12000000000, bytes_accessed=8000000, transcendentals=0),
         name="attend_back",
     )(qkv, w, raw, rate, taps, marks, segc, segr, grads, tri, carried, probs)
@@ -266,7 +266,7 @@
             jax.ShapeDtypeStruct((length, width), SINGLE),
             jax.ShapeDtypeStruct((length, width), HALF),
         ],
-        compiler_params=pltpu.CompilerParams(vmem_limit_bytes=48 * 1024 * 1024),
+        compiler_params=pltpu.CompilerParams(vmem_limit_bytes=60 * 1024 * 1024),
         cost_estimate=pl.CostEstimate(flops=6000000000, bytes_accessed=14000000, transcendentals=0),
         name="leave_attention",
     )(places, rows, gain, *groups, *own, *other)
@@ -308,10 +308,75 @@
             jax.ShapeDtypeStruct((1, width), SINGLE),
             jax.ShapeDtypeStruct((4, length, width // 4), HALF),
         ],
-        compiler_params=pltpu.CompilerParams(vmem_limit_bytes=48 * 1024 * 1024),
+        compiler_params=pltpu.CompilerParams(vmem_limit_bytes=60 * 1024 * 1024),
         cost_estimate=pl.CostEstimate(flops=6000000000, bytes_accessed=14000000, transcendentals=0),
         name="return_to_attention",
     )(places, own_sum, last, upstream, middle, gain, *own, *other)
+
+
+def feed_forward_kernel(units, rows_ref, feed_ref, down_ref, both_ref, hidden_ref, part_ref):
+    both_ref[...] = mm(rows_ref[...], feed_ref[...])
+    gate = both_ref[:, :units]
+    hidden_ref[...] = (gate * jax.nn.sigmoid(gate) * both_ref[:, units:]).astype(HALF)
+    part_ref[...] = mm(hidden_ref[...], down_ref[...]).astype(HALF)
+
+
+def feed_forward(rows, mat_feed, mat_down, blocks):
+    total, width = rows.shape
+    units = mat_down.shape[0]
+    size = total // blocks
+    by_rows = lambda columns: pl.BlockSpec((size, columns), lambda i: (i, 0))
+    whole = lambda a: pl.BlockSpec(a.shape, lambda i: (0, 0))
+    return pl.pallas_call(
+        functools.partial(feed_forward_kernel, units),
+        grid=(blocks,),
+        in_specs=[by_rows(width), whole(mat_feed), whole(mat_down)],
+        out_specs=[by_rows(2 * units), by_rows(units), by_rows(width)],
+        out_shape=[
+            jax.ShapeDtypeStruct((total, 2 * units), SINGLE),
+            jax.ShapeDtypeStruct((total, units), HALF),
+            jax.ShapeDtypeStruct((total, width), HALF),
+        ],
+        compiler_params=pltpu.CompilerParams(vmem_limit_bytes=60 * 1024 * 1024),
+        cost_estimate=pl.CostEstimate(flops=18000000000, bytes_accessed=30000000, transcendentals=0),
+        name="feed_forward",
+    )(rows, mat_feed, mat_down)
+
+
+def feed_backward_kernel(units, *refs):
+    upstream_ref, both_ref, feed_ref, down_ref = refs[:4]
+    rows_ref, part_ref = refs[-2:]
+    grad = mm_nt(upstream_ref[...], down_ref[...])
+    gate = both_ref[:, :units]
+    up = both_ref[:, units:]
+    sig = jax.nn.sigmoid(gate)
+    rows_ref[:, units:] = (grad * gate * sig).astype(HALF)
+    rows_ref[:, :units] = (grad * up * sig * (1.0 + gate * (1.0 - sig))).astype(HALF)
+    part_ref[...] = mm_nt(rows_ref[...], feed_ref[...]).astype(HALF)
+
+
+def feed_backward(upstream, both, mat_feed, mat_down, blocks, first, number, filled=None):
+    total, width = upstream.shape
+    units = mat_down.shape[0]
+    size = total // blocks
+    by_rows = lambda columns: pl.BlockSpec((size, columns), lambda i: (i + first, 0))
+    whole = lambda a: pl.BlockSpec(a.shape, lambda i: (0, 0))
+    more = [] if filled is None else [filled]
+    return pl.pallas_call(
+        functools.partial(feed_backward_kernel, units),
+        grid=(number,),
+        in_specs=[by_rows(width), by_rows(2 * units), whole(mat_feed), whole(mat_down)]
+        + [pl.BlockSpec(memory_space=pl.ANY)] * len(more),
+        out_specs=[by_rows(2 * units), pl.BlockSpec((size, width), lambda i: (i, 0))],
+        out_shape=[
+            jax.ShapeDtypeStruct((total, 2 * units), HALF),
+            jax.ShapeDtypeStruct((size * number, width), HALF),
+        ],
+        input_output_aliases={4: 0} if more else {},
+        compiler_params=pltpu.CompilerParams(vmem_limit_bytes=60 * 1024 * 1024),
+        cost_estimate=pl.CostEstimate(flops=9000000000, bytes_accessed=25000000, transcendentals=0),
+        name="feed_backward",
+    )(upstream, both, mat_feed, mat_down, *more)
 
 
 AXES = ("grp", "fsdp")
@@ -492,12 +557,17 @@
             "near": permutation(lambda z, c, f: (2 * z + c, f ^ (1 + c))),
             "next": permutation(lambda z, c, f: (2 * z + c, f ^ (2 - c))),
             "twin": permutation(lambda z, c, f: (2 * z + 1 - c, f)),
+            "far": permutation(lambda z, c, f: (2 * z + c, f ^ 3)),
+            "level": permutation(lambda z, c, f: (2 * (z ^ 1) + c, f)),
+            "pair": permutation(lambda z, c, f: (2 * (3 - z) + c, f)),
             "inward": permutation(lambda z, c, f: (2 * (z ^ 1) + c, f) if z in (0, 3) else None),
             "across": permutation(lambda z, c, f: (2 * (3 - z) + c, f) if z in (1, 2) else None),
             "outward": permutation(lambda z, c, f: (2 * (z ^ 1) + c, f) if z in (1, 2) else None),
         }
         level = lax.axis_index("grp") // 2
         self.edge = (level == 0) | (level == 3)
+        self.keep = jnp.where(self.edge, 0, 1)
+        self.columns = [[2 * z + c for z in range(groups // 2)] for c in range(2)]
 
     def near(self, array):
         return lax.ppermute(array, AXES, self.pairs["near"])
@@ -508,6 +578,15 @@
     def twin(self, array):
         return lax.ppermute(array, AXES, self.pairs["twin"])
 
+    def far(self, array):
+        return lax.ppermute(array, AXES, self.pairs["far"])
+
+    def level(self, array):
+        return lax.ppermute(array, AXES, self.pairs["level"])
+
+    def pair(self, array):
+        return lax.ppermute(array, AXES, self.pairs["pair"])
+
     def inward(self, array):
         return lax.ppermute(array, AXES, self.pairs["inward"])
 
@@ -519,6 +598,15 @@
 
     def settled(self, total, got):
         return jnp.where(self.edge, got, total)
+
+    def halves(self, array, axis):
+        pick = lambda i: lax.dynamic_index_in_dim(array, i, axis, keepdims=False)
+        return pick(self.keep), pick(1 - self.keep)
+
+    def joined(self, mine, partner, axis):
+        return jnp.where(
+            self.edge, jnp.stack([mine, partner], axis=axis), jnp.stack([partner, mine], axis=axis)
+        )
 
     def place(self, number):
         apart = number ^ self.me
@@ -594,7 +682,7 @@
 
     small = jnp.concatenate([gain_in[:, None], gain_mid[:, None], conv_taps.T, w_rate], axis=1).astype(HALF)
     small = jnp.pad(small, ((0, 0), (0, 128 - small.shape[1])))
-    small_near, small_second = links.near(small), links.next(small)
+    small_near, small_second, small_far = links.near(small), links.next(small), links.far(small)
     block0 = group_columns(number[0])
     near0, second0 = links.near(block0), links.next(block0)
 
@@ -604,13 +692,11 @@
     unit_in = in_order(unit_in, 1)
     block1 = group_columns(number[1])
 
-    near0, second0, small_near, small_second, block1, unit_in = tie(
-        near0, second0, small_near, small_second, block1, unit_in
-    )
-    small_far = links.next(small_near)
+    near0, second0, small_near, small_second, small_far, block1, unit_in = tie(
+        near0, second0, small_near, small_second, small_far, block1, unit_in
+    )
     far0 = links.next(near0)
     twin0 = [links.twin(second0), links.twin(near0)]
-    block2 = group_columns(number[2])
     small = [small, small_near, small_second, small_far]
     small_order = jnp.concatenate(small, axis=0)
     small_plain = links.in_place(small)
@@ -624,7 +710,7 @@
     )
     rates = [cut(2.0 * rate_sig, k * count, count, 0) for k in number]
     taps = [cut(tap_values, k * wide, wide, 0).T for k in number]
-    normed, far0, block1, block2, *rest = tie(normed, far0, block1, block2, *rates, *taps)
+    normed, far0, block1, *rest = tie(normed, far0, block1, *rates, *taps)
     rates, taps = rest[:4], rest[4:]
 
     def forward(i, normed, pieces):
@@ -636,39 +722,41 @@
     twin0.append(links.twin(far0))
     near1, second1 = links.near(block1), links.next(block1)
     kept[0] = forward(0, normed, pieces[0])
-
-    normed, unused, *twin0 = tie(normed, kept[0][0], *twin0)
+    block2 = group_columns(number[2])
+    out_block = cut(w_out, own_at, half_width, 1).astype(HALF)
+
+    normed, unused, near1, second1, out_block, block2, *twin0 = tie(
+        normed, kept[0][0], near1, second1, out_block, block2, *twin0
+    )
+    far1 = links.next(near1)
+    twin1 = [links.twin(second1), links.twin(near1)]
     pieces[2] = [block2] + twin0
     kept[2] = forward(2, normed, pieces[2])
-
-    out_block = cut(w_out, own_at, half_width, 1).astype(HALF)
-    near1, second1, normed, unused, out_block = tie(near1, second1, normed, kept[2][0], out_block)
-    far1 = links.next(near1)
-    out_near, out_second = links.near(out_block), links.next(out_block)
-    twin1 = [links.twin(second1), links.twin(near1)]
-    upstream = mm(turn, cotangent[0]).astype(HALF)
     block3 = group_columns(number[3])
     out_rest = cut(w_out, other_at, half_width, 1).astype(HALF)
-    feed_first, feed_second, feed_far = [feed_block(i) for i in links.order[1:]]
-
-    far1, normed, block3, feed_first, feed_second, feed_far, upstream, out_rest = tie(
-        far1, normed, block3, feed_first, feed_second, feed_far, upstream, out_rest
-    )
+
+    far1, normed, unused, out_block, block3, out_rest = tie(far1, normed, kept[2][0], out_block, block3, out_rest)
     twin1.append(links.twin(far1))
     pieces[1] = [block1, near1, second1, far1]
-    feed_passing = links.near(feed_far)
-    feed_next = links.next(feed_second)
+    out_near, out_second = links.near(out_block), links.next(out_block)
     kept[1] = forward(1, normed, pieces[1])
-
-    normed, unused, out_near, out_second, *twin1 = tie(normed, kept[1][0], out_near, out_second, *twin1)
+    feed_first, feed_second, feed_far = [feed_block(i) for i in links.order[1:]]
+    upstream = mm(turn, cotangent[0]).astype(HALF)
+
+    normed, unused, out_near, out_second, feed_first, feed_second, feed_far, upstream, *twin1 = tie(
+        normed, kept[1][0], out_near, out_second, feed_first, feed_second, feed_far, upstream, *twin1
+    )
     pieces[3] = [block3] + twin1
     out_far = links.next(out_near)
+    feed_passing = links.near(feed_far)
     feed_near = links.near(feed_first)
+    feed_next = links.next(feed_second)
     out_twin = [links.twin(out_second), links.twin(out_near)]
     kept[3] = forward(3, normed, pieces[3])
 
     att3, out_far, feed_passing, *out_twin = tie(kept[3][0], out_far, feed_passing, *out_twin)
     feed_last = links.next(feed_passing)
+    up_near, up_second = links.near(upstream), links.next(upstream)
     out_twin.append(links.twin(out_far))
     places = [links.place(k) for k in number] + [own_at] + [k ^ (2 * core) for k in links.order]
     places = jnp.stack([jnp.asarray(p, jnp.int32) for p in places])
@@ -679,51 +767,46 @@
         places, rows, gain_second, [kept[0][0], kept[1][0], kept[2][0], att3], out_own, out_other
     )
 
+    normed_mid, feed_near, feed_next, up_near, up_second = tie(
+        normed_mid, feed_near, feed_next, up_near, up_second
+    )
+
     mid_near, mid_second = links.near(normed_mid), links.next(normed_mid)
-    feed_own = links.in_place([feed_block(links.me), feed_near, feed_next, feed_last])
+    feed_mine = feed_block(links.me)
     mat_down = jnp.concatenate(
         [cut(w_down, hid_own, h, 0), cut(w_down, hid_other, h, 0)], axis=0
     ).astype(HALF)
-    mid_near, mid_second, feed_own, mat_down = tie(mid_near, mid_second, feed_own, mat_down)
+    mid_near, mid_second, feed_mine, mat_down = tie(mid_near, mid_second, feed_mine, mat_down)
+    mid_far = links.next(mid_near)
+    feed_own = links.in_place([feed_mine, feed_near, feed_next, feed_last])
     feed_other = links.twin(feed_own)
-    mid_far = links.next(mid_near)
-    up_near, up_second = links.near(upstream), links.next(upstream)
     mat_feed = jnp.concatenate(
         [feed_own[:, :h], feed_other[:, :h], feed_own[:, h:], feed_other[:, h:]], axis=1
     )
-    mat_feed, mid_far = tie(mat_feed, mid_far)
+    mat_feed, mid_far, up_near = tie(mat_feed, mid_far, up_near)
+    up_far = links.next(up_near)
     normed_all = jnp.concatenate([normed_mid, mid_near, mid_second, mid_far], axis=0)
-    gate_up = mm(normed_all, mat_feed)
-    up_near, up_second, gate_up = tie(up_near, up_second, gate_up)
-    up_far = links.next(up_near)
-    gate_rows, up_rows = gate_up[:, :hidden_part], gate_up[:, hidden_part:]
-    gate_sig, hidden = gates(gate_rows, up_rows)
-    down_tail = mm(hidden[2 * length :], mat_down).astype(HALF)
-    up_far, down_tail, hidden = tie(up_far, down_tail, hidden)
-    down_part = links.next(down_tail)
+    gate_up, hidden, down_part = feed_forward(normed_all, mat_feed, mat_down, shards)
+    up_far, gate_up, hidden = tie(up_far, gate_up, hidden)
     upstream_all = jnp.concatenate([upstream, up_near, up_second, up_far], axis=0)
-    grad_hidden = mm_nt(upstream_all, mat_down)
-    feed_rows = gates_back(grad_hidden, gate_rows, up_rows, gate_sig)
-    mid_tail = mm_nt(feed_rows[2 * length :], mat_feed).astype(HALF)
-
-    mid_tail, feed_rows, hidden = tie(mid_tail, feed_rows, hidden)
+    feed_rows, mid_tail = feed_backward(upstream_all, gate_up, mat_feed, mat_down, shards, 2, 2)
+
+    mid_tail, feed_rows, hidden, upstream_all = tie(mid_tail, feed_rows, hidden, upstream_all)
     mid_got = links.next(mid_tail)
     grad_down = mm_tn(hidden, upstream_all).astype(HALF)
-    down_head = mm(hidden[: 2 * length], mat_down)
-    grad_down, feed_rows = tie(grad_down, feed_rows)
+    grad_down, feed_rows, upstream_all = tie(grad_down, feed_rows, upstream_all)
     down_got = links.twin(grad_down[h:])
-    mid_head = mm_nt(feed_rows[: 2 * length], mat_feed)
-    mid_got, mid_head, down_got, down_part, down_head = tie(mid_got, mid_head, down_got, down_part, down_head)
+    feed_rows, mid_head = feed_backward(upstream_all, gate_up, mat_feed, mat_down, shards, 0, 2, feed_rows)
+    mid_got, mid_head, down_got, feed_rows = tie(mid_got, mid_head, down_got, feed_rows)
     mid_own, mid_first = second_sum(mid_head, mid_got)
     mid_last = links.near(mid_first)
-    down_own, down_first = second_sum(down_head, down_part)
     down_sum = wide_sum(grad_down[:h], down_got).astype(HALF)
     down_in = links.inward(down_sum)
     grad_feed = mm_tn(normed_all, feed_rows).astype(HALF)
 
-    mid_last, grad_feed, down_first, mid_own = tie(mid_last, grad_feed, down_first, mid_own)
+    mid_last, grad_feed, mid_own, down_part = tie(mid_last, grad_feed, mid_own, down_part)
     feed_got = links.twin(jnp.concatenate([grad_feed[:, h : 2 * h], grad_feed[:, 3 * h :]], axis=1))
-    down_last = links.near(down_first)
+    result_got = links.next(down_part[2 * length :])
     grad_middle, branch_pair, grad_gain_mid, grad_att = return_to_attention(
         places, mid_own, mid_last, upstream, middle, gain_second, out_own, out_other
     )
@@ -747,17 +830,21 @@
     row_grads[2], rate_grads[2], tap_grads[2] = backward(2, grad_att)
     other = mm_tn(normed, row_grads[2]).astype(HALF)
 
-    other, out_got, grad_att, down_in, feed0, feed1 = tie(other, out_got, grad_att, down_in, feed0, feed1)
+    other, out_got, grad_att, down_in, feed0, feed1, result_got = tie(
+        other, out_got, grad_att, down_in, feed0, feed1, result_got
+    )
     got0 = links.twin(other)
     feed0_in = links.inward(feed0)
     down_sum = wide_sum(down_sum, down_in).astype(HALF)
     down_across = links.across(down_sum)
     out_head, out_tail = core_sum(out_grads[:, :half_width], out_got)
     out_part = links.next(out_tail)
+    result_own, result_first = second_sum(down_part[: 2 * length], result_got)
+    result_last = links.near(result_first)
     row_grads[0], rate_grads[0], tap_grads[0] = backward(0, grad_att)
     own0 = mm_tn(normed, row_grads[0]).astype(HALF)
 
-    own0, got0, out_part, grad_att, down_last = tie(own0, got0, out_part, grad_att, down_last)
+    own0, got0, out_part, grad_att = tie(own0, got0, out_part, grad_att)
     head0, tail0 = core_sum(own0, got0)
     part0 = links.next(tail0)
     out_own_sum, out_first = second_sum(out_head, out_part)
@@ -765,7 +852,9 @@
     row_grads[3], rate_grads[3], tap_grads[3] = backward(3, grad_att)
     other = mm_tn(normed, row_grads[3]).astype(HALF)
 
-    other, out_last, grad_att, feed0_in, down_across = tie(other, out_last, grad_att, feed0_in, down_across)
+    other, out_last, grad_att, feed0_in, down_across, result_last = tie(
+        other, out_last, grad_att, feed0_in, down_across, result_last
+    )
     got1 = links.twin(other)
     feed1_in = links.inward(feed1)
     feed0 = wide_sum(feed0, feed0_in).astype(HALF)
@@ -773,12 +862,18 @@
     down_sum = wide_sum(down_sum, down_across).astype(HALF)
     down_out = links.outward(down_sum)
     out_sum = wide_sum(out_own_sum, out_last).astype(HALF)
-    result = (middle + wide_sum(down_own, down_last)).astype(HALF)
+    result = (middle + wide_sum(result_own, result_last)).astype(HALF)
     result = mm_tn(turn, result).astype(HALF)
     row_grads[1], rate_grads[1], tap_grads[1] = backward(1, grad_att)
     own1 = mm_tn(normed, row_grads[1]).astype(HALF)
 
-    own1, got1, part0, out_sum = tie(own1, got1, part0, out_sum)
+    own1, got1, part0, out_sum, feed1_in, feed0_across, *late = tie(
+        own1, got1, part0, out_sum, feed1_in, feed0_across, *row_grads
+    )
+    feed1 = wide_sum(feed1, feed1_in).astype(HALF)
+    feed1_across = links.across(feed1)
+    feed0 = wide_sum(feed0, feed0_across).astype(HALF)
+    feed0_out = links.outward(feed0)
     sum0, first0 = second_sum(head0, part0)
     last0 = links.near(first0)
     head1, tail1 = core_sum(own1, got1)
@@ -798,20 +893,18 @@
         grad_rate_rows, mat_rate, (((0,), (1,)), ((), ())), preferred_element_type=SINGLE
     )
     for i in (0, 2):
-        grad_normed = grad_normed + mm_nt(row_grads[i], jnp.concatenate(pieces[i], axis=0))
-
-    feed1_in, feed0_across, last0, grad_normed, down_out = tie(feed1_in, feed0_across, last0, grad_normed, down_out)
-    feed1 = wide_sum(feed1, feed1_in).astype(HALF)
-    feed1_across = links.across(feed1)
-    feed0 = wide_sum(feed0, feed0_across).astype(HALF)
-    feed0_out = links.outward(feed0)
+        grad_normed = grad_normed + mm_nt(late[i], jnp.concatenate(pieces[i], axis=0))
+
+    last0, grad_normed, down_out, feed1_across = tie(last0, grad_normed, down_out, feed1_across)
+    feed1 = wide_sum(feed1, feed1_across).astype(HALF)
+    feed1_out = links.outward(feed1)
     out_in = links.inward(out_sum)
     sum0 = wide_sum(sum0, last0).astype(HALF)
     sum0_in = links.inward(sum0)
     down_sum = links.settled(down_sum, down_out)
     down_twin = links.twin(down_sum)
     for i in (1, 3):
-        grad_normed = grad_normed + mm_nt(row_grads[i], jnp.concatenate(pieces[i], axis=0))
+        grad_normed = grad_normed + mm_nt(late[i], jnp.concatenate(pieces[i], axis=0))
     grad_gain_in = jnp.sum(grad_normed * unit_in, axis=0)
     extra = jnp.concatenate(
         [grad_gain_in[:, None], in_order(grad_gain_mid[0], 0)[:, None], in_order(grad_taps.T, 0), grad_wrate],
@@ -828,11 +921,9 @@
     norm_grad = unit_back(grad_normed, unit_in, inverse_in, gain_first)
     grad_tokens = turn_back(turn, grad_middle + from_order(norm_grad, 1))
 
-    grad_tokens, feed1_across, sum0_in, extra_got, last1, feed0_out = tie(
-        grad_tokens, feed1_across, sum0_in, extra_got, last1, feed0_out
-    )
-    feed1 = wide_sum(feed1, feed1_across).astype(HALF)
-    feed1_out = links.outward(feed1)
+    grad_tokens, sum0_in, extra_got, last1, feed0_out = tie(
+        grad_tokens, sum0_in, extra_got, last1, feed0_out
+    )
     sum0 = wide_sum(sum0, sum0_in).astype(HALF)
     sum0_across = links.across(sum0)
     sum1 = wide_sum(sum1, last1).astype(HALF)
@@ -857,30 +948,31 @@
     feed_passing, feed_near = links.near(feed_blocks[3]), links.near(feed_blocks[1])
     feed_next = links.next(feed_blocks[2])
     extra_own, extra_first = second_sum(extra_head, extra_part)
-    extra_sum = wide_sum(extra_own, links.near(extra_first)).astype(HALF)
-    extra_in = links.inward(extra_sum)
-
-    feed_passing, out_out, sum0_out, extra_in, *sum1_across = tie(
-        feed_passing, out_out, sum0_out, extra_in, *sum1_across
-    )
+    extra_last = links.near(extra_first)
+
+    feed_passing, extra_last, *sum1_across = tie(feed_passing, extra_last, *sum1_across)
     feed_last = links.next(feed_passing)
     sum1 = [wide_sum(a, b).astype(HALF) for a, b in zip(sum1, sum1_across)]
     sum1_out = [links.outward(a) for a in sum1]
+    extra_sum = wide_sum(extra_own, extra_last).astype(HALF)
+    extra_level = links.level(extra_sum)
+
+    feed_last, sum0_out, out_out, extra_level, *sum1_out = tie(
+        feed_last, sum0_out, out_out, extra_level, *sum1_out
+    )
     out_sum = links.settled(out_sum, out_out)
     out_twin = links.twin(out_sum)
     sum0 = links.settled(sum0, sum0_out)
     twin0 = links.twin(sum0)
-    extra_sum = wide_sum(extra_sum, extra_in).astype(HALF)
-    extra_across = links.across(extra_sum)
+    extra_sum = wide_sum(extra_sum, extra_level).astype(HALF)
+    extra_pair = links.pair(extra_sum)
     grad_wout = links.by_core(out_sum, out_twin, 1).astype(SINGLE)
 
-    feed_last, extra_across, *sum1_out = tie(feed_last, extra_across, *sum1_out)
     feed_mine = links.in_place([feed_blocks[0], feed_near, feed_next, feed_last])
     feed_twin = links.twin(feed_mine)
     sum1 = jnp.concatenate([links.settled(a, b) for a, b in zip(sum1, sum1_out)], axis=0)
     twin1 = links.twin(sum1)
-    extra_sum = wide_sum(extra_sum, extra_across).astype(HALF)
-    extra = links.settled(extra_sum, links.outward(extra_sum)).astype(SINGLE)
+    extra = wide_sum(extra_sum, extra_pair)
 
     grad_gate, grad_up = [
         jnp.concatenate(

time: 743 us -> 718 us (0.966)
  Pallas kernels: 101 us -> 168 us
  waiting for transfers between devices: 221 us -> 173 us
  matrix products: 127 us -> 84.8 us
  local copies, waits for them, and re-layouts: 90.9 us -> 74.5 us
  other arithmetic: 85.1 us -> 98.9 us
    ppermute x22 -> x21, waiting for transfers between devices: 110 us -> 32.7 us  [next(): return lax.ppermute(array, AXES, self.pairs['next'])]
    pallas_call x0 -> x3, Pallas kernels: none -> 49.5 us  [the longest x2 28.8 us: feed_backward(): pl.pallas_call(functools.partial(feed_backward_kernel, units), grid=(numb...]
    unnamed x360 -> x196, local copies, waits for them, and re-layouts: 51.8 us -> 19.1 us
    dot_general x7 -> x4, matrix products: 54.1 us -> 27.7 us  [mm_nt(): lax.dot_general(left, right, (((1,), (1,)), ((), ())), preferred_element_...]
    dot_general x5 -> x2, matrix products: 21.4 us -> 1.73 us  [mm(): lax.dot_general(left, right, (((1,), (0,)), ((), ())), preferred_element_...]
    ppermute x0 -> x3, waiting for transfers between devices: none -> 17.9 us  [the longest x1 15 us: level(): return lax.ppermute(array, AXES, self.pairs['level'])]
    ppermute x16, waiting for transfers between devices: 46.6 us -> 60.5 us  [near(): return lax.ppermute(array, AXES, self.pairs['near'])]
    ppermute x8 -> x7, waiting for transfers between devices: 12 us -> 0.11 us  [inward(): return lax.ppermute(array, AXES, self.pairs['inward'])]
  transfers between devices with their start and end apart: 83 -> 82, of which waited for: 29 -> 19; matrix products, arithmetic and copies ran while one was open for 28% -> 31% of each run, Pallas kernels for 14% -> 22%
where the time goes in v3:
time: 718 us; the launch traced here: 706 us
  waiting for transfers between devices  173 us (24%)
  Pallas kernels  168 us (23%)
  starting transfers between devices  104 us (14%)
  other arithmetic  98.9 us (14%)
  matrix products  84.8 us (12%)
  local copies, waits for them, and re-layouts  74.5 us (10%)
    ppermute x7, waiting for transfers between devices, outward(): return lax.ppermute(array, AXES, self.pairs['outward'])  61 us
    ppermute x16, waiting for transfers between devices, near(): return lax.ppermute(array, AXES, self.pairs['near'])  60.5 us
    pallas_call x4, Pallas kernels, attn_forward(): pl.pallas_call(functools.partial(attn_forward_kernel, span, dim, count, t...  57.5 us
    dot_general x10, matrix products, mm_tn(): lax.dot_general(left, right, (((0,), (0,)), ((), ())), preferred_element_...  52.9 us
    pallas_call x4, Pallas kernels, attn_backward(): pl.pallas_call(functools.partial(attn_backward_kernel, span, dim, count,...  42.6 us
    ppermute x7, starting transfers between devices, inward(): return lax.ppermute(array, AXES, self.pairs['inward'])  34 us
    ppermute x21, waiting for transfers between devices, next(): return lax.ppermute(array, AXES, self.pairs['next'])  32.7 us
    pallas_call x2, Pallas kernels, feed_backward(): pl.pallas_call(functools.partial(feed_backward_kernel, units), grid=(numb...  28.8 us
  transfers between devices with their start and end apart: 82, of which 19 were waited for; matrix products, arithmetic and copies ran while one was open for 31% of the time, Pallas kernels for 22%

profile of v3, /device:TPU:0, one launch (start us, length us, event | category | flops | bytes accessed | tf_op | source)
XLA Modules:
  0.0 706.3 jit_solution(10347563797201540566)
XLA Ops:
  58.4 6.0 collective-permute-done.5.refs_4_
  64.9 14.4 %attend.4 = (bf16[384,384]{1,0:T(8,128)(2,1)}, bf16[384,1152]{1,0:T(8,128)(2,1)}, f32[384,384]{1,0:T(8,128)}, bf16[384,384]{1,0:T(8,128)(2,1)}, bf16[6,192,192]{...) custom-call(bf16[384,1536]{1,0:T(8,128)(2,1)} %copy-done.4, ...), custom_call_target="tpu_custom_call" | custom-call | flops 16000000000 | bytes 12000000 | tf_op jit(solution)/shard_map/attend/pallas_call | solution.py:196
  79.4 10.9 %collective-permute-done.6.refs_2_ = bf16[384,1536]{1,0:T(8,128)(2,1)} collective-permute-done((bf16[384,1536]{1,0:T(8,128)(2,1)S(1)}, bf16[384,1536]{1,0:T(8,128)(2,1)}, u32[]{:S(2)}, u32[]{:S(2)}) %collective-permute-start.6) | collective-permute-done | bytes 1179680 | tf_op jit(solution)/shard_map/ppermute | solution.py:573
  92.2 14.2 %attend.5 = (bf16[384,384]{1,0:T(8,128)(2,1)}, bf16[384,1152]{1,0:T(8,128)(2,1)}, f32[384,384]{1,0:T(8,128)}, bf16[384,384]{1,0:T(8,128)(2,1)}, bf16[6,192,192]{...) custom-call(bf16[384,1536]{1,0:T(8,128)(2,1)} %copy-done.4, ...), custom_call_target="tpu_custom_call" | custom-call | flops 16000000000 | bytes 12000000 | tf_op jit(solution)/shard_map/attend/pallas_call | solution.py:196
  108.8 14.4 %attend.6 = (bf16[384,384]{1,0:T(8,128)(2,1)}, bf16[384,1152]{1,0:T(8,128)(2,1)}, f32[384,384]{1,0:T(8,128)}, bf16[384,384]{1,0:T(8,128)(2,1)}, bf16[6,192,192]{...) custom-call(bf16[384,1536]{1,0:T(8,128)(2,1)} %copy-done.4, ...), custom_call_target="tpu_custom_call" | custom-call | flops 16000000000 | bytes 12000000 | tf_op jit(solution)/shard_map/attend/pallas_call | solution.py:196
  127.7 11.6 %collective-permute-done.17.refs_10_.refs_9_ = bf16[384,768]{1,0:T(8,128)(2,1)} collective-permute-done((bf16[384,768]{1,0:T(8,128)(2,1)}, bf16[384,768]{1,0:T(8,128)(2,1)}, u32[]{:S(2)}, u32[]{:S(2)}) %collective-permute-start.17) | collective-permute-done | bytes 589856 | tf_op jit(solution)/shard_map/ppermute | solution.py:576
  139.3 14.6 %attend.7 = (bf16[384,384]{1,0:T(8,128)(2,1)}, bf16[384,1152]{1,0:T(8,128)(2,1)}, f32[384,384]{1,0:T(8,128)}, bf16[384,384]{1,0:T(8,128)(2,1)}, bf16[6,192,192]{...) custom-call(bf16[384,1536]{1,0:T(8,128)(2,1)} %copy-done.4, ...), custom_call_target="tpu_custom_call" | custom-call | flops 16000000000 | bytes 12000000 | tf_op jit(solution)/shard_map/attend/pallas_call | solution.py:196
  153.8 12.9 %collective-permute-done.18 = bf16[384,1024]{1,0:T(8,128)(2,1)} collective-permute-done((bf16[384,1024]{1,0:T(8,128)(2,1)}, bf16[384,1024]{1,0:T(8,128)(2,1)}, u32[]{:S(2)}, u32[]{:S(2)}) %collective-permute-start.18) | collective-permute-done | bytes 786464 | tf_op jit(solution)/shard_map/ppermute | solution.py:573
  171.1 8.3 %leave_attention.1 = (bf16[384,1536]{1,0:T(8,128)(2,1)}, f32[384,1536]{1,0:T(8,128)}, bf16[384,1536]{1,0:T(8,128)(2,1)}) custom-call(s32[9]{0:T(128)} %stack.46.refs_0_, f32[384,1536]{1,0:T(8,128)} %copy-done.7, f32[1,1536]{1,0:T(1,128)} %fusion.110.refs_2_.refs_5_, bf16[384,384]{1,0:T(8,128)(2,1)} %get-tuple-element.218.refs_3_, ...), custom_call_target="tpu_custom_call" | custom-call | flops 6000000000 | bytes 14000000 | tf_op jit(solution)/shard_map/leave_attention/pallas_call | solution.py:260
  179.4 8.5 %collective-permute-done.22 = bf16[384,1024]{1,0:T(8,128)(2,1)} collective-permute-done((bf16[384,1024]{1,0:T(8,128)(2,1)}, bf16[384,1024]{1,0:T(8,128)(2,1)}, u32[]{:S(2)}, u32[]{:S(2)}) %collective-permute-start.22) | collective-permute-done | bytes 786464 | tf_op jit(solution)/shard_map/ppermute | solution.py:573
  190.3 3.3 dynamic-slice_convert_fusion.1
  197.0 20.1 %collective-permute-done.26 = bf16[384,1536]{1,0:T(8,128)(2,1)} collective-permute-done((bf16[384,1536]{1,0:T(8,128)(2,1)}, bf16[384,1536]{1,0:T(8,128)(2,1)}, u32[]{:S(2)}, u32[]{:S(2)}) %collective-permute-start.26) | collective-permute-done | bytes 1179680 | tf_op jit(solution)/shard_map/ppermute | solution.py:573
  219.9 4.2 collective-permute-done.28
  235.5 7.0 collective-permute-done.30
  246.8 20.7 %feed_forward.1 = (f32[1536,2048]{1,0:T(8,128)}, bf16[1536,1024]{1,0:T(8,128)(2,1)}, bf16[1536,1536]{1,0:T(8,128)(2,1)}) custom-call(bf16[1536,1536]{1,0:T(8,128)(2,1)} %constant_dynamic-update-slice_fusion.rows_ref, bf16[1536,2048]{1,0:T(8,128)(2,1)} %pad_maximum_fusion.feed_ref.refs_2_, bf16[1024,1536]{1,0:T(8,128)(2,1)} %pad_maximum_fusion.1.down_ref.refs_3_), custom_call_target="tpu_custom_call" | custom-call | flops 17999998976 | bytes 30000000 | tf_op jit(solution)/shard_map/feed_forward/pallas_call | solution.py:330
  269.9 14.3 %feed_backward.2 = (bf16[1536,2048]{1,0:T(8,128)(2,1)}, bf16[768,1536]{1,0:T(8,128)(2,1)}) custom-call(bf16[1536,1536]{1,0:T(8,128)(2,1)} %constant_dynamic-update-slice_fusion.4.refs_0_, f32[1536,2048]{1,0:T(8,128)} %get-tuple-element.274.refs_1_, bf16[1536,2048]{1,0:T(8,128)(2,1)} %pad_maximum_fusion.feed_ref.refs_2_, ...), custom_call_target="tpu_custom_call" | custom-call | flops 8999999488 | bytes 25000000 | tf_op jit(solution)/shard_map/feed_backward/pallas_call | solution.py:365
  285.3 8.1 %convolution_convert_fusion.6 = bf16[1024,1536]{1,0:T(8,128)(2,1)S(1)} fusion(bf16[1536,1024]{1,0:T(8,128)(2,1)} %get-tuple-element.279, bf16[1536,1536]{1,0:T(8,128)(2,1)} %constant_dynamic-update-slice_fusion.4.refs_0_), kind=kOutput, calls=%fused_computation.58 | convolution fusion | flops 4833411072 | bytes 11010048 | tf_op jit(solution)/shard_map/dot_general | solution.py:23
  295.4 14.4 %feed_backward.3 = (bf16[1536,2048]{1,0:T(8,128)(2,1)}, bf16[768,1536]{1,0:T(8,128)(2,1)}) custom-call(bf16[1536,1536]{1,0:T(8,128)(2,1)} %constant_dynamic-update-slice_fusion.4.refs_0_, f32[1536,2048]{1,0:T(8,128)} %get-tuple-element.274.refs_1_, bf16[1536,2048]{1,0:T(8,128)(2,1)} %pad_maximum_fusion.feed_ref.refs_2_, ...), custom_call_target="tpu_custom_call", output_to_operand_aliasing={{0}: (4, {})} | custom-call | flops 8999999488 | bytes 25000000 | tf_op jit(solution)/shard_map/feed_backward/pallas_call | solution.py:365
  309.8 3.5 collective-permute-done.32
  313.3 3.8 convert_add_fusion
  318.7 13.5 %convolution_convert_fusion.5 = bf16[1536,2048]{1,0:T(8,128)(2,1)S(1)} fusion(bf16[1536,1536]{1,0:T(8,128)(2,1)} %constant_dynamic-update-slice_fusion.rows_ref, bf16[1536,2048]{1,0:T(8,128)(2,1)} %get-tuple-element.289), kind=kOutput, calls=%fused_computation.5 | convolution fusion | flops 9666822144 | bytes 17301504 | tf_op jit(solution)/shard_map/dot_general | solution.py:23
  340.7 5.1 collective-permute-start.37
  348.5 9.7 %return_to_attention.1 = (f32[384,1536]{1,0:T(8,128)}, bf16[384,1536]{1,0:T(8,128)(2,1)}, f32[1,1536]{1,0:T(1,128)}, bf16[4,384,384]{2,1,0:T(8,128)(2,1)}) custom-call(s32[9]{0:T(128)} %stack.46.refs_0_, f32[384,1536]{1,0:T(8,128)} %get-tuple-element.296.refs_1_, bf16[384,1536]{1,0:T(8,128)(2,1)} %copy-done.87, bf16[384,1536]{1,0:T(8,128)(2,1)} %copy-done.14, ...), custom_call_target="tpu_custom_call" | custom-call | flops 6000000000 | bytes 14000000 | tf_op jit(solution)/shard_map/return_to_attention/pallas_call | solution.py:301
  358.2 4.3 convolution_convert_fusion.4
  369.9 11.3 %attend_back.4 = (bf16[384,1536]{1,0:T(8,128)(2,1)}, f32[3,384]{1,0:T(4,128)}, f32[4,384]{1,0:T(4,128)}) custom-call(bf16[384,1152]{1,0:T(8,128)(2,1)} %get-tuple-element.292.qkv_ref, bf16[384,384]{1,0:T(8,128)(2,1)} %get-tuple-element.293.w_ref, f32[384,384]{1,0:T(8,128)} %get-tuple-element.294.raw_ref, f32[3,384]{1,0:T(4,128)} %get-tuple-element.226.refs_5_.rate_ref, ...), custom_call_target="tpu_custom_call" | custom-call | flops 12000000000 | bytes 8000000 | tf_op jit(solution)/shard_map/attend_back/pallas_call | solution.py:217
  381.2 5.5 convolution_convert_fusion.3
  388.7 3.6 add_convert_fusion.20
  395.8 3.4 add_convert_fusion.10
  405.5 10.5 %attend_back.5 = (bf16[384,1536]{1,0:T(8,128)(2,1)}, f32[3,384]{1,0:T(4,128)}, f32[4,384]{1,0:T(4,128)}) custom-call(bf16[384,1152]{1,0:T(8,128)(2,1)} %get-tuple-element.313.qkv_ref, bf16[384,384]{1,0:T(8,128)(2,1)} %get-tuple-element.314.w_ref, f32[384,384]{1,0:T(8,128)} %get-tuple-element.315.raw_ref, f32[3,384]{1,0:T(4,128)} %get-tuple-element.216.refs_5_.rate_ref, ...), custom_call_target="tpu_custom_call" | custom-call | flops 12000000000 | bytes 8000000 | tf_op jit(solution)/shard_map/attend_back/pallas_call | solution.py:217
  416.0 5.6 convolution_convert_fusion.2
  426.1 10.5 %attend_back.6 = (bf16[384,1536]{1,0:T(8,128)(2,1)}, f32[3,384]{1,0:T(4,128)}, f32[4,384]{1,0:T(4,128)}) custom-call(bf16[384,1152]{1,0:T(8,128)(2,1)} %get-tuple-element.310.qkv_ref, bf16[384,384]{1,0:T(8,128)(2,1)} %get-tuple-element.311.w_ref, f32[384,384]{1,0:T(8,128)} %get-tuple-element.312.raw_ref, f32[3,384]{1,0:T(4,128)} %get-tuple-element.242.refs_5_.rate_ref, ...), custom_call_target="tpu_custom_call" | custom-call | flops 12000000000 | bytes 8000000 | tf_op jit(solution)/shard_map/attend_back/pallas_call | solution.py:217
  436.5 5.5 convolution_convert_fusion.1
  454.5 3.4 add_convert_fusion.8
  459.7 10.5 %attend_back.7 = (bf16[384,1536]{1,0:T(8,128)(2,1)}, f32[3,384]{1,0:T(4,128)}, f32[4,384]{1,0:T(4,128)}) custom-call(bf16[384,1152]{1,0:T(8,128)(2,1)} %get-tuple-element.335.qkv_ref, bf16[384,384]{1,0:T(8,128)(2,1)} %get-tuple-element.336.w_ref, f32[384,384]{1,0:T(8,128)} %get-tuple-element.337.raw_ref, f32[3,384]{1,0:T(4,128)} %get-tuple-element.233.refs_5_.rate_ref, ...), custom_call_target="tpu_custom_call" | custom-call | flops 12000000000 | bytes 8000000 | tf_op jit(solution)/shard_map/attend_back/pallas_call | solution.py:217
  486.8 5.4 fusion.22
  497.4 11.7 %collective-permute-start.53 = (bf16[384,768]{1,0:T(8,128)(2,1)}, bf16[384,768]{1,0:T(8,128)(2,1)S(1)}, u32[]{:S(2)}, u32[]{:S(2)}) collective-permute-start(bf16[384,768]{1,0:T(8,128)(2,1)} %add_convert_fusion.30), channel_id=1, source_target_pairs={{0,8},{1,9},{2,10},{3,11},{4,12},{5,13},{6,14},{7,15},{24,16},{25,... | collective-permute-start | bytes 1769480 | tf_op jit(solution)/shard_map/ppermute | solution.py:591
  509.2 10.9 %fusion.42 = f32[384,1536]{1,0:T(8,128)} fusion(f32[384,1536]{1,0:T(8,128)S(1)} %fusion.148, bf16[384,1536]{1,0:T(8,128)(2,1)S(1)} %copy-done.90, bf16[384,1536]{1,0:T(8,128)(2,1)} %collective-permute-done.5.refs_4_, bf16[384,1536]{1,0:T(8,128)(2,1)} %collective-permute-done.1.refs_3_, bf16[384,1536]{1,0:T(8,128)(2,1)} %collective-permute-done.refs_2_, ...), kind=kOutput, calls=%fused_computation.76 | convolution fusion | flops 1845559296 | bytes 10616832 | tf_op jit(solution)/shard_map/dot_general | solution.py:19
  523.4 5.6 fusion.39
  531.4 5.7 multiply_reduce_fusion.1
  538.9 4.7 collective-permute-start.54
  560.0 8.3 %collective-permute-done.57 = bf16[768,1024]{1,0:T(8,128)(2,1)S(1)} collective-permute-done((bf16[768,1024]{1,0:T(8,128)(2,1)S(1)}, bf16[768,1024]{1,0:T(8,128)(2,1)S(1)}, u32[]{:S(2)}, u32[]{:S(2)}) %collective-permute-start.57) | collective-permute-done | bytes 1572896 | tf_op jit(solution)/shard_map/ppermute | solution.py:597
  570.6 5.9 collective-permute-start.63
  579.2 20.3 %collective-permute-done.58 = bf16[768,1024]{1,0:T(8,128)(2,1)S(1)} collective-permute-done((bf16[768,1024]{1,0:T(8,128)(2,1)S(1)}, bf16[768,1024]{1,0:T(8,128)(2,1)S(1)}, u32[]{:S(2)}, u32[]{:S(2)}) %collective-permute-start.58) | collective-permute-done | bytes 1572896 | tf_op jit(solution)/shard_map/ppermute | solution.py:597
  600.2 4.5 fusion.60
  610.8 7.1 collective-permute-done.66
  623.3 32.4 %collective-permute-done.71 = bf16[384,768]{1,0:T(8,128)(2,1)S(1)} collective-permute-done((bf16[384,768]{1,0:T(8,128)(2,1)S(1)}, bf16[384,768]{1,0:T(8,128)(2,1)S(1)}, u32[]{:S(2)}, u32[]{:S(2)}) %collective-permute-start.71) | collective-permute-done | bytes 589856 | tf_op jit(solution)/shard_map/ppermute | solution.py:597
  658.3 4.0 fusion.45
  665.3 15.0 %collective-permute-done.72 = bf16[384,128]{0,1:T(8,128)(2,1)S(1)} collective-permute-done((bf16[384,128]{0,1:T(8,128)(2,1)S(1)}, bf16[384,128]{0,1:T(8,128)(2,1)S(1)}, u32[]{:S(2)}, u32[]{:S(2)}) %collective-permute-start.72) | collective-permute-done | bytes 98336 | tf_op jit(solution)/shard_map/ppermute | solution.py:585
  (499 shorter events, 244.0 us)
Async XLA Ops:
  8.2 39.5 %collective-permute-start = (bf16[384,1536]{1,0:T(8,128)(2,1)}, bf16[384,1536]{1,0:T(8,128)(2,1)}, u32[]{:S(2)}, u32[]{:S(2)}) collective-permute-start(bf16[384,1536]{1,0:T(8,128)(2,1)} %pad_maximum_fusion.5.refs_1_), channel_id=1, source_target_pairs={{0,1},{1,0},{2,3},{3,2},{4,6},{5,7},{6,4},{7,5},{8,9},{9,8},{10,11... | collective-permute-start | bytes 3538952 | tf_op jit(solution)/shard_map/ppermute | solution.py:573
  11.2 36.6 %collective-permute-start.1 = (bf16[384,1536]{1,0:T(8,128)(2,1)}, bf16[384,1536]{1,0:T(8,128)(2,1)}, u32[]{:S(2)}, u32[]{:S(2)}) collective-permute-start(bf16[384,1536]{1,0:T(8,128)(2,1)} %pad_maximum_fusion.5.refs_1_), channel_id=1, source_target_pairs={{0,2},{1,3},{2,0},{3,1},{4,5},{5,4},{6,7},{7,6},{8,10},{9,11},{10,... | collective-permute-start | bytes 3538952 | tf_op jit(solution)/shard_map/ppermute | solution.py:576
  14.2 33.5 %collective-permute-start.2 = (bf16[384,128]{0,1:T(8,128)(2,1)}, bf16[384,128]{0,1:T(8,128)(2,1)}, u32[]{:S(2)}, u32[]{:S(2)}) collective-permute-start(bf16[384,128]{0,1:T(8,128)(2,1)} %get-tuple-element.524), channel_id=1, source_target_pairs={{0,1},{1,0},{2,3},{3,2},{4,6},{5,7},{6,4},{7,5},{8,9},{9,8},{10,11... | collective-permute-start | bytes 294920 | tf_op jit(solution)/shard_map/ppermute | solution.py:573
  14.8 33.0 %collective-permute-start.3 = (bf16[384,128]{0,1:T(8,128)(2,1)}, bf16[384,128]{0,1:T(8,128)(2,1)}, u32[]{:S(2)}, u32[]{:S(2)}) collective-permute-start(bf16[384,128]{0,1:T(8,128)(2,1)} %get-tuple-element.524), channel_id=1, source_target_pairs={{0,2},{1,3},{2,0},{3,1},{4,5},{5,4},{6,7},{7,6},{8,10},{9,11},{10,... | collective-permute-start | bytes 294920 | tf_op jit(solution)/shard_map/ppermute | solution.py:576
  14.8 32.9 %collective-permute-start.4 = (bf16[384,128]{0,1:T(8,128)(2,1)}, bf16[384,128]{0,1:T(8,128)(2,1)}, u32[]{:S(2)}, u32[]{:S(2)}) collective-permute-start(bf16[384,128]{0,1:T(8,128)(2,1)} %get-tuple-element.524), channel_id=1, source_target_pairs={{0,3},{1,2},{2,1},{3,0},{4,7},{5,6},{6,5},{7,4},{8,11},{9,10},{10,... | collective-permute-start | bytes 294920 | tf_op jit(solution)/shard_map/ppermute | solution.py:582
  48.3 31.0 %collective-permute-start.9 = (bf16[384,1536]{1,0:T(8,128)(2,1)}, bf16[384,1536]{1,0:T(8,128)(2,1)}, u32[]{:S(2)}, u32[]{:S(2)}) collective-permute-start(bf16[384,1536]{1,0:T(8,128)(2,1)} %collective-permute-done.refs_2_), channel_id=1, source_target_pairs={{0,4},{1,5},{2,6},{3,7},{4,0},{5,1},{6,2},{7,3},{8,12},{9,13},{10,... | collective-permute-start | bytes 3538952 | tf_op jit(solution)/shard_map/ppermute | solution.py:579
  54.3 25.0 %collective-permute-start.8 = (bf16[384,1536]{1,0:T(8,128)(2,1)}, bf16[384,1536]{1,0:T(8,128)(2,1)}, u32[]{:S(2)}, u32[]{:S(2)}) collective-permute-start(bf16[384,1536]{1,0:T(8,128)(2,1)} %collective-permute-done.1.refs_3_), channel_id=1, source_target_pairs={{0,4},{1,5},{2,6},{3,7},{4,0},{5,1},{6,2},{7,3},{8,12},{9,13},{10,... | collective-permute-start | bytes 3538952 | tf_op jit(solution)/shard_map/ppermute | solution.py:579
  64.4 25.9 %collective-permute-start.6 = (bf16[384,1536]{1,0:T(8,128)(2,1)S(1)}, bf16[384,1536]{1,0:T(8,128)(2,1)}, u32[]{:S(2)}, u32[]{:S(2)}) collective-permute-start(bf16[384,1536]{1,0:T(8,128)(2,1)S(1)} %pad_maximum_fusion.6.refs_1_), channel_id=1, source_target_pairs={{0,1},{1,0},{2,3},{3,2},{4,6},{5,7},{6,4},{7,5},{8,9},{9,8},{10,11... | collective-permute-start | bytes 3538952 | tf_op jit(solution)/shard_map/ppermute | solution.py:573
  64.9 25.4 %collective-permute-start.7 = (bf16[384,1536]{1,0:T(8,128)(2,1)S(1)}, bf16[384,1536]{1,0:T(8,128)(2,1)}, u32[]{:S(2)}, u32[]{:S(2)}) collective-permute-start(bf16[384,1536]{1,0:T(8,128)(2,1)S(1)} %pad_maximum_fusion.6.refs_1_), channel_id=1, source_target_pairs={{0,2},{1,3},{2,0},{3,1},{4,5},{5,4},{6,7},{7,6},{8,10},{9,11},{10,... | collective-permute-start | bytes 3538952 | tf_op jit(solution)/shard_map/ppermute | solution.py:576
  64.9 25.3 %collective-permute-start.10 = (bf16[384,1536]{1,0:T(8,128)(2,1)}, bf16[384,1536]{1,0:T(8,128)(2,1)}, u32[]{:S(2)}, u32[]{:S(2)}) collective-permute-start(bf16[384,1536]{1,0:T(8,128)(2,1)} %collective-permute-done.5.refs_4_), channel_id=1, source_target_pairs={{0,4},{1,5},{2,6},{3,7},{4,0},{5,1},{6,2},{7,3},{8,12},{9,13},{10,... | collective-permute-start | bytes 3538952 | tf_op jit(solution)/shard_map/ppermute | solution.py:579
  91.7 31.4 %collective-permute-start.15 = (bf16[384,1536]{1,0:T(8,128)(2,1)}, bf16[384,1536]{1,0:T(8,128)(2,1)S(1)}, u32[]{:S(2)}, u32[]{:S(2)}) collective-permute-start(bf16[384,1536]{1,0:T(8,128)(2,1)} %collective-permute-done.6.refs_2_), channel_id=1, source_target_pairs={{0,4},{1,5},{2,6},{3,7},{4,0},{5,1},{6,2},{7,3},{8,12},{9,13},{10,... | collective-permute-start | bytes 3538952 | tf_op jit(solution)/shard_map/ppermute | solution.py:579
  91.7 31.4 %collective-permute-start.14 = (bf16[384,1536]{1,0:T(8,128)(2,1)}, bf16[384,1536]{1,0:T(8,128)(2,1)}, u32[]{:S(2)}, u32[]{:S(2)}) collective-permute-start(bf16[384,1536]{1,0:T(8,128)(2,1)} %collective-permute-done.7.refs_3_), channel_id=1, source_target_pairs={{0,4},{1,5},{2,6},{3,7},{4,0},{5,1},{6,2},{7,3},{8,12},{9,13},{10,... | collective-permute-start | bytes 3538952 | tf_op jit(solution)/shard_map/ppermute | solution.py:579
  124.1 29.7 %collective-permute-start.20 = (bf16[384,768]{1,0:T(8,128)(2,1)}, bf16[384,768]{1,0:T(8,128)(2,1)}, u32[]{:S(2)}, u32[]{:S(2)}) collective-permute-start(bf16[384,768]{1,0:T(8,128)(2,1)} %collective-permute-done.12.refs_8_.refs_7_), channel_id=1, source_target_pairs={{0,4},{1,5},{2,6},{3,7},{4,0},{5,1},{6,2},{7,3},{8,12},{9,13},{10,... | collective-permute-start | bytes 1769480 | tf_op jit(solution)/shard_map/ppermute | solution.py:579
  125.0 62.9 %collective-permute-start.24 = (bf16[384,1536]{1,0:T(8,128)(2,1)S(1)}, bf16[384,1536]{1,0:T(8,128)(2,1)S(1)}, u32[]{:S(2)}, u32[]{:S(2)}) collective-permute-start(bf16[384,1536]{1,0:T(8,128)(2,1)S(1)} %convolution_convert_fusion.8.refs_3_), channel_id=1, source_target_pairs={{0,1},{1,0},{2,3},{3,2},{4,6},{5,7},{6,4},{7,5},{8,9},{9,8},{10,11... | collective-permute-start | bytes 3538952 | tf_op jit(solution)/shard_map/ppermute | solution.py:573
  126.1 61.8 %collective-permute-start.25 = (bf16[384,1536]{1,0:T(8,128)(2,1)S(1)}, bf16[384,1536]{1,0:T(8,128)(2,1)S(1)}, u32[]{:S(2)}, u32[]{:S(2)}) collective-permute-start(bf16[384,1536]{1,0:T(8,128)(2,1)S(1)} %convolution_convert_fusion.8.refs_3_), channel_id=1, source_target_pairs={{0,2},{1,3},{2,0},{3,1},{4,5},{5,4},{6,7},{7,6},{8,10},{9,11},{10,... | collective-permute-start | bytes 3538952 | tf_op jit(solution)/shard_map/ppermute | solution.py:576
  126.9 39.9 %collective-permute-start.18 = (bf16[384,1024]{1,0:T(8,128)(2,1)}, bf16[384,1024]{1,0:T(8,128)(2,1)}, u32[]{:S(2)}, u32[]{:S(2)}) collective-permute-start(bf16[384,1024]{1,0:T(8,128)(2,1)} %pad_maximum_fusion.11), channel_id=1, source_target_pairs={{0,1},{1,0},{2,3},{3,2},{4,6},{5,7},{6,4},{7,5},{8,9},{9,8},{10,11... | collective-permute-start | bytes 2359304 | tf_op jit(solution)/shard_map/ppermute | solution.py:573
  187.9 29.1 %collective-permute-start.26 = (bf16[384,1536]{1,0:T(8,128)(2,1)}, bf16[384,1536]{1,0:T(8,128)(2,1)}, u32[]{:S(2)}, u32[]{:S(2)}) collective-permute-start(bf16[384,1536]{1,0:T(8,128)(2,1)} %get-tuple-element.258), channel_id=1, source_target_pairs={{0,1},{1,0},{2,3},{3,2},{4,6},{5,7},{6,4},{7,5},{8,9},{9,8},{10,11... | collective-permute-start | bytes 3538952 | tf_op jit(solution)/shard_map/ppermute | solution.py:573
  189.5 27.5 %collective-permute-start.27 = (bf16[384,1536]{1,0:T(8,128)(2,1)}, bf16[384,1536]{1,0:T(8,128)(2,1)}, u32[]{:S(2)}, u32[]{:S(2)}) collective-permute-start(bf16[384,1536]{1,0:T(8,128)(2,1)} %get-tuple-element.258), channel_id=1, source_target_pairs={{0,2},{1,3},{2,0},{3,1},{4,5},{5,4},{6,7},{7,6},{8,10},{9,11},{10,... | collective-permute-start | bytes 3538952 | tf_op jit(solution)/shard_map/ppermute | solution.py:576
  193.6 30.6 %collective-permute-start.28 = (bf16[384,1024]{1,0:T(8,128)(2,1)}, bf16[384,1024]{1,0:T(8,128)(2,1)S(1)}, u32[]{:S(2)}, u32[]{:S(2)}) collective-permute-start(bf16[384,1024]{1,0:T(8,128)(2,1)} %collective-permute-done.18), channel_id=1, source_target_pairs={{0,2},{1,3},{2,0},{3,1},{4,5},{5,4},{6,7},{7,6},{8,10},{9,11},{10,... | collective-permute-start | bytes 2359304 | tf_op jit(solution)/shard_map/ppermute | solution.py:576
  242.5 25.0 %collective-permute-start.31 = (bf16[384,1536]{1,0:T(8,128)(2,1)S(1)}, bf16[384,1536]{1,0:T(8,128)(2,1)}, u32[]{:S(2)}, u32[]{:S(2)}) collective-permute-start(bf16[384,1536]{1,0:T(8,128)(2,1)S(1)} %collective-permute-done.24), channel_id=1, source_target_pairs={{0,2},{1,3},{2,0},{3,1},{4,5},{5,4},{6,7},{7,6},{8,10},{9,11},{10,... | collective-permute-start | bytes 3538952 | tf_op jit(solution)/shard_map/ppermute | solution.py:576
  284.3 29.1 %collective-permute-start.32 = (bf16[768,1536]{1,0:T(8,128)(2,1)}, bf16[768,1536]{1,0:T(8,128)(2,1)S(1)}, u32[]{:S(2)}, u32[]{:S(2)}) collective-permute-start(bf16[768,1536]{1,0:T(8,128)(2,1)} %get-tuple-element.278), channel_id=1, source_target_pairs={{0,2},{1,3},{2,0},{3,1},{4,5},{5,4},{6,7},{7,6},{8,10},{9,11},{10,... | collective-permute-start | bytes 7077896 | tf_op jit(solution)/shard_map/ppermute | solution.py:576
  336.8 25.7 %collective-permute-start.35 = (bf16[1536,1024]{1,0:T(8,128)(2,1)}, bf16[1536,1024]{1,0:T(8,128)(2,1)}, u32[]{:S(2)}, u32[]{:S(2)}) collective-permute-start(bf16[1536,1024]{1,0:T(8,128)(2,1)} %pad_maximum_fusion.2), channel_id=1, source_target_pairs={{0,4},{1,5},{2,6},{3,7},{4,0},{5,1},{6,2},{7,3},{8,12},{9,13},{10,... | collective-permute-start | bytes 9437192 | tf_op jit(solution)/shard_map/ppermute | solution.py:579
  340.7 46.0 %collective-permute-start.37 = (bf16[512,1536]{1,0:T(8,128)(2,1)}, bf16[512,1536]{1,0:T(8,128)(2,1)}, u32[]{:S(2)}, u32[]{:S(2)}) collective-permute-start(bf16[512,1536]{1,0:T(8,128)(2,1)} %add_convert_fusion.11), channel_id=1, source_target_pairs={{0,8},{1,9},{2,10},{3,11},{4,12},{5,13},{6,14},{7,15},{24,16},{25,... | collective-permute-start | bytes 4718600 | tf_op jit(solution)/shard_map/ppermute | solution.py:591
  347.4 39.3 %collective-permute-start.38 = (bf16[768,1536]{1,0:T(8,128)(2,1)}, bf16[768,1536]{1,0:T(8,128)(2,1)}, u32[]{:S(2)}, u32[]{:S(2)}) collective-permute-start(bf16[768,1536]{1,0:T(8,128)(2,1)} %slice.380), channel_id=1, source_target_pairs={{0,2},{1,3},{2,0},{3,1},{4,5},{5,4},{6,7},{7,6},{8,10},{9,11},{10,... | collective-permute-start | bytes 7077896 | tf_op jit(solution)/shard_map/ppermute | solution.py:576
  386.7 37.6 %collective-permute-start.39 = (bf16[1536,1536]{1,0:T(8,128)(2,1)}, bf16[1536,1536]{1,0:T(8,128)(2,1)}, u32[]{:S(2)}, u32[]{:S(2)}) collective-permute-start(bf16[1536,1536]{1,0:T(8,128)(2,1)} %convolution_convert_fusion.3), channel_id=1, source_target_pairs={{0,4},{1,5},{2,6},{3,7},{4,0},{5,1},{6,2},{7,3},{8,12},{9,13},{10,... | collective-permute-start | bytes 14155784 | tf_op jit(solution)/shard_map/ppermute | solution.py:579
  392.3 29.3 %collective-permute-start.40 = (bf16[768,768]{1,0:T(8,128)(2,1)}, bf16[768,768]{1,0:T(8,128)(2,1)}, u32[]{:S(2)}, u32[]{:S(2)}) collective-permute-start(bf16[768,768]{1,0:T(8,128)(2,1)} %get-tuple-element.431), channel_id=1, source_target_pairs={{0,2},{1,3},{2,0},{3,1},{4,5},{5,4},{6,7},{7,6},{8,10},{9,11},{10,... | collective-permute-start | bytes 3538952 | tf_op jit(solution)/shard_map/ppermute | solution.py:576
  393.3 48.8 %collective-permute-start.42 = (bf16[768,1024]{1,0:T(8,128)(2,1)S(1)}, bf16[768,1024]{1,0:T(8,128)(2,1)}, u32[]{:S(2)}, u32[]{:S(2)}) collective-permute-start(bf16[768,1024]{1,0:T(8,128)(2,1)S(1)} %get-tuple-element.329), channel_id=1, source_target_pairs={{0,8},{1,9},{2,10},{3,11},{4,12},{5,13},{6,14},{7,15},{24,16},{25,... | collective-permute-start | bytes 4718600 | tf_op jit(solution)/shard_map/ppermute | solution.py:591
  399.2 42.8 %collective-permute-start.43 = (bf16[512,1536]{1,0:T(8,128)(2,1)}, bf16[512,1536]{1,0:T(8,128)(2,1)}, u32[]{:S(2)}, u32[]{:S(2)}) collective-permute-start(bf16[512,1536]{1,0:T(8,128)(2,1)} %add_convert_fusion.10), channel_id=1, source_target_pairs={{8,16},{9,17},{10,18},{11,19},{12,20},{13,21},{14,22},{15,23},{16,... | collective-permute-start | bytes 4718600 | tf_op jit(solution)/shard_map/ppermute | solution.py:594
  404.0 38.1 %collective-permute-start.44 = (bf16[384,1536]{1,0:T(8,128)(2,1)}, bf16[384,1536]{1,0:T(8,128)(2,1)}, u32[]{:S(2)}, u32[]{:S(2)}) collective-permute-start(bf16[384,1536]{1,0:T(8,128)(2,1)} %add_convert_fusion.19), channel_id=1, source_target_pairs={{0,1},{1,0},{2,3},{3,2},{4,6},{5,7},{6,4},{7,5},{8,9},{9,8},{10,11... | collective-permute-start | bytes 3538952 | tf_op jit(solution)/shard_map/ppermute | solution.py:573
  421.6 57.6 %collective-permute-start.47 = (bf16[768,1024]{1,0:T(8,128)(2,1)}, bf16[768,1024]{1,0:T(8,128)(2,1)}, u32[]{:S(2)}, u32[]{:S(2)}) collective-permute-start(bf16[768,1024]{1,0:T(8,128)(2,1)} %get-tuple-element.345), channel_id=1, source_target_pairs={{0,8},{1,9},{2,10},{3,11},{4,12},{5,13},{6,14},{7,15},{24,16},{25,... | collective-permute-start | bytes 4718600 | tf_op jit(solution)/shard_map/ppermute | solution.py:591
  442.1 37.2 %collective-permute-start.45 = (bf16[1536,1536]{1,0:T(8,128)(2,1)}, bf16[1536,1536]{1,0:T(8,128)(2,1)}, u32[]{:S(2)}, u32[]{:S(2)}) collective-permute-start(bf16[1536,1536]{1,0:T(8,128)(2,1)} %convolution_convert_fusion.1), channel_id=1, source_target_pairs={{0,4},{1,5},{2,6},{3,7},{4,0},{5,1},{6,2},{7,3},{8,12},{9,13},{10,... | collective-permute-start | bytes 14155784 | tf_op jit(solution)/shard_map/ppermute | solution.py:579
  448.4 30.8 %collective-permute-start.46 = (bf16[768,1536]{1,0:T(8,128)(2,1)}, bf16[768,1536]{1,0:T(8,128)(2,1)}, u32[]{:S(2)}, u32[]{:S(2)}) collective-permute-start(bf16[768,1536]{1,0:T(8,128)(2,1)} %get-tuple-element.424), channel_id=1, source_target_pairs={{0,2},{1,3},{2,0},{3,1},{4,5},{5,4},{6,7},{7,6},{8,10},{9,11},{10,... | collective-permute-start | bytes 7077896 | tf_op jit(solution)/shard_map/ppermute | solution.py:576
  452.6 26.6 %collective-permute-start.48 = (bf16[768,1024]{1,0:T(8,128)(2,1)}, bf16[768,1024]{1,0:T(8,128)(2,1)}, u32[]{:S(2)}, u32[]{:S(2)}) collective-permute-start(bf16[768,1024]{1,0:T(8,128)(2,1)} %add_convert_fusion.9), channel_id=1, source_target_pairs={{8,16},{9,17},{10,18},{11,19},{12,20},{13,21},{14,22},{15,23},{16,... | collective-permute-start | bytes 4718600 | tf_op jit(solution)/shard_map/ppermute | solution.py:594
  457.9 71.2 %collective-permute-start.50 = (bf16[512,1536]{1,0:T(8,128)(2,1)}, bf16[512,1536]{1,0:T(8,128)(2,1)}, u32[]{:S(2)}, u32[]{:S(2)}) collective-permute-start(bf16[512,1536]{1,0:T(8,128)(2,1)} %add_convert_fusion.8), channel_id=1, source_target_pairs={{8,0},{9,1},{10,2},{11,3},{12,4},{13,5},{14,6},{15,7},{16,24},{17,... | collective-permute-start | bytes 4718600 | tf_op jit(solution)/shard_map/ppermute | solution.py:597
  480.8 49.6 %collective-permute-start.49 = (bf16[384,1536]{1,0:T(8,128)(2,1)S(1)}, bf16[384,1536]{1,0:T(8,128)(2,1)S(1)}, u32[]{:S(2)}, u32[]{:S(2)}) collective-permute-start(bf16[384,1536]{1,0:T(8,128)(2,1)S(1)} %add_convert_fusion.17), channel_id=1, source_target_pairs={{0,1},{1,0},{2,3},{3,2},{4,6},{5,7},{6,4},{7,5},{8,9},{9,8},{10,11... | collective-permute-start | bytes 3538952 | tf_op jit(solution)/shard_map/ppermute | solution.py:573
  484.9 46.5 %collective-permute-start.51 = (bf16[768,1024]{1,0:T(8,128)(2,1)S(1)}, bf16[768,1024]{1,0:T(8,128)(2,1)}, u32[]{:S(2)}, u32[]{:S(2)}) collective-permute-start(bf16[768,1024]{1,0:T(8,128)(2,1)S(1)} %add_convert_fusion.7), channel_id=1, source_target_pairs={{8,16},{9,17},{10,18},{11,19},{12,20},{13,21},{14,22},{15,23},{16,... | collective-permute-start | bytes 4718600 | tf_op jit(solution)/shard_map/ppermute | solution.py:594
  496.3 52.7 %collective-permute-start.52 = (bf16[768,1536]{1,0:T(8,128)(2,1)S(1)}, bf16[768,1536]{1,0:T(8,128)(2,1)S(1)}, u32[]{:S(2)}, u32[]{:S(2)}) collective-permute-start(bf16[768,1536]{1,0:T(8,128)(2,1)S(1)} %get-tuple-element.419), channel_id=1, source_target_pairs={{0,2},{1,3},{2,0},{3,1},{4,5},{5,4},{6,7},{7,6},{8,10},{9,11},{10,... | collective-permute-start | bytes 7077896 | tf_op jit(solution)/shard_map/ppermute | solution.py:576
  497.4 51.5 %collective-permute-start.53 = (bf16[384,768]{1,0:T(8,128)(2,1)}, bf16[384,768]{1,0:T(8,128)(2,1)S(1)}, u32[]{:S(2)}, u32[]{:S(2)}) collective-permute-start(bf16[384,768]{1,0:T(8,128)(2,1)} %add_convert_fusion.30), channel_id=1, source_target_pairs={{0,8},{1,9},{2,10},{3,11},{4,12},{5,13},{6,14},{7,15},{24,16},{25,... | collective-permute-start | bytes 1769480 | tf_op jit(solution)/shard_map/ppermute | solution.py:591
  529.1 39.2 %collective-permute-start.57 = (bf16[768,1024]{1,0:T(8,128)(2,1)S(1)}, bf16[768,1024]{1,0:T(8,128)(2,1)S(1)}, u32[]{:S(2)}, u32[]{:S(2)}) collective-permute-start(bf16[768,1024]{1,0:T(8,128)(2,1)S(1)} %add_convert_fusion.6), channel_id=1, source_target_pairs={{8,0},{9,1},{10,2},{11,3},{12,4},{13,5},{14,6},{15,7},{16,24},{17,... | collective-permute-start | bytes 4718600 | tf_op jit(solution)/shard_map/ppermute | solution.py:597
  538.9 30.1 %collective-permute-start.54 = (bf16[384,1536]{1,0:T(8,128)(2,1)S(1)}, bf16[384,1536]{1,0:T(8,128)(2,1)S(1)}, u32[]{:S(2)}, u32[]{:S(2)}) collective-permute-start(bf16[384,1536]{1,0:T(8,128)(2,1)S(1)} %add_convert_fusion.16), channel_id=1, source_target_pairs={{0,8},{1,9},{2,10},{3,11},{4,12},{5,13},{6,14},{7,15},{24,16},{25,... | collective-permute-start | bytes 3538952 | tf_op jit(solution)/shard_map/ppermute | solution.py:591
  545.7 53.8 %collective-permute-start.58 = (bf16[768,1024]{1,0:T(8,128)(2,1)S(1)}, bf16[768,1024]{1,0:T(8,128)(2,1)S(1)}, u32[]{:S(2)}, u32[]{:S(2)}) collective-permute-start(bf16[768,1024]{1,0:T(8,128)(2,1)S(1)} %add_convert_fusion.5), channel_id=1, source_target_pairs={{8,0},{9,1},{10,2},{11,3},{12,4},{13,5},{14,6},{15,7},{16,24},{17,... | collective-permute-start | bytes 4718600 | tf_op jit(solution)/shard_map/ppermute | solution.py:597
  569.3 30.3 %collective-permute-start.59 = (bf16[384,1536]{1,0:T(8,128)(2,1)S(1)}, bf16[384,1536]{1,0:T(8,128)(2,1)S(1)}, u32[]{:S(2)}, u32[]{:S(2)}) collective-permute-start(bf16[384,1536]{1,0:T(8,128)(2,1)S(1)} %add_convert_fusion.14), channel_id=1, source_target_pairs={{8,16},{9,17},{10,18},{11,19},{12,20},{13,21},{14,22},{15,23},{16,... | collective-permute-start | bytes 3538952 | tf_op jit(solution)/shard_map/ppermute | solution.py:594
  570.6 28.9 %collective-permute-start.63 = (bf16[192,1536]{1,0:T(8,128)(2,1)S(1)}, bf16[192,1536]{1,0:T(8,128)(2,1)S(1)}, u32[]{:S(2)}, u32[]{:S(2)}) collective-permute-start(bf16[192,1536]{1,0:T(8,128)(2,1)S(1)} %get-tuple-element.509), channel_id=1, source_target_pairs={{0,8},{1,9},{2,10},{3,11},{4,12},{5,13},{6,14},{7,15},{24,16},{25,... | collective-permute-start | bytes 1769480 | tf_op jit(solution)/shard_map/ppermute | solution.py:591
  609.0 71.4 %collective-permute-start.70 = (bf16[384,1536]{1,0:T(8,128)(2,1)S(1)}, bf16[384,1536]{1,0:T(8,128)(2,1)S(1)}, u32[]{:S(2)}, u32[]{:S(2)}) collective-permute-start(bf16[384,1536]{1,0:T(8,128)(2,1)S(1)} %add_convert_fusion.12), channel_id=1, source_target_pairs={{8,0},{9,1},{10,2},{11,3},{12,4},{13,5},{14,6},{15,7},{16,24},{17,... | collective-permute-start | bytes 3538952 | tf_op jit(solution)/shard_map/ppermute | solution.py:597
  617.9 37.8 %collective-permute-start.71 = (bf16[384,768]{1,0:T(8,128)(2,1)S(1)}, bf16[384,768]{1,0:T(8,128)(2,1)S(1)}, u32[]{:S(2)}, u32[]{:S(2)}) collective-permute-start(bf16[384,768]{1,0:T(8,128)(2,1)S(1)} %add_convert_fusion.26), channel_id=1, source_target_pairs={{8,0},{9,1},{10,2},{11,3},{12,4},{13,5},{14,6},{15,7},{16,24},{17,... | collective-permute-start | bytes 1769480 | tf_op jit(solution)/shard_map/ppermute | solution.py:597
  619.2 37.8 %collective-permute-start.79 = (bf16[384,1024]{1,0:T(8,128)(2,1)S(1)}, bf16[384,1024]{1,0:T(8,128)(2,1)S(1)}, u32[]{:S(2)}, u32[]{:S(2)}) collective-permute-start(bf16[384,1024]{1,0:T(8,128)(2,1)S(1)} %get-tuple-element.453), channel_id=1, source_target_pairs={{0,1},{1,0},{2,3},{3,2},{4,6},{5,7},{6,4},{7,5},{8,9},{9,8},{10,11... | collective-permute-start | bytes 2359304 | tf_op jit(solution)/shard_map/ppermute | solution.py:573
  620.9 41.6 %collective-permute-start.80 = (bf16[384,1024]{1,0:T(8,128)(2,1)S(1)}, bf16[384,1024]{1,0:T(8,128)(2,1)S(1)}, u32[]{:S(2)}, u32[]{:S(2)}) collective-permute-start(bf16[384,1024]{1,0:T(8,128)(2,1)S(1)} %get-tuple-element.450), channel_id=1, source_target_pairs={{0,2},{1,3},{2,0},{3,1},{4,5},{5,4},{6,7},{7,6},{8,10},{9,11},{10,... | collective-permute-start | bytes 2359304 | tf_op jit(solution)/shard_map/ppermute | solution.py:576
  621.8 58.5 %collective-permute-start.69 = (bf16[384,1024]{1,0:T(8,128)(2,1)S(1)}, bf16[384,1024]{1,0:T(8,128)(2,1)S(1)}, u32[]{:S(2)}, u32[]{:S(2)}) collective-permute-start(bf16[384,1024]{1,0:T(8,128)(2,1)S(1)} %collective-permute-done.65), channel_id=1, source_target_pairs={{0,2},{1,3},{2,0},{3,1},{4,5},{5,4},{6,7},{7,6},{8,10},{9,11},{10,... | collective-permute-start | bytes 2359304 | tf_op jit(solution)/shard_map/ppermute | solution.py:576
  (129 other events, 1365.6 us)

commit v4 on v3

--- a/solution.py
+++ b/solution.py
@@ -895,7 +895,9 @@
     for i in (0, 2):
         grad_normed = grad_normed + mm_nt(late[i], jnp.concatenate(pieces[i], axis=0))
 
-    last0, grad_normed, down_out, feed1_across = tie(last0, grad_normed, down_out, feed1_across)
+    last0, grad_normed, down_out, feed1_across, feed0_out = tie(
+        last0, grad_normed, down_out, feed1_across, feed0_out
+    )
     feed1 = wide_sum(feed1, feed1_across).astype(HALF)
     feed1_out = links.outward(feed1)
     out_in = links.inward(out_sum)
@@ -921,9 +923,7 @@
     norm_grad = unit_back(grad_normed, unit_in, inverse_in, gain_first)
     grad_tokens = turn_back(turn, grad_middle + from_order(norm_grad, 1))
 
-    grad_tokens, sum0_in, extra_got, last1, feed0_out = tie(
-        grad_tokens, sum0_in, extra_got, last1, feed0_out
-    )
+    grad_tokens, sum0_in, extra_got, last1 = tie(grad_tokens, sum0_in, extra_got, last1)
     sum0 = wide_sum(sum0, sum0_in).astype(HALF)
     sum0_across = links.across(sum0)
     sum1 = wide_sum(sum1, last1).astype(HALF)
@@ -934,21 +934,19 @@
     grad_down = links.by_core(down_sum, down_twin, 0).astype(SINGLE)
     feed0 = links.settled(feed0, feed0_out)
 
-    feed1_out, sum0_across, out_across, extra_part, grad_down, feed0, *sum1_in = tie(
-        feed1_out, sum0_across, out_across, extra_part, grad_down, feed0, *sum1_in
-    )
-    sum0 = wide_sum(sum0, sum0_across).astype(HALF)
-    sum0_out = links.outward(sum0)
+    sum0_across, out_across, grad_down, extra_part = tie(sum0_across, out_across, grad_down, extra_part)
+    extra_own, extra_first = second_sum(extra_head, extra_part)
+    extra_last = links.near(extra_first)
+    both0 = jnp.concatenate([wide_sum(sum0, sum0_across), wide_sum(out_sum, out_across)], axis=1).astype(HALF)
+    both0_out = links.outward(both0)
+
+    feed1_out, feed0, both0, extra_first, *sum1_in = tie(feed1_out, feed0, both0, extra_first, *sum1_in)
     sum1 = [wide_sum(a, b).astype(HALF) for a, b in zip(sum1, sum1_in)]
     sum1_across = [links.across(a) for a in sum1]
-    out_sum = wide_sum(out_sum, out_across).astype(HALF)
-    out_out = links.outward(out_sum)
     feed_sum = jnp.concatenate([feed0, links.settled(feed1, feed1_out)], axis=0)
     feed_blocks = [cut(feed_sum, i * part, part, 0) for i in links.order]
     feed_passing, feed_near = links.near(feed_blocks[3]), links.near(feed_blocks[1])
     feed_next = links.next(feed_blocks[2])
-    extra_own, extra_first = second_sum(extra_head, extra_part)
-    extra_last = links.near(extra_first)
 
     feed_passing, extra_last, *sum1_across = tie(feed_passing, extra_last, *sum1_across)
     feed_last = links.next(feed_passing)
@@ -957,13 +955,12 @@
     extra_sum = wide_sum(extra_own, extra_last).astype(HALF)
     extra_level = links.level(extra_sum)
 
-    feed_last, sum0_out, out_out, extra_level, *sum1_out = tie(
-        feed_last, sum0_out, out_out, extra_level, *sum1_out
-    )
-    out_sum = links.settled(out_sum, out_out)
-    out_twin = links.twin(out_sum)
-    sum0 = links.settled(sum0, sum0_out)
-    twin0 = links.twin(sum0)
+    feed_last, both0_out, extra_level, *sum1_out = tie(feed_last, both0_out, extra_level, *sum1_out)
+    both0 = links.settled(both0, both0_out)
+    both_twin = links.twin(both0)
+    sum0, out_sum = both0[:, : 4 * wide], both0[:, 4 * wide :]
+    twin0, out_twin = both_twin[:, : 4 * wide], both_twin[:, 4 * wide :]
+
     extra_sum = wide_sum(extra_sum, extra_level).astype(HALF)
     extra_pair = links.pair(extra_sum)
     grad_wout = links.by_core(out_sum, out_twin, 1).astype(SINGLE)

time: 718 us -> 721 us (level)
    ppermute x7 -> x6, waiting for transfers between devices: 61 us -> 1.95 us  [outward(): return lax.ppermute(array, AXES, self.pairs['outward'])]
    ppermute x7, waiting for transfers between devices: 0.11 us -> 29.3 us  [inward(): return lax.ppermute(array, AXES, self.pairs['inward'])]
    ppermute x1, waiting for transfers between devices: 15 us -> 33 us  [level(): return lax.ppermute(array, AXES, self.pairs['level'])]
    ppermute x16, waiting for transfers between devices: 60.5 us -> 76.4 us  [near(): return lax.ppermute(array, AXES, self.pairs['near'])]
    unnamed x196 -> x200, local copies, waits for them, and re-layouts: 19.1 us -> 20.7 us
  transfers between devices with their start and end apart: 82 -> 80, of which waited for: 19 -> 20; matrix products, arithmetic and copies ran while one was open for 31% -> 30% of each run, Pallas kernels for 22% -> 22%
where the time goes in v4:
time: 721 us; the launch traced here: 709 us
  waiting for transfers between devices  179 us (25%)
  Pallas kernels  168 us (23%)
  starting transfers between devices  101 us (14%)
  other arithmetic  97 us (13%)
  matrix products  85.2 us (12%)
  local copies, waits for them, and re-layouts  76.4 us (11%)
    ppermute x16, waiting for transfers between devices, near(): return lax.ppermute(array, AXES, self.pairs['near'])  76.4 us
    pallas_call x4, Pallas kernels, attn_forward(): pl.pallas_call(functools.partial(attn_forward_kernel, span, dim, count, t...  57.5 us
    dot_general x10, matrix products, mm_tn(): lax.dot_general(left, right, (((0,), (0,)), ((), ())), preferred_element_...  52.8 us
    pallas_call x4, Pallas kernels, attn_backward(): pl.pallas_call(functools.partial(attn_backward_kernel, span, dim, count,...  42.7 us
    ppermute x7, starting transfers between devices, inward(): return lax.ppermute(array, AXES, self.pairs['inward'])  34.9 us
    ppermute x1, waiting for transfers between devices, level(): return lax.ppermute(array, AXES, self.pairs['level'])  33 us
    ppermute x21, waiting for transfers between devices, next(): return lax.ppermute(array, AXES, self.pairs['next'])  32.7 us
    ppermute x7, waiting for transfers between devices, inward(): return lax.ppermute(array, AXES, self.pairs['inward'])  29.3 us
  transfers between devices with their start and end apart: 80, of which 20 were waited for; matrix products, arithmetic and copies ran while one was open for 30% of the time, Pallas kernels for 22%

profile of v4, /device:TPU:0, one launch (start us, length us, event | category | flops | bytes accessed | tf_op | source)
XLA Modules:
  0.0 709.1 jit_solution(1242130367638931030)
XLA Ops:
  58.5 6.0 collective-permute-done.5.refs_4_
  65.1 14.4 %attend.4 = (bf16[384,384]{1,0:T(8,128)(2,1)}, bf16[384,1152]{1,0:T(8,128)(2,1)}, f32[384,384]{1,0:T(8,128)}, bf16[384,384]{1,0:T(8,128)(2,1)}, bf16[6,192,192]{...) custom-call(bf16[384,1536]{1,0:T(8,128)(2,1)} %copy-done.4, ...), custom_call_target="tpu_custom_call" | custom-call | flops 16000000000 | bytes 12000000 | tf_op jit(solution)/shard_map/attend/pallas_call | solution.py:196
  79.5 10.9 %collective-permute-done.6.refs_2_ = bf16[384,1536]{1,0:T(8,128)(2,1)} collective-permute-done((bf16[384,1536]{1,0:T(8,128)(2,1)S(1)}, bf16[384,1536]{1,0:T(8,128)(2,1)}, u32[]{:S(2)}, u32[]{:S(2)}) %collective-permute-start.6) | collective-permute-done | bytes 1179680 | tf_op jit(solution)/shard_map/ppermute | solution.py:573
  92.4 14.1 %attend.5 = (bf16[384,384]{1,0:T(8,128)(2,1)}, bf16[384,1152]{1,0:T(8,128)(2,1)}, f32[384,384]{1,0:T(8,128)}, bf16[384,384]{1,0:T(8,128)(2,1)}, bf16[6,192,192]{...) custom-call(bf16[384,1536]{1,0:T(8,128)(2,1)} %copy-done.4, ...), custom_call_target="tpu_custom_call" | custom-call | flops 16000000000 | bytes 12000000 | tf_op jit(solution)/shard_map/attend/pallas_call | solution.py:196
  108.9 14.4 %attend.6 = (bf16[384,384]{1,0:T(8,128)(2,1)}, bf16[384,1152]{1,0:T(8,128)(2,1)}, f32[384,384]{1,0:T(8,128)}, bf16[384,384]{1,0:T(8,128)(2,1)}, bf16[6,192,192]{...) custom-call(bf16[384,1536]{1,0:T(8,128)(2,1)} %copy-done.4, ...), custom_call_target="tpu_custom_call" | custom-call | flops 16000000000 | bytes 12000000 | tf_op jit(solution)/shard_map/attend/pallas_call | solution.py:196
  127.8 11.6 %collective-permute-done.17.refs_10_.refs_9_ = bf16[384,768]{1,0:T(8,128)(2,1)} collective-permute-done((bf16[384,768]{1,0:T(8,128)(2,1)}, bf16[384,768]{1,0:T(8,128)(2,1)}, u32[]{:S(2)}, u32[]{:S(2)}) %collective-permute-start.17) | collective-permute-done | bytes 589856 | tf_op jit(solution)/shard_map/ppermute | solution.py:576
  139.4 14.5 %attend.7 = (bf16[384,384]{1,0:T(8,128)(2,1)}, bf16[384,1152]{1,0:T(8,128)(2,1)}, f32[384,384]{1,0:T(8,128)}, bf16[384,384]{1,0:T(8,128)(2,1)}, bf16[6,192,192]{...) custom-call(bf16[384,1536]{1,0:T(8,128)(2,1)} %copy-done.4, ...), custom_call_target="tpu_custom_call" | custom-call | flops 16000000000 | bytes 12000000 | tf_op jit(solution)/shard_map/attend/pallas_call | solution.py:196
  154.0 12.9 %collective-permute-done.18 = bf16[384,1024]{1,0:T(8,128)(2,1)} collective-permute-done((bf16[384,1024]{1,0:T(8,128)(2,1)}, bf16[384,1024]{1,0:T(8,128)(2,1)}, u32[]{:S(2)}, u32[]{:S(2)}) %collective-permute-start.18) | collective-permute-done | bytes 786464 | tf_op jit(solution)/shard_map/ppermute | solution.py:573
  171.3 8.3 %leave_attention.1 = (bf16[384,1536]{1,0:T(8,128)(2,1)}, f32[384,1536]{1,0:T(8,128)}, bf16[384,1536]{1,0:T(8,128)(2,1)}) custom-call(s32[9]{0:T(128)} %stack.46.refs_0_, f32[384,1536]{1,0:T(8,128)} %copy-done.7, f32[1,1536]{1,0:T(1,128)} %fusion.110.refs_2_.refs_5_, bf16[384,384]{1,0:T(8,128)(2,1)} %get-tuple-element.218.refs_3_, ...), custom_call_target="tpu_custom_call" | custom-call | flops 6000000000 | bytes 14000000 | tf_op jit(solution)/shard_map/leave_attention/pallas_call | solution.py:260
  179.6 8.5 %collective-permute-done.22 = bf16[384,1024]{1,0:T(8,128)(2,1)} collective-permute-done((bf16[384,1024]{1,0:T(8,128)(2,1)}, bf16[384,1024]{1,0:T(8,128)(2,1)}, u32[]{:S(2)}, u32[]{:S(2)}) %collective-permute-start.22) | collective-permute-done | bytes 786464 | tf_op jit(solution)/shard_map/ppermute | solution.py:573
  197.2 20.0 %collective-permute-done.26 = bf16[384,1536]{1,0:T(8,128)(2,1)} collective-permute-done((bf16[384,1536]{1,0:T(8,128)(2,1)}, bf16[384,1536]{1,0:T(8,128)(2,1)}, u32[]{:S(2)}, u32[]{:S(2)}) %collective-permute-start.26) | collective-permute-done | bytes 1179680 | tf_op jit(solution)/shard_map/ppermute | solution.py:573
  220.1 4.2 collective-permute-done.28
  235.7 7.0 collective-permute-done.30
  247.0 20.7 %feed_forward.1 = (f32[1536,2048]{1,0:T(8,128)}, bf16[1536,1024]{1,0:T(8,128)(2,1)}, bf16[1536,1536]{1,0:T(8,128)(2,1)}) custom-call(bf16[1536,1536]{1,0:T(8,128)(2,1)} %constant_dynamic-update-slice_fusion.rows_ref, bf16[1536,2048]{1,0:T(8,128)(2,1)} %pad_maximum_fusion.feed_ref.refs_2_, bf16[1024,1536]{1,0:T(8,128)(2,1)} %pad_maximum_fusion.1.down_ref.refs_3_), custom_call_target="tpu_custom_call" | custom-call | flops 17999998976 | bytes 30000000 | tf_op jit(solution)/shard_map/feed_forward/pallas_call | solution.py:330
  270.1 14.3 %feed_backward.2 = (bf16[1536,2048]{1,0:T(8,128)(2,1)}, bf16[768,1536]{1,0:T(8,128)(2,1)}) custom-call(bf16[1536,1536]{1,0:T(8,128)(2,1)} %constant_dynamic-update-slice_fusion.4.refs_0_, f32[1536,2048]{1,0:T(8,128)} %get-tuple-element.274.refs_1_, bf16[1536,2048]{1,0:T(8,128)(2,1)} %pad_maximum_fusion.feed_ref.refs_2_, ...), custom_call_target="tpu_custom_call" | custom-call | flops 8999999488 | bytes 25000000 | tf_op jit(solution)/shard_map/feed_backward/pallas_call | solution.py:365
  285.5 8.1 %convolution_convert_fusion.6 = bf16[1024,1536]{1,0:T(8,128)(2,1)S(1)} fusion(bf16[1536,1024]{1,0:T(8,128)(2,1)} %get-tuple-element.279, bf16[1536,1536]{1,0:T(8,128)(2,1)} %constant_dynamic-update-slice_fusion.4.refs_0_), kind=kOutput, calls=%fused_computation.58 | convolution fusion | flops 4833411072 | bytes 11010048 | tf_op jit(solution)/shard_map/dot_general | solution.py:23
  295.6 14.4 %feed_backward.3 = (bf16[1536,2048]{1,0:T(8,128)(2,1)}, bf16[768,1536]{1,0:T(8,128)(2,1)}) custom-call(bf16[1536,1536]{1,0:T(8,128)(2,1)} %constant_dynamic-update-slice_fusion.4.refs_0_, f32[1536,2048]{1,0:T(8,128)} %get-tuple-element.274.refs_1_, bf16[1536,2048]{1,0:T(8,128)(2,1)} %pad_maximum_fusion.feed_ref.refs_2_, ...), custom_call_target="tpu_custom_call", output_to_operand_aliasing={{0}: (4, {})} | custom-call | flops 8999999488 | bytes 25000000 | tf_op jit(solution)/shard_map/feed_backward/pallas_call | solution.py:365
  310.1 3.4 collective-permute-done.32
  313.5 3.8 convert_add_fusion
  318.9 13.5 %convolution_convert_fusion.5 = bf16[1536,2048]{1,0:T(8,128)(2,1)S(1)} fusion(bf16[1536,1536]{1,0:T(8,128)(2,1)} %constant_dynamic-update-slice_fusion.rows_ref, bf16[1536,2048]{1,0:T(8,128)(2,1)} %get-tuple-element.289), kind=kOutput, calls=%fused_computation.5 | convolution fusion | flops 9666822144 | bytes 17301504 | tf_op jit(solution)/shard_map/dot_general | solution.py:23
  340.9 5.2 collective-permute-start.37
  348.7 9.7 %return_to_attention.1 = (f32[384,1536]{1,0:T(8,128)}, bf16[384,1536]{1,0:T(8,128)(2,1)}, f32[1,1536]{1,0:T(1,128)}, bf16[4,384,384]{2,1,0:T(8,128)(2,1)}) custom-call(s32[9]{0:T(128)} %stack.46.refs_0_, f32[384,1536]{1,0:T(8,128)} %get-tuple-element.296.refs_1_, bf16[384,1536]{1,0:T(8,128)(2,1)} %copy-done.89, bf16[384,1536]{1,0:T(8,128)(2,1)} %copy-done.14, ...), custom_call_target="tpu_custom_call" | custom-call | flops 6000000000 | bytes 14000000 | tf_op jit(solution)/shard_map/return_to_attention/pallas_call | solution.py:301
  358.4 4.3 convolution_convert_fusion.4
  370.1 11.3 %attend_back.4 = (bf16[384,1536]{1,0:T(8,128)(2,1)}, f32[3,384]{1,0:T(4,128)}, f32[4,384]{1,0:T(4,128)}) custom-call(bf16[384,1152]{1,0:T(8,128)(2,1)} %get-tuple-element.292.qkv_ref, bf16[384,384]{1,0:T(8,128)(2,1)} %get-tuple-element.293.w_ref, f32[384,384]{1,0:T(8,128)} %get-tuple-element.294.raw_ref, f32[3,384]{1,0:T(4,128)} %get-tuple-element.226.refs_5_.rate_ref, ...), custom_call_target="tpu_custom_call" | custom-call | flops 12000000000 | bytes 8000000 | tf_op jit(solution)/shard_map/attend_back/pallas_call | solution.py:217
  381.4 5.5 convolution_convert_fusion.3
  388.9 3.6 add_convert_fusion.20
  396.0 3.5 add_convert_fusion.10
  405.7 10.5 %attend_back.5 = (bf16[384,1536]{1,0:T(8,128)(2,1)}, f32[3,384]{1,0:T(4,128)}, f32[4,384]{1,0:T(4,128)}) custom-call(bf16[384,1152]{1,0:T(8,128)(2,1)} %get-tuple-element.313.qkv_ref, bf16[384,384]{1,0:T(8,128)(2,1)} %get-tuple-element.314.w_ref, f32[384,384]{1,0:T(8,128)} %get-tuple-element.315.raw_ref, f32[3,384]{1,0:T(4,128)} %get-tuple-element.216.refs_5_.rate_ref, ...), custom_call_target="tpu_custom_call" | custom-call | flops 12000000000 | bytes 8000000 | tf_op jit(solution)/shard_map/attend_back/pallas_call | solution.py:217
  416.1 5.6 convolution_convert_fusion.2
  426.3 10.5 %attend_back.6 = (bf16[384,1536]{1,0:T(8,128)(2,1)}, f32[3,384]{1,0:T(4,128)}, f32[4,384]{1,0:T(4,128)}) custom-call(bf16[384,1152]{1,0:T(8,128)(2,1)} %get-tuple-element.310.qkv_ref, bf16[384,384]{1,0:T(8,128)(2,1)} %get-tuple-element.311.w_ref, f32[384,384]{1,0:T(8,128)} %get-tuple-element.312.raw_ref, f32[3,384]{1,0:T(4,128)} %get-tuple-element.242.refs_5_.rate_ref, ...), custom_call_target="tpu_custom_call" | custom-call | flops 12000000000 | bytes 8000000 | tf_op jit(solution)/shard_map/attend_back/pallas_call | solution.py:217
  436.7 5.5 convolution_convert_fusion.1
  454.7 3.4 add_convert_fusion.8
  459.8 10.5 %attend_back.7 = (bf16[384,1536]{1,0:T(8,128)(2,1)}, f32[3,384]{1,0:T(4,128)}, f32[4,384]{1,0:T(4,128)}) custom-call(bf16[384,1152]{1,0:T(8,128)(2,1)} %get-tuple-element.335.qkv_ref, bf16[384,384]{1,0:T(8,128)(2,1)} %get-tuple-element.336.w_ref, f32[384,384]{1,0:T(8,128)} %get-tuple-element.337.raw_ref, f32[3,384]{1,0:T(4,128)} %get-tuple-element.233.refs_5_.rate_ref, ...), custom_call_target="tpu_custom_call" | custom-call | flops 12000000000 | bytes 8000000 | tf_op jit(solution)/shard_map/attend_back/pallas_call | solution.py:217
  494.3 10.9 %fusion.42 = f32[384,1536]{1,0:T(8,128)} fusion(f32[384,1536]{1,0:T(8,128)S(1)} %fusion.148, bf16[384,1536]{1,0:T(8,128)(2,1)S(1)} %copy-done.93, bf16[384,1536]{1,0:T(8,128)(2,1)} %collective-permute-done.5.refs_4_, bf16[384,1536]{1,0:T(8,128)(2,1)} %collective-permute-done.1.refs_3_, bf16[384,1536]{1,0:T(8,128)(2,1)} %collective-permute-done.refs_2_, ...), kind=kOutput, calls=%fused_computation.76 | convolution fusion | flops 1845559296 | bytes 10616832 | tf_op jit(solution)/shard_map/dot_general | solution.py:19
  505.2 5.6 fusion.22
  510.9 6.4 fusion.39
  517.2 14.8 %collective-permute-start.54 = (bf16[384,768]{1,0:T(8,128)(2,1)S(1)}, bf16[384,768]{1,0:T(8,128)(2,1)S(1)}, u32[]{:S(2)}, u32[]{:S(2)}) collective-permute-start(bf16[384,768]{1,0:T(8,128)(2,1)S(1)} %add_convert_fusion.30), channel_id=1, source_target_pairs={{0,8},{1,9},{2,10},{3,11},{4,12},{5,13},{6,14},{7,15},{24,16},{25,... | collective-permute-start | bytes 1769480 | tf_op jit(solution)/shard_map/ppermute | solution.py:591
  535.0 5.4 multiply_reduce_fusion.1
  560.4 8.5 %collective-permute-done.55 = bf16[384,1536]{1,0:T(8,128)(2,1)S(1)} collective-permute-done((bf16[384,1536]{1,0:T(8,128)(2,1)S(1)}, bf16[384,1536]{1,0:T(8,128)(2,1)S(1)}, u32[]{:S(2)}, u32[]{:S(2)}) %collective-permute-start.55) | collective-permute-done | bytes 1179680 | tf_op jit(solution)/shard_map/ppermute | solution.py:591
  571.6 7.2 %collective-permute-start.63 = (bf16[192,1536]{1,0:T(8,128)(2,1)S(1)}, bf16[192,1536]{1,0:T(8,128)(2,1)S(1)}, u32[]{:S(2)}, u32[]{:S(2)}) collective-permute-start(bf16[192,1536]{1,0:T(8,128)(2,1)S(1)} %get-tuple-element.509), channel_id=1, source_target_pairs={{0,8},{1,9},{2,10},{3,11},{4,12},{5,13},{6,14},{7,15},{24,16},{25,... | collective-permute-start | bytes 1769480 | tf_op jit(solution)/shard_map/ppermute | solution.py:591
  581.9 10.6 %collective-permute-done.63 = bf16[192,1536]{1,0:T(8,128)(2,1)S(1)} collective-permute-done((bf16[192,1536]{1,0:T(8,128)(2,1)S(1)}, bf16[192,1536]{1,0:T(8,128)(2,1)S(1)}, u32[]{:S(2)}, u32[]{:S(2)}) %collective-permute-start.63) | collective-permute-done | bytes 589856 | tf_op jit(solution)/shard_map/ppermute | solution.py:591
  592.5 10.1 %collective-permute-done.64 = bf16[192,1536]{1,0:T(8,128)(2,1)S(1)} collective-permute-done((bf16[192,1536]{1,0:T(8,128)(2,1)S(1)}, bf16[192,1536]{1,0:T(8,128)(2,1)S(1)}, u32[]{:S(2)}, u32[]{:S(2)}) %collective-permute-start.64) | collective-permute-done | bytes 589856 | tf_op jit(solution)/shard_map/ppermute | solution.py:591
  603.2 4.5 fusion.60
  613.3 7.7 %collective-permute-done.66 = bf16[384,128]{0,1:T(8,128)(2,1)S(1)} collective-permute-done((bf16[384,128]{0,1:T(8,128)(2,1)S(1)}, bf16[384,128]{0,1:T(8,128)(2,1)S(1)}, u32[]{:S(2)}, u32[]{:S(2)}) %collective-permute-start.66) | collective-permute-done | bytes 98336 | tf_op jit(solution)/shard_map/ppermute | solution.py:573
  626.3 15.2 %collective-permute-done.77 = bf16[384,1024]{1,0:T(8,128)(2,1)S(1)} collective-permute-done((bf16[384,1024]{1,0:T(8,128)(2,1)S(1)}, bf16[384,1024]{1,0:T(8,128)(2,1)S(1)}, u32[]{:S(2)}, u32[]{:S(2)}) %collective-permute-start.77) | collective-permute-done | bytes 786464 | tf_op jit(solution)/shard_map/ppermute | solution.py:573
  642.8 4.0 fusion.45
  649.8 33.0 %collective-permute-done.71 = bf16[384,128]{0,1:T(8,128)(2,1)S(1)} collective-permute-done((bf16[384,128]{0,1:T(8,128)(2,1)S(1)}, bf16[384,128]{0,1:T(8,128)(2,1)S(1)}, u32[]{:S(2)}, u32[]{:S(2)}) %collective-permute-start.71) | collective-permute-done | bytes 98336 | tf_op jit(solution)/shard_map/ppermute | solution.py:585
  686.2 5.2 collective-permute-done.74
  (501 shorter events, 242.6 us)
Async XLA Ops:
  8.2 39.7 %collective-permute-start = (bf16[384,1536]{1,0:T(8,128)(2,1)}, bf16[384,1536]{1,0:T(8,128)(2,1)}, u32[]{:S(2)}, u32[]{:S(2)}) collective-permute-start(bf16[384,1536]{1,0:T(8,128)(2,1)} %pad_maximum_fusion.6.refs_1_), channel_id=1, source_target_pairs={{0,1},{1,0},{2,3},{3,2},{4,6},{5,7},{6,4},{7,5},{8,9},{9,8},{10,11... | collective-permute-start | bytes 3538952 | tf_op jit(solution)/shard_map/ppermute | solution.py:573
  11.1 36.8 %collective-permute-start.1 = (bf16[384,1536]{1,0:T(8,128)(2,1)}, bf16[384,1536]{1,0:T(8,128)(2,1)}, u32[]{:S(2)}, u32[]{:S(2)}) collective-permute-start(bf16[384,1536]{1,0:T(8,128)(2,1)} %pad_maximum_fusion.6.refs_1_), channel_id=1, source_target_pairs={{0,2},{1,3},{2,0},{3,1},{4,5},{5,4},{6,7},{7,6},{8,10},{9,11},{10,... | collective-permute-start | bytes 3538952 | tf_op jit(solution)/shard_map/ppermute | solution.py:576
  14.2 33.7 %collective-permute-start.2 = (bf16[384,128]{0,1:T(8,128)(2,1)}, bf16[384,128]{0,1:T(8,128)(2,1)}, u32[]{:S(2)}, u32[]{:S(2)}) collective-permute-start(bf16[384,128]{0,1:T(8,128)(2,1)} %get-tuple-element.524), channel_id=1, source_target_pairs={{0,1},{1,0},{2,3},{3,2},{4,6},{5,7},{6,4},{7,5},{8,9},{9,8},{10,11... | collective-permute-start | bytes 294920 | tf_op jit(solution)/shard_map/ppermute | solution.py:573
  14.7 33.2 %collective-permute-start.3 = (bf16[384,128]{0,1:T(8,128)(2,1)}, bf16[384,128]{0,1:T(8,128)(2,1)}, u32[]{:S(2)}, u32[]{:S(2)}) collective-permute-start(bf16[384,128]{0,1:T(8,128)(2,1)} %get-tuple-element.524), channel_id=1, source_target_pairs={{0,2},{1,3},{2,0},{3,1},{4,5},{5,4},{6,7},{7,6},{8,10},{9,11},{10,... | collective-permute-start | bytes 294920 | tf_op jit(solution)/shard_map/ppermute | solution.py:576
  14.8 33.1 %collective-permute-start.4 = (bf16[384,128]{0,1:T(8,128)(2,1)}, bf16[384,128]{0,1:T(8,128)(2,1)}, u32[]{:S(2)}, u32[]{:S(2)}) collective-permute-start(bf16[384,128]{0,1:T(8,128)(2,1)} %get-tuple-element.524), channel_id=1, source_target_pairs={{0,3},{1,2},{2,1},{3,0},{4,7},{5,6},{6,5},{7,4},{8,11},{9,10},{10,... | collective-permute-start | bytes 294920 | tf_op jit(solution)/shard_map/ppermute | solution.py:582
  48.5 31.0 %collective-permute-start.9 = (bf16[384,1536]{1,0:T(8,128)(2,1)}, bf16[384,1536]{1,0:T(8,128)(2,1)}, u32[]{:S(2)}, u32[]{:S(2)}) collective-permute-start(bf16[384,1536]{1,0:T(8,128)(2,1)} %collective-permute-done.refs_2_), channel_id=1, source_target_pairs={{0,4},{1,5},{2,6},{3,7},{4,0},{5,1},{6,2},{7,3},{8,12},{9,13},{10,... | collective-permute-start | bytes 3538952 | tf_op jit(solution)/shard_map/ppermute | solution.py:579
  54.5 25.0 %collective-permute-start.8 = (bf16[384,1536]{1,0:T(8,128)(2,1)}, bf16[384,1536]{1,0:T(8,128)(2,1)}, u32[]{:S(2)}, u32[]{:S(2)}) collective-permute-start(bf16[384,1536]{1,0:T(8,128)(2,1)} %collective-permute-done.1.refs_3_), channel_id=1, source_target_pairs={{0,4},{1,5},{2,6},{3,7},{4,0},{5,1},{6,2},{7,3},{8,12},{9,13},{10,... | collective-permute-start | bytes 3538952 | tf_op jit(solution)/shard_map/ppermute | solution.py:579
  64.5 25.9 %collective-permute-start.6 = (bf16[384,1536]{1,0:T(8,128)(2,1)S(1)}, bf16[384,1536]{1,0:T(8,128)(2,1)}, u32[]{:S(2)}, u32[]{:S(2)}) collective-permute-start(bf16[384,1536]{1,0:T(8,128)(2,1)S(1)} %pad_maximum_fusion.7.refs_1_), channel_id=1, source_target_pairs={{0,1},{1,0},{2,3},{3,2},{4,6},{5,7},{6,4},{7,5},{8,9},{9,8},{10,11... | collective-permute-start | bytes 3538952 | tf_op jit(solution)/shard_map/ppermute | solution.py:573
  65.0 25.4 %collective-permute-start.7 = (bf16[384,1536]{1,0:T(8,128)(2,1)S(1)}, bf16[384,1536]{1,0:T(8,128)(2,1)}, u32[]{:S(2)}, u32[]{:S(2)}) collective-permute-start(bf16[384,1536]{1,0:T(8,128)(2,1)S(1)} %pad_maximum_fusion.7.refs_1_), channel_id=1, source_target_pairs={{0,2},{1,3},{2,0},{3,1},{4,5},{5,4},{6,7},{7,6},{8,10},{9,11},{10,... | collective-permute-start | bytes 3538952 | tf_op jit(solution)/shard_map/ppermute | solution.py:576
  65.1 25.3 %collective-permute-start.10 = (bf16[384,1536]{1,0:T(8,128)(2,1)}, bf16[384,1536]{1,0:T(8,128)(2,1)}, u32[]{:S(2)}, u32[]{:S(2)}) collective-permute-start(bf16[384,1536]{1,0:T(8,128)(2,1)} %collective-permute-done.5.refs_4_), channel_id=1, source_target_pairs={{0,4},{1,5},{2,6},{3,7},{4,0},{5,1},{6,2},{7,3},{8,12},{9,13},{10,... | collective-permute-start | bytes 3538952 | tf_op jit(solution)/shard_map/ppermute | solution.py:579
  91.9 31.5 %collective-permute-start.15 = (bf16[384,1536]{1,0:T(8,128)(2,1)}, bf16[384,1536]{1,0:T(8,128)(2,1)S(1)}, u32[]{:S(2)}, u32[]{:S(2)}) collective-permute-start(bf16[384,1536]{1,0:T(8,128)(2,1)} %collective-permute-done.6.refs_2_), channel_id=1, source_target_pairs={{0,4},{1,5},{2,6},{3,7},{4,0},{5,1},{6,2},{7,3},{8,12},{9,13},{10,... | collective-permute-start | bytes 3538952 | tf_op jit(solution)/shard_map/ppermute | solution.py:579
  91.9 31.4 %collective-permute-start.14 = (bf16[384,1536]{1,0:T(8,128)(2,1)}, bf16[384,1536]{1,0:T(8,128)(2,1)}, u32[]{:S(2)}, u32[]{:S(2)}) collective-permute-start(bf16[384,1536]{1,0:T(8,128)(2,1)} %collective-permute-done.7.refs_3_), channel_id=1, source_target_pairs={{0,4},{1,5},{2,6},{3,7},{4,0},{5,1},{6,2},{7,3},{8,12},{9,13},{10,... | collective-permute-start | bytes 3538952 | tf_op jit(solution)/shard_map/ppermute | solution.py:579
  124.2 29.7 %collective-permute-start.20 = (bf16[384,768]{1,0:T(8,128)(2,1)}, bf16[384,768]{1,0:T(8,128)(2,1)}, u32[]{:S(2)}, u32[]{:S(2)}) collective-permute-start(bf16[384,768]{1,0:T(8,128)(2,1)} %collective-permute-done.12.refs_8_.refs_7_), channel_id=1, source_target_pairs={{0,4},{1,5},{2,6},{3,7},{4,0},{5,1},{6,2},{7,3},{8,12},{9,13},{10,... | collective-permute-start | bytes 1769480 | tf_op jit(solution)/shard_map/ppermute | solution.py:579
  125.2 62.9 %collective-permute-start.24 = (bf16[384,1536]{1,0:T(8,128)(2,1)S(1)}, bf16[384,1536]{1,0:T(8,128)(2,1)S(1)}, u32[]{:S(2)}, u32[]{:S(2)}) collective-permute-start(bf16[384,1536]{1,0:T(8,128)(2,1)S(1)} %convolution_convert_fusion.8.refs_3_), channel_id=1, source_target_pairs={{0,1},{1,0},{2,3},{3,2},{4,6},{5,7},{6,4},{7,5},{8,9},{9,8},{10,11... | collective-permute-start | bytes 3538952 | tf_op jit(solution)/shard_map/ppermute | solution.py:573
  126.2 61.9 %collective-permute-start.25 = (bf16[384,1536]{1,0:T(8,128)(2,1)S(1)}, bf16[384,1536]{1,0:T(8,128)(2,1)S(1)}, u32[]{:S(2)}, u32[]{:S(2)}) collective-permute-start(bf16[384,1536]{1,0:T(8,128)(2,1)S(1)} %convolution_convert_fusion.8.refs_3_), channel_id=1, source_target_pairs={{0,2},{1,3},{2,0},{3,1},{4,5},{5,4},{6,7},{7,6},{8,10},{9,11},{10,... | collective-permute-start | bytes 3538952 | tf_op jit(solution)/shard_map/ppermute | solution.py:576
  127.1 39.8 %collective-permute-start.18 = (bf16[384,1024]{1,0:T(8,128)(2,1)}, bf16[384,1024]{1,0:T(8,128)(2,1)}, u32[]{:S(2)}, u32[]{:S(2)}) collective-permute-start(bf16[384,1024]{1,0:T(8,128)(2,1)} %pad_maximum_fusion.12), channel_id=1, source_target_pairs={{0,1},{1,0},{2,3},{3,2},{4,6},{5,7},{6,4},{7,5},{8,9},{9,8},{10,11... | collective-permute-start | bytes 2359304 | tf_op jit(solution)/shard_map/ppermute | solution.py:573
  188.1 29.1 %collective-permute-start.26 = (bf16[384,1536]{1,0:T(8,128)(2,1)}, bf16[384,1536]{1,0:T(8,128)(2,1)}, u32[]{:S(2)}, u32[]{:S(2)}) collective-permute-start(bf16[384,1536]{1,0:T(8,128)(2,1)} %get-tuple-element.258), channel_id=1, source_target_pairs={{0,1},{1,0},{2,3},{3,2},{4,6},{5,7},{6,4},{7,5},{8,9},{9,8},{10,11... | collective-permute-start | bytes 3538952 | tf_op jit(solution)/shard_map/ppermute | solution.py:573
  189.7 27.5 %collective-permute-start.27 = (bf16[384,1536]{1,0:T(8,128)(2,1)}, bf16[384,1536]{1,0:T(8,128)(2,1)}, u32[]{:S(2)}, u32[]{:S(2)}) collective-permute-start(bf16[384,1536]{1,0:T(8,128)(2,1)} %get-tuple-element.258), channel_id=1, source_target_pairs={{0,2},{1,3},{2,0},{3,1},{4,5},{5,4},{6,7},{7,6},{8,10},{9,11},{10,... | collective-permute-start | bytes 3538952 | tf_op jit(solution)/shard_map/ppermute | solution.py:576
  193.7 30.6 %collective-permute-start.28 = (bf16[384,1024]{1,0:T(8,128)(2,1)}, bf16[384,1024]{1,0:T(8,128)(2,1)S(1)}, u32[]{:S(2)}, u32[]{:S(2)}) collective-permute-start(bf16[384,1024]{1,0:T(8,128)(2,1)} %collective-permute-done.18), channel_id=1, source_target_pairs={{0,2},{1,3},{2,0},{3,1},{4,5},{5,4},{6,7},{7,6},{8,10},{9,11},{10,... | collective-permute-start | bytes 2359304 | tf_op jit(solution)/shard_map/ppermute | solution.py:576
  242.7 25.0 %collective-permute-start.31 = (bf16[384,1536]{1,0:T(8,128)(2,1)S(1)}, bf16[384,1536]{1,0:T(8,128)(2,1)}, u32[]{:S(2)}, u32[]{:S(2)}) collective-permute-start(bf16[384,1536]{1,0:T(8,128)(2,1)S(1)} %collective-permute-done.24), channel_id=1, source_target_pairs={{0,2},{1,3},{2,0},{3,1},{4,5},{5,4},{6,7},{7,6},{8,10},{9,11},{10,... | collective-permute-start | bytes 3538952 | tf_op jit(solution)/shard_map/ppermute | solution.py:576
  284.4 29.1 %collective-permute-start.32 = (bf16[768,1536]{1,0:T(8,128)(2,1)}, bf16[768,1536]{1,0:T(8,128)(2,1)S(1)}, u32[]{:S(2)}, u32[]{:S(2)}) collective-permute-start(bf16[768,1536]{1,0:T(8,128)(2,1)} %get-tuple-element.278), channel_id=1, source_target_pairs={{0,2},{1,3},{2,0},{3,1},{4,5},{5,4},{6,7},{7,6},{8,10},{9,11},{10,... | collective-permute-start | bytes 7077896 | tf_op jit(solution)/shard_map/ppermute | solution.py:576
  337.0 25.7 %collective-permute-start.35 = (bf16[1536,1024]{1,0:T(8,128)(2,1)}, bf16[1536,1024]{1,0:T(8,128)(2,1)}, u32[]{:S(2)}, u32[]{:S(2)}) collective-permute-start(bf16[1536,1024]{1,0:T(8,128)(2,1)} %pad_maximum_fusion.2), channel_id=1, source_target_pairs={{0,4},{1,5},{2,6},{3,7},{4,0},{5,1},{6,2},{7,3},{8,12},{9,13},{10,... | collective-permute-start | bytes 9437192 | tf_op jit(solution)/shard_map/ppermute | solution.py:579
  340.9 46.0 %collective-permute-start.37 = (bf16[512,1536]{1,0:T(8,128)(2,1)}, bf16[512,1536]{1,0:T(8,128)(2,1)}, u32[]{:S(2)}, u32[]{:S(2)}) collective-permute-start(bf16[512,1536]{1,0:T(8,128)(2,1)} %add_convert_fusion.11), channel_id=1, source_target_pairs={{0,8},{1,9},{2,10},{3,11},{4,12},{5,13},{6,14},{7,15},{24,16},{25,... | collective-permute-start | bytes 4718600 | tf_op jit(solution)/shard_map/ppermute | solution.py:591
  347.6 39.3 %collective-permute-start.38 = (bf16[768,1536]{1,0:T(8,128)(2,1)}, bf16[768,1536]{1,0:T(8,128)(2,1)}, u32[]{:S(2)}, u32[]{:S(2)}) collective-permute-start(bf16[768,1536]{1,0:T(8,128)(2,1)} %slice.396), channel_id=1, source_target_pairs={{0,2},{1,3},{2,0},{3,1},{4,5},{5,4},{6,7},{7,6},{8,10},{9,11},{10,... | collective-permute-start | bytes 7077896 | tf_op jit(solution)/shard_map/ppermute | solution.py:576
  386.9 37.5 %collective-permute-start.39 = (bf16[1536,1536]{1,0:T(8,128)(2,1)}, bf16[1536,1536]{1,0:T(8,128)(2,1)}, u32[]{:S(2)}, u32[]{:S(2)}) collective-permute-start(bf16[1536,1536]{1,0:T(8,128)(2,1)} %convolution_convert_fusion.3), channel_id=1, source_target_pairs={{0,4},{1,5},{2,6},{3,7},{4,0},{5,1},{6,2},{7,3},{8,12},{9,13},{10,... | collective-permute-start | bytes 14155784 | tf_op jit(solution)/shard_map/ppermute | solution.py:579
  392.5 29.3 %collective-permute-start.40 = (bf16[768,768]{1,0:T(8,128)(2,1)}, bf16[768,768]{1,0:T(8,128)(2,1)}, u32[]{:S(2)}, u32[]{:S(2)}) collective-permute-start(bf16[768,768]{1,0:T(8,128)(2,1)} %get-tuple-element.431), channel_id=1, source_target_pairs={{0,2},{1,3},{2,0},{3,1},{4,5},{5,4},{6,7},{7,6},{8,10},{9,11},{10,... | collective-permute-start | bytes 3538952 | tf_op jit(solution)/shard_map/ppermute | solution.py:576
  393.5 48.8 %collective-permute-start.42 = (bf16[768,1024]{1,0:T(8,128)(2,1)S(1)}, bf16[768,1024]{1,0:T(8,128)(2,1)}, u32[]{:S(2)}, u32[]{:S(2)}) collective-permute-start(bf16[768,1024]{1,0:T(8,128)(2,1)S(1)} %get-tuple-element.329), channel_id=1, source_target_pairs={{0,8},{1,9},{2,10},{3,11},{4,12},{5,13},{6,14},{7,15},{24,16},{25,... | collective-permute-start | bytes 4718600 | tf_op jit(solution)/shard_map/ppermute | solution.py:591
  399.5 42.8 %collective-permute-start.43 = (bf16[512,1536]{1,0:T(8,128)(2,1)}, bf16[512,1536]{1,0:T(8,128)(2,1)}, u32[]{:S(2)}, u32[]{:S(2)}) collective-permute-start(bf16[512,1536]{1,0:T(8,128)(2,1)} %add_convert_fusion.10), channel_id=1, source_target_pairs={{8,16},{9,17},{10,18},{11,19},{12,20},{13,21},{14,22},{15,23},{16,... | collective-permute-start | bytes 4718600 | tf_op jit(solution)/shard_map/ppermute | solution.py:594
  404.2 38.1 %collective-permute-start.44 = (bf16[384,1536]{1,0:T(8,128)(2,1)}, bf16[384,1536]{1,0:T(8,128)(2,1)}, u32[]{:S(2)}, u32[]{:S(2)}) collective-permute-start(bf16[384,1536]{1,0:T(8,128)(2,1)} %add_convert_fusion.19), channel_id=1, source_target_pairs={{0,1},{1,0},{2,3},{3,2},{4,6},{5,7},{6,4},{7,5},{8,9},{9,8},{10,11... | collective-permute-start | bytes 3538952 | tf_op jit(solution)/shard_map/ppermute | solution.py:573
  421.8 56.8 %collective-permute-start.47 = (bf16[768,1024]{1,0:T(8,128)(2,1)}, bf16[768,1024]{1,0:T(8,128)(2,1)}, u32[]{:S(2)}, u32[]{:S(2)}) collective-permute-start(bf16[768,1024]{1,0:T(8,128)(2,1)} %get-tuple-element.345), channel_id=1, source_target_pairs={{0,8},{1,9},{2,10},{3,11},{4,12},{5,13},{6,14},{7,15},{24,16},{25,... | collective-permute-start | bytes 4718600 | tf_op jit(solution)/shard_map/ppermute | solution.py:591
  442.3 36.3 %collective-permute-start.45 = (bf16[1536,1536]{1,0:T(8,128)(2,1)}, bf16[1536,1536]{1,0:T(8,128)(2,1)}, u32[]{:S(2)}, u32[]{:S(2)}) collective-permute-start(bf16[1536,1536]{1,0:T(8,128)(2,1)} %convolution_convert_fusion.1), channel_id=1, source_target_pairs={{0,4},{1,5},{2,6},{3,7},{4,0},{5,1},{6,2},{7,3},{8,12},{9,13},{10,... | collective-permute-start | bytes 14155784 | tf_op jit(solution)/shard_map/ppermute | solution.py:579
  448.6 30.0 %collective-permute-start.46 = (bf16[768,1536]{1,0:T(8,128)(2,1)}, bf16[768,1536]{1,0:T(8,128)(2,1)}, u32[]{:S(2)}, u32[]{:S(2)}) collective-permute-start(bf16[768,1536]{1,0:T(8,128)(2,1)} %get-tuple-element.424), channel_id=1, source_target_pairs={{0,2},{1,3},{2,0},{3,1},{4,5},{5,4},{6,7},{7,6},{8,10},{9,11},{10,... | collective-permute-start | bytes 7077896 | tf_op jit(solution)/shard_map/ppermute | solution.py:576
  452.8 25.8 %collective-permute-start.48 = (bf16[768,1024]{1,0:T(8,128)(2,1)}, bf16[768,1024]{1,0:T(8,128)(2,1)}, u32[]{:S(2)}, u32[]{:S(2)}) collective-permute-start(bf16[768,1024]{1,0:T(8,128)(2,1)} %add_convert_fusion.9), channel_id=1, source_target_pairs={{8,16},{9,17},{10,18},{11,19},{12,20},{13,21},{14,22},{15,23},{16,... | collective-permute-start | bytes 4718600 | tf_op jit(solution)/shard_map/ppermute | solution.py:594
  458.1 59.2 %collective-permute-start.50 = (bf16[512,1536]{1,0:T(8,128)(2,1)}, bf16[512,1536]{1,0:T(8,128)(2,1)}, u32[]{:S(2)}, u32[]{:S(2)}) collective-permute-start(bf16[512,1536]{1,0:T(8,128)(2,1)} %add_convert_fusion.8), channel_id=1, source_target_pairs={{8,0},{9,1},{10,2},{11,3},{12,4},{13,5},{14,6},{15,7},{16,24},{17,... | collective-permute-start | bytes 4718600 | tf_op jit(solution)/shard_map/ppermute | solution.py:597
  480.2 51.9 %collective-permute-start.49 = (bf16[384,1536]{1,0:T(8,128)(2,1)S(1)}, bf16[384,1536]{1,0:T(8,128)(2,1)S(1)}, u32[]{:S(2)}, u32[]{:S(2)}) collective-permute-start(bf16[384,1536]{1,0:T(8,128)(2,1)S(1)} %add_convert_fusion.17), channel_id=1, source_target_pairs={{0,1},{1,0},{2,3},{3,2},{4,6},{5,7},{6,4},{7,5},{8,9},{9,8},{10,11... | collective-permute-start | bytes 3538952 | tf_op jit(solution)/shard_map/ppermute | solution.py:573
  484.3 47.7 %collective-permute-start.51 = (bf16[768,1024]{1,0:T(8,128)(2,1)S(1)}, bf16[768,1024]{1,0:T(8,128)(2,1)S(1)}, u32[]{:S(2)}, u32[]{:S(2)}) collective-permute-start(bf16[768,1024]{1,0:T(8,128)(2,1)S(1)} %add_convert_fusion.7), channel_id=1, source_target_pairs={{8,16},{9,17},{10,18},{11,19},{12,20},{13,21},{14,22},{15,23},{16,... | collective-permute-start | bytes 4718600 | tf_op jit(solution)/shard_map/ppermute | solution.py:594
  487.6 47.4 %collective-permute-start.52 = (bf16[768,1024]{1,0:T(8,128)(2,1)S(1)}, bf16[768,1024]{1,0:T(8,128)(2,1)}, u32[]{:S(2)}, u32[]{:S(2)}) collective-permute-start(bf16[768,1024]{1,0:T(8,128)(2,1)S(1)} %add_convert_fusion.6), channel_id=1, source_target_pairs={{8,0},{9,1},{10,2},{11,3},{12,4},{13,5},{14,6},{15,7},{16,24},{17,... | collective-permute-start | bytes 4718600 | tf_op jit(solution)/shard_map/ppermute | solution.py:597
  493.3 56.1 %collective-permute-start.53 = (bf16[768,1536]{1,0:T(8,128)(2,1)S(1)}, bf16[768,1536]{1,0:T(8,128)(2,1)S(1)}, u32[]{:S(2)}, u32[]{:S(2)}) collective-permute-start(bf16[768,1536]{1,0:T(8,128)(2,1)S(1)} %get-tuple-element.419), channel_id=1, source_target_pairs={{0,2},{1,3},{2,0},{3,1},{4,5},{5,4},{6,7},{7,6},{8,10},{9,11},{10,... | collective-permute-start | bytes 7077896 | tf_op jit(solution)/shard_map/ppermute | solution.py:576
  517.2 32.1 %collective-permute-start.54 = (bf16[384,768]{1,0:T(8,128)(2,1)S(1)}, bf16[384,768]{1,0:T(8,128)(2,1)S(1)}, u32[]{:S(2)}, u32[]{:S(2)}) collective-permute-start(bf16[384,768]{1,0:T(8,128)(2,1)S(1)} %add_convert_fusion.30), channel_id=1, source_target_pairs={{0,8},{1,9},{2,10},{3,11},{4,12},{5,13},{6,14},{7,15},{24,16},{25,... | collective-permute-start | bytes 1769480 | tf_op jit(solution)/shard_map/ppermute | solution.py:591
  542.3 26.6 %collective-permute-start.55 = (bf16[384,1536]{1,0:T(8,128)(2,1)S(1)}, bf16[384,1536]{1,0:T(8,128)(2,1)S(1)}, u32[]{:S(2)}, u32[]{:S(2)}) collective-permute-start(bf16[384,1536]{1,0:T(8,128)(2,1)S(1)} %add_convert_fusion.16), channel_id=1, source_target_pairs={{0,8},{1,9},{2,10},{3,11},{4,12},{5,13},{6,14},{7,15},{24,16},{25,... | collective-permute-start | bytes 3538952 | tf_op jit(solution)/shard_map/ppermute | solution.py:591
  544.5 37.4 %collective-permute-start.62 = (bf16[768,1024]{1,0:T(8,128)(2,1)S(1)}, bf16[768,1024]{1,0:T(8,128)(2,1)S(1)}, u32[]{:S(2)}, u32[]{:S(2)}) collective-permute-start(bf16[768,1024]{1,0:T(8,128)(2,1)S(1)} %add_convert_fusion.5), channel_id=1, source_target_pairs={{8,0},{9,1},{10,2},{11,3},{12,4},{13,5},{14,6},{15,7},{16,24},{17,... | collective-permute-start | bytes 4718600 | tf_op jit(solution)/shard_map/ppermute | solution.py:597
  578.8 23.8 %collective-permute-start.64 = (bf16[192,1536]{1,0:T(8,128)(2,1)S(1)}, bf16[192,1536]{1,0:T(8,128)(2,1)S(1)}, u32[]{:S(2)}, u32[]{:S(2)}) collective-permute-start(bf16[192,1536]{1,0:T(8,128)(2,1)S(1)} %get-tuple-element.508), channel_id=1, source_target_pairs={{0,8},{1,9},{2,10},{3,11},{4,12},{5,13},{6,14},{7,15},{24,16},{25,... | collective-permute-start | bytes 1769480 | tf_op jit(solution)/shard_map/ppermute | solution.py:591
  612.0 70.8 %collective-permute-start.70 = (bf16[384,2304]{1,0:T(8,128)(2,1)S(1)}, bf16[384,2304]{1,0:T(8,128)(2,1)S(1)}, u32[]{:S(2)}, u32[]{:S(2)}) collective-permute-start(bf16[384,2304]{1,0:T(8,128)(2,1)S(1)} %pad_maximum_fusion.5), channel_id=1, source_target_pairs={{8,0},{9,1},{10,2},{11,3},{12,4},{13,5},{14,6},{15,7},{16,24},{17,... | collective-permute-start | bytes 5308424 | tf_op jit(solution)/shard_map/ppermute | solution.py:597
  622.7 24.3 %collective-permute-start.78 = (bf16[384,1024]{1,0:T(8,128)(2,1)S(1)}, bf16[384,1024]{1,0:T(8,128)(2,1)S(1)}, u32[]{:S(2)}, u32[]{:S(2)}) collective-permute-start(bf16[384,1024]{1,0:T(8,128)(2,1)S(1)} %get-tuple-element.450), channel_id=1, source_target_pairs={{0,2},{1,3},{2,0},{3,1},{4,5},{5,4},{6,7},{7,6},{8,10},{9,11},{10,... | collective-permute-start | bytes 2359304 | tf_op jit(solution)/shard_map/ppermute | solution.py:576
  623.2 59.6 %collective-permute-start.69 = (bf16[384,1024]{1,0:T(8,128)(2,1)S(1)}, bf16[384,1024]{1,0:T(8,128)(2,1)S(1)}, u32[]{:S(2)}, u32[]{:S(2)}) collective-permute-start(bf16[384,1024]{1,0:T(8,128)(2,1)S(1)} %collective-permute-done.65), channel_id=1, source_target_pairs={{0,2},{1,3},{2,0},{3,1},{4,5},{5,4},{6,7},{7,6},{8,10},{9,11},{10,... | collective-permute-start | bytes 2359304 | tf_op jit(solution)/shard_map/ppermute | solution.py:576
  624.8 58.0 %collective-permute-start.72 = (bf16[192,1536]{1,0:T(8,128)(2,1)S(1)}, bf16[192,1536]{1,0:T(8,128)(2,1)S(1)}, u32[]{:S(2)}, u32[]{:S(2)}) collective-permute-start(bf16[192,1536]{1,0:T(8,128)(2,1)S(1)} %add_convert_fusion.25), channel_id=1, source_target_pairs={{8,0},{9,1},{10,2},{11,3},{12,4},{13,5},{14,6},{15,7},{16,24},{17,... | collective-permute-start | bytes 1769480 | tf_op jit(solution)/shard_map/ppermute | solution.py:597
  641.5 41.3 %collective-permute-start.73 = (bf16[192,1536]{1,0:T(8,128)(2,1)S(1)}, bf16[192,1536]{1,0:T(8,128)(2,1)S(1)}, u32[]{:S(2)}, u32[]{:S(2)}) collective-permute-start(bf16[192,1536]{1,0:T(8,128)(2,1)S(1)} %add_convert_fusion.24), channel_id=1, source_target_pairs={{8,0},{9,1},{10,2},{11,3},{12,4},{13,5},{14,6},{15,7},{16,24},{17,... | collective-permute-start | bytes 1769480 | tf_op jit(solution)/shard_map/ppermute | solution.py:597
  647.0 35.8 %collective-permute-start.71 = (bf16[384,128]{0,1:T(8,128)(2,1)S(1)}, bf16[384,128]{0,1:T(8,128)(2,1)S(1)}, u32[]{:S(2)}, u32[]{:S(2)}) collective-permute-start(bf16[384,128]{0,1:T(8,128)(2,1)S(1)} %add_convert_fusion.35), channel_id=1, source_target_pairs={{0,8},{1,9},{2,10},{3,11},{4,12},{5,13},{6,14},{7,15},{8,0},{9,1},... | collective-permute-start | bytes 294920 | tf_op jit(solution)/shard_map/ppermute | solution.py:585
  (129 other events, 1325.9 us)
